TPU v7x, 32 devices: a whole 2x2x4 slice. The times are simulated.
32 devices in a mesh: dp: 4 (over y, x), fsdp: 8 (over z, core).
Axes of the slice: x: 2, y: 2, z: 4, core: 2. Of those that a mesh axis runs over, the one named last changes fastest.
Arguments:
- tokens: bfloat16 [512, 196, 512], P(('dp', 'fsdp')), may hold values from -6 to 6
- valid_mask: int32 [512, 196], P(('dp', 'fsdp')), may hold values from 0 to 1, as said below
- keep_mask: int32 [512], P(('dp', 'fsdp')), may hold values 0 or 1
- out_cotangent: bfloat16 [512, 196, 512], P(('dp', 'fsdp')), may hold values from -6 to 6
- pool_cotangent: bfloat16 [512, 512], P(('dp', 'fsdp')), may hold values from -256 to 256
- inner_weight: float32 [2, 512, 1536], P(None, None, ('dp', 'fsdp')), may hold values from -0.25 to 0.25
- outer_weight: float32 [1536, 512], P(('dp', 'fsdp')), may hold values from -0.3125 to 0.3125
- vectors: float32 [7680], P(('dp', 'fsdp')), may hold values from -1.2 to 3
- spatial: float32 [197, 196], replicated, may hold values from -0.6 to 0.6
- inner_first: float32 [2, 512, 1536], P(None, None, ('dp', 'fsdp')), may hold values from -0.0004272461 to 0.0004272461
- inner_second: float32 [2, 512, 1536], P(None, None, ('dp', 'fsdp')), may hold values from 2.2032035e-08 to 8.729675e-08
- outer_first: float32 [1536, 512], P(('dp', 'fsdp')), may hold values from -0.0004272461 to 0.0004272461
- outer_second: float32 [1536, 512], P(('dp', 'fsdp')), may hold values from 2.2032035e-08 to 8.729675e-08
- vector_first: float32 [7680], P(('dp', 'fsdp')), may hold values from -0.0012207031 to 0.0012207031
- vector_second: float32 [7680], P(('dp', 'fsdp')), may hold values from 1.9537843e-07 to 7.898277e-07
- spatial_first: float32 [197, 196], replicated, may hold values from -0.0017089844 to 0.0017089844
- spatial_second: float32 [197, 196], replicated, may hold values from 3.444525e-07 to 1.3726303e-06
Outputs:
- output: float32 [512, 196, 512], P(('dp', 'fsdp'))
- input_grad: float32 [512, 196, 512], P(('dp', 'fsdp'))
- pooled: float32 [512, 512], P(('dp', 'fsdp'))
- grad_norm: float32 [], replicated
- inner_new: float32 [2, 512, 1536], P(None, None, ('dp', 'fsdp'))
- inner_first_new: float32 [2, 512, 1536], P(None, None, ('dp', 'fsdp'))
- inner_second_new: float32 [2, 512, 1536], P(None, None, ('dp', 'fsdp'))
- outer_new: float32 [1536, 512], P(('dp', 'fsdp'))
- outer_first_new: float32 [1536, 512], P(('dp', 'fsdp'))
- outer_second_new: float32 [1536, 512], P(('dp', 'fsdp'))
- vectors_new: float32 [7680], P(('dp', 'fsdp'))
- vector_first_new: float32 [7680], P(('dp', 'fsdp'))
- vector_second_new: float32 [7680], P(('dp', 'fsdp'))
- spatial_new: float32 [197, 196], replicated
- spatial_first_new: float32 [197, 196], replicated
- spatial_second_new: float32 [197, 196], replicated
Inputs may be any that keep to these rules, and one draw needn't show every extreme that they name: `valid_mask`: each image's valid patch slots come first, at least 49 of them.
All inputs are finite; a program needn't handle non-finite values. No bound on the sum of `keep_mask` on one device may be relied on, other than what follows from the above.
Results may differ from a plain program's by a relative error of at most 0.0084.
Values may be sent and summed in bfloat16 or wider, within the bound.
A program may use at most 448 MiB of HBM per device.

v0:
```python
import jax
import jax.numpy as jnp
from jax import lax
from jax.sharding import PartitionSpec as P

STEP = 10


NORM_EPS = 1e-05
DROP_RATE = 0.1
BETA_FIRST = 0.9
BETA_SECOND = 0.95
ADAM_EPS = 1e-08
DECAY_RATE = 0.05
RATE_MATRIX = 0.05
RATE_VECTOR = 0.8
CLIP_BOUND = 1.0


def norm_stats(values):
    center = values - jnp.mean(values, axis=-1, keepdims=True)
    inverse = lax.rsqrt(jnp.mean(center * center, axis=-1, keepdims=True) + NORM_EPS)
    return (center * inverse, inverse)


def norm_back(grad_normed, unit_values, inverse):
    centered = grad_normed - jnp.mean(grad_normed, axis=-1, keepdims=True)
    return inverse * (
        centered - unit_values * jnp.mean(grad_normed * unit_values, axis=-1, keepdims=True)
    )


def unpack(packed, model_width, gate_width):
    gain_one = packed[0:model_width]
    shift_one = packed[model_width : 2 * model_width]
    bias_out = packed[2 * model_width : 3 * model_width]
    base_index = 3 * model_width
    gain_two = packed[base_index : base_index + gate_width]
    shift_two = packed[base_index + gate_width : base_index + 2 * gate_width]
    bias_in = packed[base_index + 2 * gate_width :].reshape(2, gate_width)
    return (gain_one, shift_one, bias_out, gain_two, shift_two, bias_in)


def gelu_tanh(values):
    return jax.nn.gelu(values, approximate=True)


def adam_step(weight, first, second, gradient, step_rate, weight_decay):
    first_new = BETA_FIRST * first + (1.0 - BETA_FIRST) * gradient
    second_new = BETA_SECOND * second + (1.0 - BETA_SECOND) * gradient * gradient
    first_hat = first_new / (1.0 - BETA_FIRST**STEP)
    second_hat = second_new / (1.0 - BETA_SECOND**STEP)
    weight_new = weight - step_rate * (
        first_hat / (jnp.sqrt(second_hat) + ADAM_EPS) + weight_decay * weight
    )
    return (weight_new, first_new, second_new)


def per_device(
    tokens,
    valid_mask,
    keep_mask,
    out_cotangent,
    pool_cotangent,
    inner_weight,
    outer_weight,
    vectors,
    spatial,
    inner_first,
    inner_second,
    outer_first,
    outer_second,
    vector_first,
    vector_second,
    spatial_first,
    spatial_second,
):
    model_width = tokens.shape[2]
    patches = spatial.shape[1]
    inner_low = inner_weight.astype(jnp.bfloat16)
    outer_low = outer_weight.astype(jnp.bfloat16)
    vector_all, inner_all = (
        lax.all_gather(vectors.astype(jnp.bfloat16), ("dp", "fsdp"), axis=0, tiled=True),
        lax.all_gather(inner_low, ("dp", "fsdp"), axis=2, tiled=True),
    )
    gate_width = inner_all.shape[2]
    gain_one, shift_one, bias_out, gain_two, shift_two, bias_in = unpack(
        vector_all.astype(jnp.float32), model_width, gate_width
    )
    patch_mask = valid_mask.astype(jnp.float32)[:, :, None]
    keep_scale = keep_mask.astype(jnp.float32) / (1.0 - DROP_RATE)
    inputs = tokens.astype(jnp.float32)
    unit_one, inverse_one = norm_stats(inputs)
    normed = (unit_one * gain_one + shift_one).astype(jnp.bfloat16)
    before = (
        jnp.einsum("bpd,adg->abpg", normed, inner_all, preferred_element_type=jnp.float32)
        + bias_in[:, None, None, :]
    )
    hidden, gelu_back = jax.vjp(gelu_tanh, before)
    first_half = hidden[0]
    unit_two, inverse_two = norm_stats(hidden[1])
    mixed_in = ((unit_two * gain_two + shift_two) * patch_mask).astype(jnp.bfloat16)
    spatial_low = spatial[:patches].astype(jnp.bfloat16)
    spatial_out = (
        jnp.einsum("ij,bjg->big", spatial_low, mixed_in, preferred_element_type=jnp.float32)
        + spatial[patches][None, :, None]
    )
    gated_low = (first_half * spatial_out * patch_mask).astype(jnp.bfloat16)
    outer_group = lax.all_gather(outer_low, "fsdp", axis=0, tiled=True)
    columns = gated_low
    branch = (
        jnp.einsum(
            "bpg,gd->bpd",
            columns,
            lax.all_gather(outer_group, "dp", axis=0, tiled=True),
            preferred_element_type=jnp.float32,
        )
        + bias_out
    )
    output = inputs + keep_scale[:, None, None] * branch
    patch_count = jnp.sum(patch_mask, axis=1)
    pooled = jnp.sum(output * patch_mask, axis=1) / patch_count
    out_grad = (
        out_cotangent.astype(jnp.float32)
        + patch_mask * (pool_cotangent.astype(jnp.float32) / patch_count)[:, None, :]
    )
    branch_grad = (keep_scale[:, None, None] * out_grad).astype(jnp.bfloat16)
    bias_out_grad = jnp.sum(branch_grad, axis=(0, 1), dtype=jnp.float32)
    outer_grad = jnp.einsum(
        "bpg,bpd->gd", gated_low, branch_grad, preferred_element_type=jnp.float32
    )
    outer_again = lax.all_gather(outer_low, "fsdp", axis=0, tiled=True)
    gated_grad = jnp.einsum(
        "bpd,gd->bpg",
        branch_grad,
        lax.all_gather(outer_again, "dp", axis=0, tiled=True),
        preferred_element_type=jnp.float32,
    )
    mixer_grad = (gated_grad * first_half * patch_mask).astype(jnp.bfloat16)
    first_grad = gated_grad * spatial_out * patch_mask
    spatial_matrix_grad = jnp.einsum(
        "big,bjg->ij", mixer_grad, mixed_in, preferred_element_type=jnp.float32
    )
    spatial_bias_grad = jnp.sum(mixer_grad, axis=(0, 2), dtype=jnp.float32)
    spatial_local = jnp.concatenate([spatial_matrix_grad, spatial_bias_grad[None, :]], axis=0)
    spatial_total = lax.psum(spatial_local, ("dp", "fsdp"))
    mixed_grad = (
        jnp.einsum("ij,big->bjg", spatial_low, mixer_grad, preferred_element_type=jnp.float32)
        * patch_mask
    )
    gain_two_grad = jnp.sum(mixed_grad * unit_two, axis=(0, 1))
    shift_two_grad = jnp.sum(mixed_grad, axis=(0, 1))
    second_grad = norm_back(mixed_grad * gain_two, unit_two, inverse_two)
    pre_grad = gelu_back(jnp.stack([first_grad, second_grad]))[0].astype(jnp.bfloat16)
    bias_in_grad = jnp.sum(pre_grad, axis=(1, 2), dtype=jnp.float32)
    inner_grad = jnp.einsum("bpd,abpg->adg", normed, pre_grad, preferred_element_type=jnp.float32)
    inner_group = lax.all_gather(inner_low, "fsdp", axis=2, tiled=True)
    columns = pre_grad
    normed_grad = jnp.einsum(
        "abpg,adg->bpd",
        columns,
        lax.all_gather(inner_group, "dp", axis=2, tiled=True),
        preferred_element_type=jnp.float32,
    )
    gain_one_grad = jnp.sum(normed_grad * unit_one, axis=(0, 1))
    shift_one_grad = jnp.sum(normed_grad, axis=(0, 1))
    input_grad = out_grad + norm_back(normed_grad * gain_one, unit_one, inverse_one)
    vector_grad = jnp.concatenate(
        [
            gain_one_grad,
            shift_one_grad,
            bias_out_grad,
            gain_two_grad,
            shift_two_grad,
            bias_in_grad.reshape(-1),
        ]
    )
    vector_red, inner_red, outer_red = (
        lax.psum_scatter(vector_grad, ("dp", "fsdp"), scatter_dimension=0, tiled=True),
        lax.psum_scatter(inner_grad, ("dp", "fsdp"), scatter_dimension=2, tiled=True),
        lax.psum_scatter(outer_grad, ("dp", "fsdp"), scatter_dimension=0, tiled=True),
    )
    shard_squares = (
        jnp.sum(inner_red * inner_red)
        + jnp.sum(outer_red * outer_red)
        + jnp.sum(vector_red * vector_red)
    )
    squares_total = lax.psum(shard_squares, ("dp", "fsdp"))
    squares_total = squares_total + jnp.sum(spatial_total * spatial_total)
    grad_norm = jnp.sqrt(squares_total)
    clip_factor = CLIP_BOUND / jnp.maximum(grad_norm, CLIP_BOUND)
    inner_new, inner_first_new, inner_second_new = adam_step(
        inner_weight, inner_first, inner_second, inner_red * clip_factor, RATE_MATRIX, DECAY_RATE
    )
    outer_new, outer_first_new, outer_second_new = adam_step(
        outer_weight, outer_first, outer_second, outer_red * clip_factor, RATE_MATRIX, DECAY_RATE
    )
    vectors_new, vector_first_new, vector_second_new = adam_step(
        vectors, vector_first, vector_second, vector_red * clip_factor, RATE_VECTOR, 0.0
    )
    row_index = jnp.arange(patches + 1)[:, None]
    spatial_rate = jnp.where(row_index < patches, RATE_MATRIX, RATE_VECTOR)
    spatial_decay = jnp.where(row_index < patches, DECAY_RATE, 0.0)
    spatial_new, spatial_first_new, spatial_second_new = adam_step(
        spatial,
        spatial_first,
        spatial_second,
        spatial_total * clip_factor,
        spatial_rate,
        spatial_decay,
    )
    return (
        output,
        input_grad,
        pooled,
        grad_norm,
        inner_new,
        inner_first_new,
        inner_second_new,
        outer_new,
        outer_first_new,
        outer_second_new,
        vectors_new,
        vector_first_new,
        vector_second_new,
        spatial_new,
        spatial_first_new,
        spatial_second_new,
    )


def solution(mesh):
    in_specs = (
        P(("dp", "fsdp"), None, None),
        P(("dp", "fsdp"), None),
        P(("dp", "fsdp")),
        P(("dp", "fsdp"), None, None),
        P(("dp", "fsdp"), None),
        P(None, None, ("dp", "fsdp")),
        P(("dp", "fsdp"), None),
        P(("dp", "fsdp")),
        P(),
        P(None, None, ("dp", "fsdp")),
        P(None, None, ("dp", "fsdp")),
        P(("dp", "fsdp"), None),
        P(("dp", "fsdp"), None),
        P(("dp", "fsdp")),
        P(("dp", "fsdp")),
        P(),
        P(),
    )
    out_specs = (
        P(("dp", "fsdp"), None, None),
        P(("dp", "fsdp"), None, None),
        P(("dp", "fsdp"), None),
        P(),
        P(None, None, ("dp", "fsdp")),
        P(None, None, ("dp", "fsdp")),
        P(None, None, ("dp", "fsdp")),
        P(("dp", "fsdp"), None),
        P(("dp", "fsdp"), None),
        P(("dp", "fsdp"), None),
        P(("dp", "fsdp")),
        P(("dp", "fsdp")),
        P(("dp", "fsdp")),
        P(),
        P(),
        P(),
    )
    return jax.shard_map(
        per_device, mesh=mesh, in_specs=in_specs, out_specs=out_specs, check_vma=False
    )
```

profile of v0, /device:TPU:0, one launch (start us, length us, event | category | flops | bytes accessed | tf_op | source)
XLA Modules:
  0.0 720.6 jit_solution(18312424633975866661)
XLA Ops:
  7.2 1.7 convert_element_type.60
  9.0 0.0 all-gather.6.cloned.1.call-start
  9.1 0.9 convert_element_type.64
  10.0 17.3 %all_gather.22 = bf16[384,512]{1,0:T(8,128)(2,1)} all-gather(bf16[48,512]{1,0:T(8,128)(2,1)S(1)} %convert_element_type.64), channel_id=1, replica_groups=mesh['dp'=4,'fsdp'=8] {'fsdp'}, dimensions={0}, use_global_device_ids=true | all-gather | bytes 442368 | tf_op jit(solution)/shard_map/all_gather | solution.py:109
  27.3 17.3 %all_gather.24 = bf16[2,512,384]{1,2,0:T(8,128)(2,1)} all-gather(bf16[2,512,48]{1,2,0:T(8,128)(2,1)} %convert_element_type.60), channel_id=1, replica_groups=mesh['dp'=4,'fsdp'=8] {'fsdp'}, dimensions={2}, use_global_device_ids=true | all-gather | bytes 884736 | tf_op jit(solution)/shard_map/all_gather | solution.py:157
  44.7 0.0 reduce-scatter.5.cloned.1.call-start
  44.7 0.6 fusion.69
  45.3 0.8 convert_reduce_fusion.4
  46.2 0.7 convert_element_type.61
  46.9 0.7 convert_element_type.57
  47.6 0.2 dynamic-update-slice
  47.8 41.0 %all-reduce = bf16[7680]{0:T(1024)(128)(2,1)S(1)} all-reduce(bf16[7680]{0:T(1024)(128)(2,1)S(1)} %dynamic-update-slice), channel_id=1, replica_groups=mesh['dp'=4,'fsdp'=8] {'dp','fsdp'}, use_global_device_ids=true, to_apply=%add | all-reduce | flops 7680 | bytes 30720
  88.8 0.6 fusion.78
  89.4 0.7 convert_multiply_fusion
  90.0 0.7 slice.50
  90.7 5.3 convert_reduce_fusion.2
  96.1 3.9 fusion.39
  100.0 0.1 copy.110
  100.2 0.1 convert_divide_fusion
  100.2 0.6 copy-done.22
  100.9 4.9 convert_reduce_fusion.3
  105.8 5.9 fusion.33
  111.8 34.3 %bitcast_multiply_fusion = (f32[2,16,196,1536]{3,1,2,0:T(8,128)}, f32[16,196,2,1536]{3,0,1,2:T(8,128)}) fusion(f32[2,1536]{1,0:T(2,128)S(1)} %slice.44, bf16[2,512,1536]{1,2,0:T(8,128)(2,1)} %all-gather.4.cloned.1.call-done, bf16[16,196,512,1]{2,1,0,3:T(8,128)(2,1)} %get-tuple-element.126), kind=kOutput, calls=%fused_computation.10 | convolution fusion | flops 9951707136 | bytes 83439616 | tf_op jit(solution)/shard_map/bpd,adg->abpg/dot_general | solution.py:96
  146.1 7.4 %slice_reduce_fusion = f32[16,196]{0,1:T(8,128)S(1)} fusion(f32[2,16,196,1536]{3,1,2,0:T(8,128)} %get-tuple-element.134), kind=kLoop, calls=%fused_computation.37 | loop fusion | flops 4813760 | bytes 19280128 | tf_op jit(solution)/shard_map/reduce_sum | solution.py:21
  153.5 0.1 copy.106
  153.5 0.1 copy.107
  153.7 30.4 %convert_reduce_fusion.1 = (f32[196]{0:T(256)}, bf16[16,196,1536]{2,0,1:T(8,128)(2,1)}, f32[16,196]{0,1:T(8,128)S(1)}, f32[16,196,1536]{2,0,1:T(8,128)}) fusion(f32[16,196]{0,1:T(8,128)S(1)} %copy.110, f32[2,16,196,1536]{3,1,2,0:T(8,128)} %get-tuple-element.134, f32[16,196]{0,1:T(8,128)S(1)} %copy.107, bf16[1536,512]{1,0:T(8,128)(2,1)} %all-gather.6.cloned.1.call-done, ...), kind=kOutput, calls=%fused_computation.29 | convolution fusion | flops 4971033600 | bytes 72259088 | tf_op jit(solution)/shard_map/bpd,gd->bpg/dot_general | solution.py:133
  184.1 0.1 copy.108
  184.2 0.1 copy.109
  184.3 17.3 %fusion.21 = f32[16,1536,196]{1,2,0:T(8,128)} fusion(bf16[16,196,1536]{2,0,1:T(8,128)(2,1)} %get-tuple-element.115, f32[197,196]{1,0:T(8,128)S(1)} %copy-done.8), kind=kOutput, calls=%fused_computation.46 | convolution fusion | flops 1888223232 | bytes 29003776 | tf_op jit(solution)/shard_map/ij,big->bjg/dot_general | solution.py:148
  201.6 28.5 %fusion.9 = (f32[1536]{0:T(1024)}, f32[16,196]{0,1:T(8,128)S(1)}, f32[16,196]{0,1:T(8,128)S(1)}) fusion(f32[16,196]{0,1:T(8,128)S(1)} %copy.110, f32[16,1536,196]{1,2,0:T(8,128)} %fusion.21, f32[16,196]{0,1:T(8,128)S(1)} %copy.109, f32[16,196]{0,1:T(8,128)S(1)} %copy.107, f32[2,16,196,1536]{3,1,2,0:T(8,128)} %get-tuple-element.134, ...), kind=kLoop, calls=%fused_computation.19 | loop fusion | flops 43344256 | bytes 38610176 | tf_op jit(solution)/shard_map/reduce_sum | solution.py:151
  230.1 0.1 copy.123
  230.2 0.1 copy.121
  230.3 0.1 copy.122
  230.4 0.1 copy.124
  230.5 25.9 %multiply_bitcast_fusion = (f32[1,16,196,1536]{3,1,2,0:T(8,128)}, bf16[16,196,1536]{2,0,1:T(8,128)(2,1)S(1)}) fusion(f32[16,196]{0,1:T(8,128)S(1)} %copy.124, f32[16,196]{0,1:T(8,128)S(1)} %copy.122, f32[1536]{0:T(1024)S(1)} %get-tuple-element.129, f32[16,196]{0,1:T(8,128)S(1)} %copy.109, f32[16,196]{0,1:T(8,128)S(1)} %copy.110, ...), kind=kLoop, calls=%fused_computation.30 | loop fusion | flops 57802752 | bytes 68067328 | tf_op jit(solution)/shard_map/stack | solution.py:154
  256.3 10.8 %fusion.24 = f32[16,1536,196]{1,2,0:T(8,128)} fusion(bf16[16,196,1536]{2,0,1:T(8,128)(2,1)S(1)} %get-tuple-element.121, f32[197,196]{1,0:T(8,128)S(1)} %copy-done.8), kind=kOutput, calls=%fused_computation.49 | convolution fusion | flops 1888223232 | bytes 29003776 | tf_op jit(solution)/shard_map/ij,bjg->big/dot_general | solution.py:105
  267.2 34.1 %fusion.13 = (f32[1,16,196,1536]{3,1,2,0:T(8,128)}, bf16[16,196,1536]{2,0,1:T(8,128)(2,1)S(1)}) fusion(f32[16,196,1536]{2,0,1:T(8,128)} %get-tuple-element.136, f32[16,1536,196]{1,2,0:T(8,128)} %fusion.24, f32[196]{0:T(256)S(1)} %bitcast.116, f32[16,196]{0,1:T(8,128)S(1)} %copy.110, f32[2,16,196,1536]{3,1,2,0:T(8,128)} %get-tuple-element.134), kind=kLoop, calls=%fused_computation.25 | loop fusion | flops 28901376 | bytes 86717456 | tf_op jit(solution)/shard_map/stack | solution.py:154
  301.2 3.7 copy-done.3
  304.9 7.1 convolution_bitcast_fusion.1
  312.1 0.0 reduce-scatter.3.cloned.1.call-start
  312.1 35.2 %convert_reduce_fusion = (f32[2,1536]{1,0:T(2,128)}, bf16[2,16,196,1536]{3,1,2,0:T(8,128)(2,1)}) fusion(f32[16,196,2,1536]{3,0,1,2:T(8,128)} %get-tuple-element.135, f32[1,16,196,1536]{3,1,2,0:T(8,128)} %get-tuple-element.120, f32[1,16,196,1536]{3,1,2,0:T(8,128)} %get-tuple-element.123), kind=kLoop, calls=%fused_computation.14 | loop fusion | flops 221574144 | bytes 96350208 | tf_op jit(solution)/shard_map/reduce_sum | solution.py:155
  347.3 16.7 %convolution_bitcast_fusion = f32[2,512,1536]{1,2,0:T(8,128)} fusion(bf16[2,16,196,1536]{3,1,2,0:T(8,128)(2,1)} %get-tuple-element.117, bf16[16,196,512]{2,1,0:T(8,128)(2,1)S(1)} %copy-done.6), kind=kOutput, calls=%fused_computation.71 | convolution fusion | flops 9865003008 | bytes 28770304 | tf_op jit(solution)/shard_map/bpd,abpg->adg/dot_general | solution.py:156
  364.2 17.1 %fusion.79 = (f32[512]{0:T(512)S(1)}, f32[16,196,512]{2,0,1:T(8,128)}) fusion(bf16[2,16,196,1536]{3,1,2,0:T(8,128)(2,1)} %get-tuple-element.117, bf16[2,512,1536]{1,2,0:T(8,128)(2,1)} %all-gather.8.cloned.1.call-done), kind=kOutput, calls=%fused_computation.133 | convolution fusion | flops 9866608640 | bytes 28837888 | tf_op jit(solution)/shard_map/abpg,adg->bpd/dot_general | solution.py:159
  381.4 13.9 %fusion.38 = (f32[512]{0:T(512)S(1)}, f32[16,196]{1,0:T(8,128)S(1)}, f32[16,196]{1,0:T(8,128)S(1)}) fusion(f32[16,196,512]{2,0,1:T(8,128)} %get-tuple-element.139, f32[16,196]{1,0:T(8,128)S(1)} %copy-done.19, f32[16,196]{1,0:T(8,128)S(1)} %copy-done.13, bf16[16,196,512]{2,0,1:T(8,128)(2,1)S(1)} %copy-done.2, f32[512]{0:T(512)S(1)} %copy-done.30), kind=kLoop, calls=%fused_computation.63 | loop fusion | flops 14443904 | bytes 9688064 | tf_op jit(solution)/shard_map/reduce_sum | solution.py:165
  395.3 26.5 %multiply_reduce_fusion.2 = (f32[16,512]{1,0:T(8,128)S(1)}, f32[16,196,512]{2,1,0:T(8,128)}, f32[16,196,512]{2,1,0:T(8,128)}) fusion(f32[16,196]{1,0:T(8,128)S(1)} %copy-done.21, f32[16,196]{1,0:T(8,128)S(1)} %get-tuple-element.140, f32[16,196]{1,0:T(8,128)S(1)} %copy-done.13, bf16[16,196,512]{2,0,1:T(8,128)(2,1)S(1)} %copy-done.2, ...), kind=kOutput, calls=%fused_computation.66 | convolution fusion | flops 4959789056 | bytes 37029184 | tf_op jit(solution)/shard_map/bpg,gd->bpd/dot_general | solution.py:112
  421.9 9.6 %copy.133 = f32[16,196,512]{2,0,1:T(8,128)} copy(f32[16,196,512]{2,1,0:T(8,128)} %get-tuple-element.128) | data formatting | bytes 12845056
  431.5 6.5 copy.132
  438.0 19.3 %fusion.18 = f32[1536]{0:T(1024)S(1)} fusion(f32[16,196]{0,1:T(8,128)S(1)} %copy-done.5, f32[16,1536,196]{1,2,0:T(8,128)} %fusion.21), kind=kLoop, calls=%fused_computation.43 | loop fusion | flops 9632256 | bytes 19286272 | tf_op jit(solution)/shard_map/reduce_sum | solution.py:152
  457.3 41.7 %all-reduce.1 = f32[7680]{0:T(1024)S(1)} all-reduce(f32[7680]{0:T(1024)S(1)} %constant_dynamic-update-slice_fusion), channel_id=4, replica_groups=mesh['dp'=4,'fsdp'=8] {'dp','fsdp'}, use_global_device_ids=true, to_apply=%region_20.0.clone | all-reduce | flops 7680 | bytes 61440
  499.2 27.1 %fusion.57 = f32[196,196]{1,0:T(8,128)S(1)} fusion(bf16[16,196,1536]{2,0,1:T(8,128)(2,1)} %copy-done, bf16[16,196,1536]{2,0,1:T(8,128)(2,1)} %get-tuple-element.115), kind=kOutput, calls=%fused_computation.85 | convolution fusion | flops 1888223232 | bytes 19421248 | tf_op jit(solution)/shard_map/big,bjg->ij/dot_general | solution.py:141
  526.3 0.7 pad_maximum_fusion.1
  527.0 0.7 broadcast_divide_fusion
  527.7 0.7 multiply_reduce_fusion.6
  528.4 1.5 multiply_reduce_fusion.5
  529.9 2.8 reduce-scatter.3.cloned.1.call-done
  532.8 1.6 multiply_reduce_fusion.4
  536.3 125.7 %all-reduce.4.cloned.1.call-done = f32[197,196]{1,0:T(8,128)} async-done(((f32[197,196]{1,0:T(8,128)}), f32[197,196]{1,0:T(8,128)}) %all-reduce.4.cloned.1.call-update) | async-done | bytes 154464 | tf_op jit(solution)/shard_map/psum | solution.py:146
  662.0 1.6 multiply_reduce_fusion.3
  663.6 41.1 %psum.14 = f32[]{:T(128)} all-reduce(f32[]{:T(128)S(6)} %add.180), channel_id=1, replica_groups=mesh['dp'=4,'fsdp'=8] {'dp','fsdp'}, use_global_device_ids=true, to_apply=%region_22.0 | all-reduce | flops 1 | bytes 8 | tf_op jit(solution)/shard_map/psum | solution.py:188
  706.1 0.7 multiply_subtract_fusion.3
  706.8 1.6 multiply_subtract_fusion.2
  708.4 1.8 multiply_subtract_fusion.1
  710.3 1.9 multiply_subtract_fusion
  (123 shorter events, 0.7 us)
Async XLA Ops:
  7.2 98.6 %copy-start.1 = (bf16[16,196,512]{2,0,1:T(8,128)(2,1)S(1)}, bf16[16,196,512]{2,0,1:T(8,128)(2,1)}, u32[]{:S(2)}) copy-start(bf16[16,196,512]{2,0,1:T(8,128)(2,1)} %param.17) | copy-start | bytes 9633796
  7.2 93.0 %copy-start.31 = (bf16[16,512]{1,0:T(8,128)(2,1)S(1)}, bf16[16,512]{1,0:T(8,128)(2,1)}, u32[]{:S(2)}) copy-start(bf16[16,512]{1,0:T(8,128)(2,1)} %param.21) | copy-start | bytes 49156
  7.2 104.5 %all-gather.4.cloned.1.call-start = ((), (), s32[]{:S(2)}) async-start(), calls=%async_computation.2 | async-start | bytes 3244032 | tf_op jit(solution)/shard_map/all_gather | solution.py:84
  9.0 144.7 %all-gather.6.cloned.1.call-start = ((), (), s32[]{:S(2)}) async-start(), calls=%async_computation.3 | async-start | bytes 1966080 | tf_op jit(solution)/shard_map/all_gather | solution.py:115
  27.3 337.0 %all-gather.8.cloned.1.call-start = ((), (), s32[]{:S(2)}) async-start(), calls=%async_computation.4 | async-start | bytes 3932160 | tf_op jit(solution)/shard_map/all_gather | solution.py:162
  44.7 483.8 %reduce-scatter.5.cloned.1.call-start = ((), (), s32[]{:S(2)}) async-start(), calls=%async_computation.6 | async-start | bytes 3244032 | tf_op jit(solution)/shard_map/reduce_scatter | solution.py:181
  46.2 65.5 %copy-start.33 = (f32[16]{0:T(128)}, f32[16]{0:T(128)S(1)}, u32[]{:S(2)}) copy-start(f32[16]{0:T(128)S(1)} %convert_reduce_fusion.4) | copy-start | bytes 196
  46.9 64.8 %copy-start.20 = (f32[16,196]{1,0:T(8,128)}, f32[16,196]{1,0:T(8,128)S(1)}, u32[]{:S(2)}) copy-start(f32[16,196]{1,0:T(8,128)S(1)} %convert_element_type.61) | copy-start | bytes 37636
  89.4 22.3 %copy-start.29 = (f32[512]{0:T(512)}, f32[512]{0:T(512)S(1)}, u32[]{:S(2)}) copy-start(f32[512]{0:T(512)S(1)} %get-tuple-element.131) | copy-start | bytes 6148
  90.0 21.7 %copy-start.42 = (f32[16]{0:T(128)}, f32[16]{0:T(128)S(1)}, u32[]{:S(2)}) copy-start(f32[16]{0:T(128)S(1)} %convert_multiply_fusion) | copy-start | bytes 196
  96.1 15.6 %copy-start.12 = (f32[16,196]{1,0:T(8,128)}, f32[16,196]{1,0:T(8,128)S(1)}, u32[]{:S(2)}) copy-start(f32[16,196]{1,0:T(8,128)S(1)} %broadcast_multiply_fusion.5) | copy-start | bytes 37636
  100.0 46.1 %copy-start.18 = (f32[16,196]{1,0:T(8,128)}, f32[16,196]{1,0:T(8,128)S(1)}, u32[]{:S(2)}) copy-start(f32[16,196]{1,0:T(8,128)S(1)} %add_rsqrt_fusion.1) | copy-start | bytes 37636
  100.1 167.0 %copy-start.4 = (f32[16,196]{0,1:T(8,128)}, f32[16,196]{0,1:T(8,128)S(1)}, u32[]{:S(2)}) copy-start(f32[16,196]{0,1:T(8,128)S(1)} %copy.110) | copy-start | bytes 37636
  100.2 0.6 copy-start.22
  153.7 30.6 %copy-start.8 = (f32[197,196]{1,0:T(8,128)S(1)}, f32[197,196]{1,0:T(8,128)}, u32[]{:S(2)}) copy-start(f32[197,196]{1,0:T(8,128)} %param.25) | copy-start | bytes 463348
  256.3 10.8 %copy-start = (bf16[16,196,1536]{2,0,1:T(8,128)(2,1)}, bf16[16,196,1536]{2,0,1:T(8,128)(2,1)S(1)}, u32[]{:S(2)}) copy-start(bf16[16,196,1536]{2,0,1:T(8,128)(2,1)S(1)} %get-tuple-element.121) | copy-start | bytes 28901380
  267.2 37.7 %copy-start.7 = (bf16[16,196,512]{2,1,0:T(8,128)(2,1)S(1)}, bf16[16,196,512]{2,1,0:T(8,128)(2,1)}, u32[]{:S(2)}) copy-start(bf16[16,196,512]{2,1,0:T(8,128)(2,1)} %get-tuple-element.119) | copy-start | bytes 9633796
  301.2 3.7 copy-start.3
  312.1 220.7 %reduce-scatter.3.cloned.1.call-start = ((), (), s32[]{:S(2)}) async-start(), calls=%async_computation.5 | async-start | bytes 6488064 | tf_op jit(solution)/shard_map/reduce_scatter | solution.py:180
  312.1 35.2 %copy-start.6 = (bf16[16,196,512]{2,1,0:T(8,128)(2,1)S(1)}, bf16[16,196,512]{2,1,0:T(8,128)(2,1)}, u32[]{:S(2)}) copy-start(bf16[16,196,512]{2,1,0:T(8,128)(2,1)} %get-tuple-element.125) | copy-start | bytes 9633796
  364.0 17.3 %copy-start.26 = (f32[2,1536]{1,0:T(2,128)S(1)}, f32[2,1536]{1,0:T(2,128)}, u32[]{:S(2)}) copy-start(f32[2,1536]{1,0:T(2,128)} %get-tuple-element.116) | copy-start | bytes 36868
  364.0 17.3 %copy-start.2 = (bf16[16,196,512]{2,0,1:T(8,128)(2,1)S(1)}, bf16[16,196,512]{2,0,1:T(8,128)(2,1)}, u32[]{:S(2)}) copy-start(bf16[16,196,512]{2,0,1:T(8,128)(2,1)} %param.17) | copy-start | bytes 9633796
  364.1 17.3 %copy-start.13 = (f32[16,196]{1,0:T(8,128)S(1)}, f32[16,196]{1,0:T(8,128)}, u32[]{:S(2)}) copy-start(f32[16,196]{1,0:T(8,128)} %copy-done.12) | copy-start | bytes 37636
  364.1 17.3 %copy-start.19 = (f32[16,196]{1,0:T(8,128)S(1)}, f32[16,196]{1,0:T(8,128)}, u32[]{:S(2)}) copy-start(f32[16,196]{1,0:T(8,128)} %copy-done.18) | copy-start | bytes 37636
  364.1 17.3 %copy-start.30 = (f32[512]{0:T(512)S(1)}, f32[512]{0:T(512)}, u32[]{:S(2)}) copy-start(f32[512]{0:T(512)} %copy-done.29) | copy-start | bytes 6148
  364.1 31.2 %copy-start.21 = (f32[16,196]{1,0:T(8,128)S(1)}, f32[16,196]{1,0:T(8,128)}, u32[]{:S(2)}) copy-start(f32[16,196]{1,0:T(8,128)} %copy-done.20) | copy-start | bytes 37636
  364.1 31.2 %copy-start.23 = (f32[16,512]{1,0:T(8,128)S(1)}, f32[16,512]{1,0:T(8,128)}, u32[]{:S(2)}) copy-start(f32[16,512]{1,0:T(8,128)} %copy-done.22) | copy-start | bytes 98308
  364.1 31.2 %copy-start.37 = (f32[512]{0:T(512)S(1)}, f32[512]{0:T(512)}, u32[]{:S(2)}) copy-start(f32[512]{0:T(512)} %get-tuple-element.133) | copy-start | bytes 6148
  364.1 31.2 %copy-start.43 = (f32[16]{0:T(128)S(1)}, f32[16]{0:T(128)}, u32[]{:S(2)}) copy-start(f32[16]{0:T(128)} %copy-done.42) | copy-start | bytes 196
  364.1 297.8 %all-reduce.4.cloned.1.call-start = ((), (), s32[]{:S(2)}) async-start(), calls=%async_computation.7 | async-start | bytes 409600 | tf_op jit(solution)/shard_map/psum | solution.py:146
  421.8 9.7 %slice-start = ((s8[6553600]{0:T(1024)(128)(4,1)}), s8[4194304]{0:T(1024)(128)(4,1)S(1)}, s32[]{:S(2)}) async-start(s8[6553600]{0:T(1024)(128)(4,1)} %bitcast.114), calls=%async_computation.8 | async-start | bytes 8388608
  421.8 9.7 %slice-start.1 = ((s8[6553600]{0:T(1024)(128)(4,1)}), s8[2359296]{0:T(1024)(128)(4,1)S(1)}, s32[]{:S(2)}) async-start(s8[6553600]{0:T(1024)(128)(4,1)} %bitcast.114), calls=%async_computation.9 | async-start | bytes 4718592
  421.8 16.1 %copy-start.28 = (f32[7680]{0:T(1024)S(1)}, f32[7680]{0:T(1024)}, u32[]{:S(2)}) copy-start(f32[7680]{0:T(1024)} %custom-call) | copy-start | bytes 92164
  421.8 16.1 %copy-start.32 = (f32[512]{0:T(512)S(1)}, f32[512]{0:T(512)}, u32[]{:S(2)}) copy-start(f32[512]{0:T(512)} %get-tuple-element.118) | copy-start | bytes 6148
  421.9 16.2 %copy-start.27 = (f32[1536]{0:T(1024)S(1)}, f32[1536]{0:T(1024)}, u32[]{:S(2)}) copy-start(f32[1536]{0:T(1024)} %get-tuple-element.96) | copy-start | bytes 18436
  421.9 16.2 %copy-start.5 = (f32[16,196]{0,1:T(8,128)S(1)}, f32[16,196]{0,1:T(8,128)}, u32[]{:S(2)}) copy-start(f32[16,196]{0,1:T(8,128)} %copy-done.4) | copy-start | bytes 37636
  499.0 27.3 %copy-start.38 = (f32[196]{0:T(256)S(1)}, f32[196]{0:T(256)}, u32[]{:S(2)}) copy-start(f32[196]{0:T(256)} %get-tuple-element.114) | copy-start | bytes 2356
  499.0 28.0 %copy-start.34 = (f32[16]{0:T(128)S(1)}, f32[16]{0:T(128)}, u32[]{:S(2)}) copy-start(f32[16]{0:T(128)} %copy-done.33) | copy-start | bytes 196
  499.0 207.0 %copy-start.39 = (f32[240]{0:T(256)S(1)}, f32[240]{0:T(256)}, u32[]{:S(2)}) copy-start(f32[240]{0:T(256)} %param.24) | copy-start | bytes 2884
  499.1 207.0 %copy-start.40 = (f32[240]{0:T(256)S(1)}, f32[240]{0:T(256)}, u32[]{:S(2)}) copy-start(f32[240]{0:T(256)} %param.30) | copy-start | bytes 2884
  499.1 207.0 %copy-start.41 = (f32[240]{0:T(256)S(1)}, f32[240]{0:T(256)}, u32[]{:S(2)}) copy-start(f32[240]{0:T(256)} %param.31) | copy-start | bytes 2884
  499.1 207.7 %copy-start.11 = (f32[48,512]{1,0:T(8,128)S(1)}, f32[48,512]{1,0:T(8,128)}, u32[]{:S(2)}) copy-start(f32[48,512]{1,0:T(8,128)} %param.23) | copy-start | bytes 294916
  499.1 207.7 %copy-start.24 = (f32[48,512]{1,0:T(8,128)S(1)}, f32[48,512]{1,0:T(8,128)}, u32[]{:S(2)}) copy-start(f32[48,512]{1,0:T(8,128)} %param.28) | copy-start | bytes 294916
  499.1 207.7 %copy-start.25 = (f32[48,512]{1,0:T(8,128)S(1)}, f32[48,512]{1,0:T(8,128)}, u32[]{:S(2)}) copy-start(f32[48,512]{1,0:T(8,128)} %param.29) | copy-start | bytes 294916
  499.1 209.3 %copy-start.10 = (f32[2,512,48]{1,2,0:T(8,128)S(1)}, f32[2,512,48]{1,2,0:T(8,128)}, u32[]{:S(2)}) copy-start(f32[2,512,48]{1,2,0:T(8,128)} %param.22) | copy-start | bytes 589828
  499.1 209.3 %copy-start.16 = (f32[2,512,48]{1,2,0:T(8,128)S(1)}, f32[2,512,48]{1,2,0:T(8,128)}, u32[]{:S(2)}) copy-start(f32[2,512,48]{1,2,0:T(8,128)} %param.26) | copy-start | bytes 589828
  499.1 209.3 %copy-start.17 = (f32[2,512,48]{1,2,0:T(8,128)S(1)}, f32[2,512,48]{1,2,0:T(8,128)}, u32[]{:S(2)}) copy-start(f32[2,512,48]{1,2,0:T(8,128)} %param.27) | copy-start | bytes 589828
  499.2 211.1 %copy-start.9 = (f32[197,196]{1,0:T(8,128)S(1)}, f32[197,196]{1,0:T(8,128)}, u32[]{:S(2)}) copy-start(f32[197,196]{1,0:T(8,128)} %param.25) | copy-start | bytes 463348
  499.2 211.1 %copy-start.14 = (f32[197,196]{1,0:T(8,128)S(1)}, f32[197,196]{1,0:T(8,128)}, u32[]{:S(2)}) copy-start(f32[197,196]{1,0:T(8,128)} %param.32) | copy-start | bytes 463348
  499.2 211.1 %copy-start.15 = (f32[197,196]{1,0:T(8,128)S(1)}, f32[197,196]{1,0:T(8,128)}, u32[]{:S(2)}) copy-start(f32[197,196]{1,0:T(8,128)} %param.33) | copy-start | bytes 463348
  499.2 211.1 %copy-start.35 = (f32[197]{0:T(256)S(1)}, f32[197]{0:T(256)}, u32[]{:S(2)}) copy-start(f32[197]{0:T(256)} %get-tuple-element.142) | copy-start | bytes 2368
  499.2 211.1 %copy-start.36 = (f32[197]{0:T(256)S(1)}, f32[197]{0:T(256)}, u32[]{:S(2)}) copy-start(f32[197]{0:T(256)} %get-tuple-element.143) | copy-start | bytes 2368
Sparse Core Ops, SparseCore 0:
  11.6 61.9 all-gather.3
  75.4 30.2 all-gather.5
  107.5 43.9 all-gather.7
  312.2 101.3 reduce-scatter.4
  419.1 113.5 reduce-scatter.2
  539.6 122.2 all-reduce.3
where the time goes:
time: 729 us; the launch traced here: 721 us
  other arithmetic  203 us (28%)
  matrix products  187 us (26%)
  blocking collectives  158 us (22%)
  waiting for transfers between devices  129 us (18%)
  local copies, waits for them, and re-layouts  22.9 us (3%)
  between operations  19.7 us (3%)
    psum x1, waiting for transfers between devices, per_device(): spatial_total = lax.psum(spatial_local, ('dp', 'fsdp'))  126 us
    unnamed x2, blocking collectives  82.7 us
    another operation x2, other arithmetic, per_device(): jnp.stack([first_grad, second_grad])  59.9 us
    psum x1, blocking collectives, per_device(): squares_total = lax.psum(shard_squares, ('dp', 'fsdp'))  41.1 us
    reduce_sum x1, other arithmetic, per_device(): bias_in_grad = jnp.sum(pre_grad, axis=(1, 2), dtype=jnp.float32)  35.2 us
    dot_general x1, matrix products, per_device(): jnp.einsum('bpd,adg->abpg', normed, inner_all, preferred_element_type=jnp...  34.3 us
    dot_general x1, matrix products, per_device(): jnp.einsum('bpd,gd->bpg', branch_grad, lax.all_gather(outer_again, 'dp',...  30.4 us
    reduce_sum x1, other arithmetic, per_device(): gain_two_grad = jnp.sum(mixed_grad * unit_two, axis=(0, 1))  28.5 us
  transfers between devices with their start and end apart: 6, of which 2 were waited for; matrix products, arithmetic and copies ran while one was open for 55% of the time, Pallas kernels for 0%

commit v1 on v0

v1 whole, which is shorter than its diff:
```python
import functools
import jax
import jax.numpy as jnp
from jax import lax
from jax.experimental import pallas as pl
from jax.experimental.pallas import tpu as pltpu
from jax.sharding import PartitionSpec as P

NORM_EPS = 1e-05
DROP_RATE = 0.1
BF = jnp.bfloat16
F32 = jnp.float32
GELU_K = 0.7978845608
GELU_C = 0.044715
NN = (((1,), (0,)), ((), ()))
NT = (((1,), (1,)), ((), ()))
TN = (((0,), (0,)), ((), ()))


def dot(a, b, dims):
    return lax.dot_general(a, b, dims, preferred_element_type=F32)


def gelu_pair(v):
    u = v * v
    s = 0.5 * jnp.tanh(v * (GELU_K + (GELU_K * GELU_C) * u)) + 0.5
    h = v * s
    d = s + (h - h * s) * (2.0 * GELU_K + (6.0 * GELU_K * GELU_C) * u)
    return h, d


def fold8(x):
    rows = x.shape[0]
    total = x[0:8]
    for r in range(8, rows, 8):
        total = total + x[r : r + 8]
    return total


def lanes(x):
    total = x[:, 0:128]
    for c in range(128, x.shape[1], 128):
        total = total + x[:, c : c + 128]
    return total


def block_kernel(
    cfg,
    counts,
    keeps,
    tokens_hbm,
    cot_hbm,
    pool_ref,
    wt_ref,
    outer_ref,
    vec_ref,
    sp_ref,
    spt_ref,
    sbias_ref,
    out_hbm,
    ig_hbm,
    pooled_ref,
    inner_acc,
    outer_acc,
    vecg_ref,
    sg_ref,
    sbg_ref,
    off_s,
    gend_s,
    grows_s,
    x_all,
    c_all,
    normed_b,
    bg_b,
    h0_b,
    e0_b,
    mg_b,
    xm_b,
    u2_b,
    d1_b,
    stat_b,
    br_b,
    ng_b,
    h1_s,
    t_s,
    out_st,
    ig_st,
    vacc,
    in_sem,
    out_sem,
):
    images, patches, width, gate, rows_cap, tm, kw, classes = cfg
    nv = width // 512
    del nv
    cw = 256
    nj = gate // cw

    def vrow(base, j):
        start = base + j * cw
        return vec_ref[start // 512 : start // 512 + 1, start % 512 : start % 512 + cw]

    gain_one = vec_ref[0:1, :]
    shift_one = vec_ref[1:2, :]
    bias_out = vec_ref[2:3, :]
    g2_base, s2_base, b0_base, b1_base = 3 * width, 3 * width + gate, 3 * width + 2 * gate, 3 * width + 3 * gate

    def in_copies(b):
        return (
            pltpu.make_async_copy(tokens_hbm.at[b], x_all.at[b], in_sem.at[0, b]),
            pltpu.make_async_copy(cot_hbm.at[b], c_all.at[b], in_sem.at[1, b]),
        )

    for b in range(images):
        for cp in in_copies(b):
            cp.start()

    def plan(b, carry):
        group, row = carry
        need = keeps[b] * (((counts[b] + 15) // 16) * 16)
        over = (row + need > rows_cap).astype(jnp.int32)
        group = group + over
        row = jnp.where(over == 1, 0, row)
        off_s[b] = row
        row = row + need
        gend_s[group] = b + 1
        grows_s[group] = row
        return group, row

    last_group, _ = lax.fori_loop(0, images, plan, (jnp.int32(0), jnp.int32(0)))

    def zero_rows(ref, n_chunks, start):
        z = jnp.zeros((16, ref.shape[1]), ref.dtype)

        def body(i, c):
            ref[pl.ds(pl.multiple_of(start + i * 16, 16), 16), :] = z
            return c

        lax.fori_loop(0, n_chunks, body, 0)

    for ref in (normed_b, bg_b, h0_b, e0_b, mg_b, xm_b, u2_b, d1_b):
        zero_rows(ref, ref.shape[0] // 16, 0)
    vacc[...] = jnp.zeros_like(vacc)
    inner_acc[...] = jnp.zeros_like(inner_acc)
    outer_acc[...] = jnp.zeros_like(outer_acc)
    sg_ref[...] = jnp.zeros_like(sg_ref)
    sbg_ref[...] = jnp.zeros_like(sbg_ref)
    stat_b[...] = jnp.zeros_like(stat_b)

    row_chunks = [(r, min(32, patches - r)) for r in range(0, patches // 16 * 16, 32)]
    row_chunks = []
    r = 0
    full = patches // 16 * 16
    while r < full:
        step = min(32, full - r)
        row_chunks.append((r, step))
        r += step
    tail = (full, patches - full) if full < patches else None

    def load_rows(ref, b, r, rs):
        return ref[b, r : r + rs, :].astype(F32)

    def norm(x):
        c = x - jnp.mean(x, axis=-1, keepdims=True)
        inv = lax.rsqrt(jnp.mean(c * c, axis=-1, keepdims=True) + NORM_EPS)
        return c * inv, inv

    def row_ids(r, rs):
        return lax.broadcasted_iota(jnp.int32, (rs, 1), 0) + r

    def scale_of(b):
        return keeps[b].astype(F32) * (1.0 / (1.0 - DROP_RATE))

    def phase_in(b):
        for cp in in_copies(b):
            cp.wait()

        @pl.when(keeps[b] == 1)
        def _():
            n = counts[b]
            o = pl.multiple_of(off_s[b], 16)
            ks = scale_of(b)
            pool = pool_ref[b]
            bsum = jnp.zeros((8, width), F32)
            for r, rs in row_chunks + ([tail] if tail else []):
                x = load_rows(x_all, b, r, rs)
                c = load_rows(c_all, b, r, rs)
                unit, _ = norm(x)
                normed = unit * gain_one + shift_one
                valid = row_ids(r, rs) < n
                og = c + jnp.where(valid, pool, 0.0)
                bg = (ks * og).astype(BF).astype(F32)
                bgm = jnp.where(valid, bg, 0.0)
                if rs % 16:
                    pad = 16 - rs
                    z = jnp.zeros((pad, width), F32)
                    normed = jnp.concatenate([normed, z], axis=0)
                    bg = jnp.concatenate([bg, z], axis=0)
                    bgm = jnp.concatenate([bgm, z], axis=0)
                    rs = 16
                bsum = bsum + fold8(bg)
                normed_b[pl.ds(o + r, rs), :] = normed.astype(BF)
                bg_b[pl.ds(o + r, rs), :] = bgm.astype(BF)
            vacc[2] += bsum

    def phase_a(t):
        r0 = pl.multiple_of(t * tm, tm)
        rows = pl.ds(r0, tm)
        nb = normed_b[rows, :]
        bgt = bg_b[rows, :]
        s1 = jnp.zeros((tm, 128), F32)
        for j in range(nj):
            cols = slice(j * cw, (j + 1) * cw)
            a1 = dot(nb, wt_ref[1, cols, :], NT) + vrow(b1_base, j)
            h1, d1 = gelu_pair(a1)
            h1_s[:, cols] = h1
            d1_b[rows, cols] = d1.astype(BF)
            s1 = s1 + lanes(h1)
        mean = jnp.sum(s1, axis=1, keepdims=True) * (1.0 / gate)
        q1 = jnp.zeros((tm, 128), F32)
        rs1 = jnp.zeros((tm, 128), F32)
        for j in range(nj):
            cols = slice(j * cw, (j + 1) * cw)
            a0 = dot(nb, wt_ref[0, cols, :], NT) + vrow(b0_base, j)
            h0, d0 = gelu_pair(a0)
            gg = dot(bgt, outer_ref[cols, :], NT)
            mg = gg * h0
            h0_b[rows, cols] = h0.astype(BF)
            mg_b[rows, cols] = mg.astype(BF)
            e0_b[rows, cols] = (gg * d0).astype(BF)
            rs1 = rs1 + lanes(mg)
            c = h1_s[:, cols] - mean
            q1 = q1 + lanes(c * c)
        inv = lax.rsqrt(jnp.sum(q1, axis=1, keepdims=True) * (1.0 / gate) + NORM_EPS)
        stat_b[rows, 0:128] = jnp.broadcast_to(inv, (tm, 128))
        stat_b[rows, 128:256] = rs1
        for j in range(nj):
            cols = slice(j * cw, (j + 1) * cw)
            u2 = (h1_s[:, cols] - mean) * inv
            u2_b[rows, cols] = u2.astype(BF)
            xm_b[rows, cols] = (u2 * vrow(g2_base, j) + vrow(s2_base, j)).astype(BF)

    def phase_b(b, m):
        n = counts[b]
        o = pl.multiple_of(off_s[b], 16)
        need = ((n + 15) // 16) * 16
        rows = pl.ds(o, m)
        rid = lax.broadcasted_iota(jnp.int32, (m, 1), 0)
        cid = lax.broadcasted_iota(jnp.int32, (m, m), 1)
        rid2 = lax.broadcasted_iota(jnp.int32, (m, m), 0)
        both = (cid < n) & (rid2 < n)
        sp = jnp.where(both, sp_ref[0:m, 0:m], 0.0).astype(BF)
        spt = jnp.where(both, spt_ref[0:m, 0:m], 0.0).astype(BF)
        sbias = sbias_ref[0:m, :]
        inside = rid < need
        inv = stat_b[rows, 0:1]
        tsum = jnp.zeros((m, 128), F32)
        tdot = jnp.zeros((m, 128), F32)
        sg = jnp.zeros((m, m), F32)
        for j in range(nj):
            cols = slice(j * cw, (j + 1) * cw)
            xm = xm_b[rows, cols]
            mg = mg_b[rows, cols]
            so = dot(sp, xm, NN) + sbias
            so = jnp.where(inside, so, 1.0)
            mix = dot(spt, mg, NN)
            sg = sg + dot(mg, xm, NT)
            h0_b[rows, cols] = (h0_b[rows, cols].astype(F32) * so).astype(BF)
            e0_b[rows, cols] = (e0_b[rows, cols].astype(F32) * so).astype(BF)
            u2 = u2_b[rows, cols].astype(F32)
            mu = mix * u2
            gain = vrow(g2_base, j)
            t = mix * gain
            t_s[0:m, cols] = t
            tsum = tsum + lanes(t)
            tdot = tdot + lanes(mu * gain)
            start = j * cw
            vi = start // 512
            lo = start % 512
            vacc[3 + vi, :, lo : lo + cw] += fold8(mu)
            vacc[3 + gate // 512 + vi, :, lo : lo + cw] += fold8(mix)
        sg_ref[0:m, 0:m] += jnp.where(both, sg, 0.0)
        sbg_ref[0:m, :] += jnp.where(rid < n, stat_b[rows, 128:256], 0.0)
        m1 = jnp.sum(tsum, axis=1, keepdims=True) * (1.0 / gate)
        m2 = jnp.sum(tdot, axis=1, keepdims=True) * (1.0 / gate)
        for j in range(nj):
            cols = slice(j * cw, (j + 1) * cw)
            u2 = u2_b[rows, cols].astype(F32)
            sec = inv * (t_s[0:m, cols] - m1 - u2 * m2)
            sec = jnp.where(inside, sec, 1.0)
            d1_b[rows, cols] = (d1_b[rows, cols].astype(F32) * sec).astype(BF)

    def phase_c(t):
        r0 = pl.multiple_of(t * tm, tm)
        rows = pl.ds(r0, tm)
        br_b[rows, :] = dot(h0_b[rows, :], outer_ref[...], NN)
        ng_b[rows, :] = dot(e0_b[rows, :], wt_ref[0], NN) + dot(d1_b[rows, :], wt_ref[1], NN)
        base = b0_base // 512
        for a, ref in ((0, e0_b), (1, d1_b)):
            for v in range(gate // 512):
                part = ref[rows, v * 512 : (v + 1) * 512].astype(F32)
                vacc[base + a * (gate // 512) + v] += fold8(part)

    def phase_w(k):
        rows = pl.ds(pl.multiple_of(k * kw, kw), kw)
        nb = normed_b[rows, :]
        bgt = bg_b[rows, :]
        for j in range(gate // 256):
            cols = slice(j * 256, (j + 1) * 256)
            outer_acc[cols, :] += dot(h0_b[rows, cols], bgt, TN)
            inner_acc[0, cols, :] += dot(e0_b[rows, cols], nb, TN)
            inner_acc[1, cols, :] += dot(d1_b[rows, cols], nb, TN)

    def out_copies(b, slot):
        return (
            pltpu.make_async_copy(out_st.at[slot], out_hbm.at[b], out_sem.at[0, slot]),
            pltpu.make_async_copy(ig_st.at[slot], ig_hbm.at[b], out_sem.at[1, slot]),
        )

    def phase_d(b):
        slot = lax.rem(b, 2)

        @pl.when(b >= 2)
        def _():
            for cp in out_copies(b - 2, slot):
                cp.wait()

        n = counts[b]
        kn = keeps[b] * n
        o = pl.multiple_of(off_s[b], 16)
        ks = scale_of(b)
        pool = pool_ref[b]
        psum = jnp.zeros((8, width), F32)
        g1 = jnp.zeros((8, width), F32)
        s1 = jnp.zeros((8, width), F32)
        for r, rs in row_chunks + ([tail] if tail else []):
            x = load_rows(x_all, b, r, rs)
            c = load_rows(c_all, b, r, rs)
            unit, inv = norm(x)
            ids = row_ids(r, rs)
            valid = ids < n
            live = ids < kn
            og = c + jnp.where(valid, pool, 0.0)
            br = jnp.where(live, br_b[pl.ds(o + r, rs), :], 0.0)
            out = x + ks * (br + bias_out)
            out_st[slot, r : r + rs, :] = out
            ng = jnp.where(live, ng_b[pl.ds(o + r, rs), :], 0.0)
            t = ng * gain_one
            m1 = jnp.mean(t, axis=-1, keepdims=True)
            m2 = jnp.mean(t * unit, axis=-1, keepdims=True)
            ig_st[slot, r : r + rs, :] = og + inv * (t - m1 - unit * m2)
            ov = jnp.where(valid, out, 0.0)
            gu = ng * unit
            if rs % 8:
                z = jnp.zeros((8 - rs % 8, width), F32)
                ov = jnp.concatenate([ov, z], axis=0)
                gu = jnp.concatenate([gu, z], axis=0)
                ng = jnp.concatenate([ng, z], axis=0)
            psum = psum + fold8(ov)
            g1 = g1 + fold8(gu)
            s1 = s1 + fold8(ng)
        vacc[0] += g1
        vacc[1] += s1
        total = jnp.sum(psum, axis=0, keepdims=True)
        pooled_ref[b] = total / jnp.full((1, width), n.astype(F32), F32)
        for cp in out_copies(b, slot):
            cp.start()

    def group(g, b_start):
        b_end = gend_s[g]
        rows = grows_s[g]

        def loop(lo, hi, fn):
            def body(i, c):
                fn(i)
                return c

            lax.fori_loop(lo, hi, body, 0)

        loop(b_start, b_end, phase_in)
        zero_rows(normed_b, kw // 16, rows)
        zero_rows(bg_b, kw // 16, rows)
        tiles = (rows + tm - 1) // tm
        loop(0, tiles, phase_a)
        zero_rows(d1_b, tm // 16, rows)

        def do_b(b):
            n = counts[b]
            low = 0
            for m in classes:
                @pl.when((keeps[b] == 1) & (n > low) & (n <= m))
                def _(m=m):
                    phase_b(b, m)
                low = m

        loop(b_start, b_end, do_b)
        loop(0, tiles, phase_c)
        loop(0, (rows + kw - 1) // kw, phase_w)
        loop(b_start, b_end, phase_d)
        return b_end

    lax.fori_loop(0, last_group + 1, group, jnp.int32(0))
    for b in (images - 2, images - 1):
        for cp in out_copies(b, b % 2):
            cp.wait()
    vecg_ref[...] = jnp.sum(vacc[...], axis=1)


def run_block(counts, keeps, tokens, cot, pool, wt, outer, vec, sp, spt, sbias, *, rows_cap=1024, tm=128, kw=256, classes=(112, 160, 208)):
    images, patches, width = tokens.shape
    gate = outer.shape[0]
    pad = sp.shape[0]
    nvec = vec.shape[0]
    cap = rows_cap + 256
    cfg = (images, patches, width, gate, rows_cap, tm, kw, classes)
    smem = pl.BlockSpec(memory_space=pltpu.SMEM)
    vmem = pl.BlockSpec(memory_space=pltpu.VMEM)
    anyb = pl.BlockSpec(memory_space=pl.ANY)
    return pl.pallas_call(
        functools.partial(block_kernel, cfg),
        out_shape=(
            jax.ShapeDtypeStruct((images, patches, width), F32),
            jax.ShapeDtypeStruct((images, patches, width), F32),
            jax.ShapeDtypeStruct((images, 1, width), F32),
            jax.ShapeDtypeStruct((2, gate, width), F32),
            jax.ShapeDtypeStruct((gate, width), F32),
            jax.ShapeDtypeStruct((nvec, width), F32),
            jax.ShapeDtypeStruct((pad, pad), F32),
            jax.ShapeDtypeStruct((pad, 128), F32),
        ),
        in_specs=[smem, smem, anyb, anyb] + [vmem] * 7,
        out_specs=[anyb, anyb] + [vmem] * 6,
        scratch_shapes=[
            pltpu.SMEM((images,), jnp.int32),
            pltpu.SMEM((images,), jnp.int32),
            pltpu.SMEM((images,), jnp.int32),
            pltpu.VMEM((images, patches, width), BF),
            pltpu.VMEM((images, patches, width), BF),
            pltpu.VMEM((cap, width), BF),
            pltpu.VMEM((cap, width), BF),
        ]
        + [pltpu.VMEM((cap, gate), BF)] * 6
        + [
            pltpu.VMEM((cap, 256), F32),
            pltpu.VMEM((cap, width), F32),
            pltpu.VMEM((cap, width), F32),
            pltpu.VMEM((tm, gate), F32),
            pltpu.VMEM((pad, gate), F32),
            pltpu.VMEM((2, patches, width), F32),
            pltpu.VMEM((2, patches, width), F32),
            pltpu.VMEM((nvec, 8, width), F32),
            pltpu.SemaphoreType.DMA((2, images)),
            pltpu.SemaphoreType.DMA((2, 2)),
        ],
        compiler_params=pltpu.CompilerParams(vmem_limit_bytes=60 * 2**20),
        name="block",
    )(counts, keeps, tokens, cot, pool, wt, outer, vec, sp, spt, sbias)


STEP = 10
BETA_FIRST = 0.9
BETA_SECOND = 0.95
ADAM_EPS = 1e-08
DECAY_RATE = 0.05
RATE_MATRIX = 0.05
RATE_VECTOR = 0.8
CLIP_BOUND = 1.0
BOTH = ("dp", "fsdp")


def adam_step(weight, first, second, gradient, step_rate, weight_decay):
    first_new = BETA_FIRST * first + (1.0 - BETA_FIRST) * gradient
    second_new = BETA_SECOND * second + (1.0 - BETA_SECOND) * gradient * gradient
    first_hat = first_new / (1.0 - BETA_FIRST**STEP)
    second_hat = second_new / (1.0 - BETA_SECOND**STEP)
    weight_new = weight - step_rate * (
        first_hat / (jnp.sqrt(second_hat) + ADAM_EPS) + weight_decay * weight
    )
    return (weight_new, first_new, second_new)


def per_device(
    tokens,
    valid_mask,
    keep_mask,
    out_cotangent,
    pool_cotangent,
    inner_weight,
    outer_weight,
    vectors,
    spatial,
    inner_first,
    inner_second,
    outer_first,
    outer_second,
    vector_first,
    vector_second,
    spatial_first,
    spatial_second,
):
    images, patches, width = tokens.shape
    pad = (patches + 15) // 16 * 16
    wt = lax.all_gather(
        inner_weight.astype(BF).transpose(0, 2, 1), BOTH, axis=1, tiled=True
    )
    outer = lax.all_gather(outer_weight.astype(BF), BOTH, axis=0, tiled=True)
    vec = lax.all_gather(vectors.astype(BF), BOTH, axis=0, tiled=True)
    vec = vec.astype(F32).reshape(-1, width)
    counts = jnp.sum(valid_mask, axis=1)
    pool = (pool_cotangent.astype(F32) / counts.astype(F32)[:, None])[:, None, :]
    low = spatial[:patches].astype(BF)
    edge = ((0, pad - patches), (0, pad - patches))
    sp = jnp.pad(low, edge)
    spt = jnp.pad(low.T, edge)
    sbias = jnp.pad(spatial[patches][:, None], ((0, pad - patches), (0, 0)))
    output, input_grad, pooled, inner_g, outer_g, vec_g, sg, sbg = run_block(
        counts, keep_mask, tokens, out_cotangent, pool, wt, outer, vec, sp, spt, sbias
    )
    pooled = pooled.reshape(images, width)
    spatial_local = jnp.concatenate(
        [sg[:patches, :patches], jnp.sum(sbg[:patches], axis=1)[None, :]], axis=0
    )
    spatial_total = lax.psum(spatial_local, BOTH)
    vector_red = lax.psum_scatter(vec_g.reshape(-1), BOTH, scatter_dimension=0, tiled=True)
    inner_red = lax.psum_scatter(inner_g, BOTH, scatter_dimension=1, tiled=True)
    inner_red = inner_red.transpose(0, 2, 1)
    outer_red = lax.psum_scatter(outer_g, BOTH, scatter_dimension=0, tiled=True)
    shard_squares = (
        jnp.sum(inner_red * inner_red)
        + jnp.sum(outer_red * outer_red)
        + jnp.sum(vector_red * vector_red)
    )
    squares_total = lax.psum(shard_squares, BOTH)
    squares_total = squares_total + jnp.sum(spatial_total * spatial_total)
    grad_norm = jnp.sqrt(squares_total)
    clip_factor = CLIP_BOUND / jnp.maximum(grad_norm, CLIP_BOUND)
    inner_out = adam_step(
        inner_weight, inner_first, inner_second, inner_red * clip_factor, RATE_MATRIX, DECAY_RATE
    )
    outer_out = adam_step(
        outer_weight, outer_first, outer_second, outer_red * clip_factor, RATE_MATRIX, DECAY_RATE
    )
    vector_out = adam_step(
        vectors, vector_first, vector_second, vector_red * clip_factor, RATE_VECTOR, 0.0
    )
    row_index = jnp.arange(patches + 1)[:, None]
    spatial_rate = jnp.where(row_index < patches, RATE_MATRIX, RATE_VECTOR)
    spatial_decay = jnp.where(row_index < patches, DECAY_RATE, 0.0)
    spatial_out = adam_step(
        spatial,
        spatial_first,
        spatial_second,
        spatial_total * clip_factor,
        spatial_rate,
        spatial_decay,
    )
    return (
        (output, input_grad, pooled, grad_norm) + inner_out + outer_out + vector_out + spatial_out
    )


def solution(mesh):
    rows3 = P(BOTH, None, None)
    rows2 = P(BOTH, None)
    rows1 = P(BOTH)
    cols3 = P(None, None, BOTH)
    in_specs = (
        (rows3, rows2, rows1, rows3, rows2, cols3, rows2, rows1, P())
        + (cols3,) * 2
        + (rows2,) * 2
        + (rows1,) * 2
        + (P(),) * 2
    )
    out_specs = (
        (rows3, rows3, rows2, P()) + (cols3,) * 3 + (rows2,) * 3 + (rows1,) * 3 + (P(),) * 3
    )
    return jax.shard_map(
        per_device, mesh=mesh, in_specs=in_specs, out_specs=out_specs, check_vma=False
    )
```

time: 729 us -> 651 us (0.89); the launches traced: 721 us -> 651 us
  waiting for transfers between devices: 129 us -> 348 us
  matrix products: 187 us -> 0 us
  other arithmetic: 203 us -> 17 us
  Pallas kernels: 0 us -> 84.8 us
  local copies, waits for them, and re-layouts: 22.9 us -> 30.7 us
    dot_general x9 -> x0, matrix products: 187 us -> none  [the longest x1 34.3 us: per_device(): jnp.einsum('bpd,adg->abpg', normed, inner_all, preferred_element_type=jnp...]
    reduce_scatter x2, waiting for transfers between devices: 2.81 us -> 159 us  [the longest x1 117 us: per_device(): inner_red = lax.psum_scatter(inner_g, BOTH, scatter_dimension=1, tiled=True)]
    reduce_sum x9 -> x2, other arithmetic: 119 us -> 0.94 us  [the longest x1 0.83 us: per_device(): counts = jnp.sum(valid_mask, axis=1)]
    pallas_call x0 -> x1, Pallas kernels: none -> 84.8 us  [run_block(): pl.pallas_call(functools.partial(block_kernel, cfg), out_shape=(jax.Shape...]
    all_gather x3 -> x2, waiting for transfers between devices: 0.06 us -> 62.7 us  [the longest x1 61.6 us: per_device(): lax.all_gather(inner_weight.astype(BF).transpose(0, 2, 1), BOTH, axis=1,...]
    another operation x2 -> x0, other arithmetic: 59.9 us -> none  [per_device(): jnp.stack([first_grad, second_grad])]
    all_gather x2 -> x0, blocking collectives: 34.6 us -> none  [the longest x1 17.3 us: per_device(): inner_group = lax.all_gather(inner_low, 'fsdp', axis=2, tiled=True)]
    unnamed x2, blocking collectives: 82.7 us -> 110 us
  transfers between devices with their start and end apart: 6 -> 5, of which waited for: 2 -> 5; matrix products, arithmetic and copies ran while one was open for 55% -> 6% of each run, Pallas kernels for 0% -> 0%
where the time goes in v1:
time: 651 us
  waiting for transfers between devices  348 us (53%)
  blocking collectives  152 us (23%)
  Pallas kernels  84.8 us (13%)
  local copies, waits for them, and re-layouts  30.7 us (5%)
  between operations  18.5 us (3%)
  other arithmetic  17 us (3%)
    psum x1, waiting for transfers between devices, per_device(): spatial_total = lax.psum(spatial_local, BOTH)  126 us
    reduce_scatter x1, waiting for transfers between devices, per_device(): inner_red = lax.psum_scatter(inner_g, BOTH, scatter_dimension=1, tiled=True)  117 us
    unnamed x2, blocking collectives  110 us
    pallas_call x1, Pallas kernels, run_block(): pl.pallas_call(functools.partial(block_kernel, cfg), out_shape=(jax.Shape...  84.8 us
    all_gather x1, waiting for transfers between devices, per_device(): lax.all_gather(inner_weight.astype(BF).transpose(0, 2, 1), BOTH, axis=1,...  61.6 us
    reduce_scatter x1, waiting for transfers between devices, per_device(): outer_red = lax.psum_scatter(outer_g, BOTH, scatter_dimension=0, tiled=True)  42.1 us
    psum x1, blocking collectives, per_device(): squares_total = lax.psum(shard_squares, BOTH)  41.1 us
    unnamed x49, local copies, waits for them, and re-layouts  26.4 us
  transfers between devices with their start and end apart: 5, of which 5 were waited for; matrix products, arithmetic and copies ran while one was open for 6% of the time, Pallas kernels for 0%

profile of v1, /device:TPU:0, one launch (start us, length us, event | category | flops | bytes accessed | tf_op | source)
XLA Modules:
  0.0 651.4 jit_solution(2627947095956962477)
XLA Ops:
  7.2 0.0 all-gather.5.cloned.1.call-start
  7.2 1.5 convert_element_type.29
  8.7 0.0 all-gather.5.cloned.1.call-update
  8.8 0.0 all-gather.3.cloned.1.call-start
  8.8 1.6 convert_bitcast_fusion
  10.4 0.0 all-gather.3.cloned.1.call-update
  10.4 0.0 reduce-scatter.5.cloned.1.call-start
  10.5 0.9 slice.17
  11.4 0.1 copy.55
  11.5 0.1 copy.54
  11.6 0.7 pad.11.clone.sp_ref
  12.3 0.7 pad.12.spt_ref
  13.0 0.8 reduce_sum.54.counts
  13.8 0.8 convert_divide_fusion
  14.6 0.6 broadcast_in_dim.20.pool_ref
  15.3 5.7 copy.48.tokens_hbm
  21.0 3.5 copy.49.cot_hbm
  24.5 0.1 copy.47
  24.7 0.2 dynamic-update-slice
  24.9 42.1 %all-reduce.3 = bf16[7680]{0:T(1024)(128)(2,1)S(1)} all-reduce(bf16[7680]{0:T(1024)(128)(2,1)S(1)} %dynamic-update-slice), channel_id=1, replica_groups=mesh['dp'=4,'fsdp'=8] {'dp','fsdp'}, use_global_device_ids=true, to_apply=%add.3 | all-reduce | flops 7680 | bytes 30720
  67.1 0.6 reshape.61.vec_ref
  67.7 0.7 pad.13.sbias_ref
  68.4 1.1 all-gather.5.cloned.1.call-done.outer_ref
  69.5 61.6 %all-gather.3.cloned.1.call-done.wt_ref = bf16[2,1536,512]{2,1,0:T(8,128)(2,1)} async-done(((bf16[2,48,512]{2,1,0:T(8,128)(2,1)}), bf16[2,1536,512]{2,1,0:T(8,128)(2,1)}) %all-gather.3.cloned.1.call-update) | async-done | bytes 3145744 | tf_op jit(solution)/shard_map/all_gather | solution.py:502
  131.1 84.8 %block.1 = (f32[16,196,512]{2,1,0:T(8,128)}, f32[16,196,512]{2,1,0:T(8,128)}, f32[16,1,512]{2,1,0:T(1,128)}, f32[2,1536,512]{2,1,0:T(8,128)}, f32[1536,512]{1,0:...) custom-call(s32[16]{0:T(128)} %copy-done.14, s32[16]{0:T(128)} %keeps.1, ...), custom_call_target="tpu_custom_call" | custom-call | tf_op jit(solution)/shard_map/block/pallas_call | solution.py:418
  215.9 0.0 reduce-scatter.5.cloned.1.call-update
  215.9 0.0 copy-start.13
  215.9 0.0 reduce-scatter.3.cloned.1.call-start
  216.0 0.5 reduce-scatter.3.cloned.1.call-update
  216.5 0.3 all-reduce.7.cloned.1.call-start
  216.8 0.0 copy-done.6
  216.9 0.0 slice-start
  216.9 0.0 slice-start.1
  216.9 9.5 %copy.51 = f32[16,196,512]{2,0,1:T(8,128)} copy(f32[16,196,512]{2,1,0:T(8,128)} %get-tuple-element.64) | data formatting | bytes 12845056
  226.4 0.0 slice-done
  226.4 0.0 copy-start.9
  226.4 0.0 copy-start.16
  226.4 0.0 copy-start.17
  226.4 0.0 copy-start.3
  226.4 0.0 copy-start.10
  226.5 0.0 copy-start.11
  226.5 0.0 copy-start.1
  226.5 0.0 copy-start.7
  226.5 0.0 copy-start.8
  226.5 6.5 copy.52
  233.0 0.6 copy.57
  233.6 68.3 %all-reduce.4 = f32[7680]{0:T(1024)S(1)} all-reduce(f32[7680]{0:T(1024)S(1)} %reshape.59), channel_id=4, replica_groups=mesh['dp'=4,'fsdp'=8] {'dp','fsdp'}, use_global_device_ids=true, to_apply=%region_5.6.clone | all-reduce | flops 7680 | bytes 61440
  301.9 0.7 multiply_reduce_fusion.3
  302.6 0.0 copy-done.9
  302.6 0.1 slice_reduce_fusion
  302.7 0.7 pad_maximum_fusion
  303.4 0.0 all-reduce.7.cloned.1.call-update
  303.4 42.1 %reduce-scatter.5.cloned.1.call-done = f32[48,512]{1,0:T(8,128)} async-done(((f32[1536,512]{1,0:T(8,128)}), f32[48,512]{1,0:T(8,128)}) %reduce-scatter.5.cloned.1.call-update) | async-done | bytes 98320 | tf_op jit(solution)/shard_map/reduce_scatter | solution.py:526
  345.5 1.5 multiply_reduce_fusion.2
  347.0 117.4 %reduce-scatter.3.cloned.1.call-done = f32[2,48,512]{2,1,0:T(8,128)} async-done(((f32[2,1536,512]{2,1,0:T(8,128)}), f32[2,48,512]{2,1,0:T(8,128)}) %reduce-scatter.3.cloned.1.call-update) | async-done | bytes 196624 | tf_op jit(solution)/shard_map/reduce_scatter | solution.py:524
  464.5 1.6 multiply_reduce_fusion.1
  468.0 125.6 %all-reduce.7.cloned.1.call-done = f32[197,196]{1,0:T(8,128)} async-done(((f32[197,196]{1,0:T(8,128)}), f32[197,196]{1,0:T(8,128)}) %all-reduce.7.cloned.1.call-update) | async-done | bytes 154464 | tf_op jit(solution)/shard_map/psum | solution.py:522
  593.6 1.6 multiply_reduce_fusion
  595.2 41.1 %psum.14 = f32[]{:T(128)} all-reduce(f32[]{:T(128)S(6)} %add.86), channel_id=1, replica_groups=mesh['dp'=4,'fsdp'=8] {'dp','fsdp'}, use_global_device_ids=true, to_apply=%region_7.8 | all-reduce | flops 1 | bytes 8 | tf_op jit(solution)/shard_map/psum | solution.py:532
  637.7 0.7 multiply_subtract_fusion.3
  638.4 1.7 multiply_subtract_fusion.2
  640.0 0.0 copy-done.7
  640.0 1.8 multiply_subtract_fusion.1
  641.9 1.9 multiply_subtract_fusion
  (32 shorter events, 0.1 us)
Async XLA Ops:
  7.2 62.3 %all-gather.5.cloned.1.call-start = ((), (), s32[]{:S(2)}) async-start(), calls=%async_computation.3 | async-start | bytes 1622016 | tf_op jit(solution)/shard_map/all_gather | solution.py:505
  8.8 122.3 %all-gather.3.cloned.1.call-start = ((), (), s32[]{:S(2)}) async-start(), calls=%async_computation.2 | async-start | bytes 3244032 | tf_op jit(solution)/shard_map/all_gather | solution.py:502
  10.4 335.1 %reduce-scatter.5.cloned.1.call-start = ((), (), s32[]{:S(2)}) async-start(), calls=%async_computation.5 | async-start | bytes 3244032 | tf_op jit(solution)/shard_map/reduce_scatter | solution.py:526
  13.8 7.2 %copy-start.14 = (s32[16]{0:T(128)}, s32[16]{0:T(128)S(1)}, u32[]{:S(2)}) copy-start(s32[16]{0:T(128)S(1)} %reduce_sum.54.counts) | copy-start | bytes 196
  14.6 6.4 copy-start
  21.0 3.5 copy-start.2
  21.0 3.7 copy-start.15
  215.9 0.9 copy-start.13
  215.9 0.9 copy-start.6
  215.9 248.5 %reduce-scatter.3.cloned.1.call-start = ((), (), s32[]{:S(2)}) async-start(), calls=%async_computation.4 | async-start | bytes 6488064 | tf_op jit(solution)/shard_map/reduce_scatter | solution.py:524
  216.5 377.1 %all-reduce.7.cloned.1.call-start = ((), (), s32[]{:S(2)}) async-start(), calls=%async_computation.6 | async-start | bytes 409600 | tf_op jit(solution)/shard_map/psum | solution.py:522
  216.9 9.5 %slice-start = ((s8[6553600]{0:T(1024)(128)(4,1)}), s8[4194304]{0:T(1024)(128)(4,1)S(1)}, s32[]{:S(2)}) async-start(s8[6553600]{0:T(1024)(128)(4,1)} %bitcast.16), calls=%async_computation.7 | async-start | bytes 8388608
  216.9 9.5 %slice-start.1 = ((s8[6553600]{0:T(1024)(128)(4,1)}), s8[2359296]{0:T(1024)(128)(4,1)S(1)}, s32[]{:S(2)}) async-start(s8[6553600]{0:T(1024)(128)(4,1)} %bitcast.16), calls=%async_computation.8 | async-start | bytes 4718592
  226.4 6.6 %copy-start.12 = (f32[16,1,512]{2,1,0:T(1,128)S(1)}, f32[16,1,512]{2,1,0:T(1,128)}, u32[]{:S(2)}) copy-start(f32[16,1,512]{2,1,0:T(1,128)} %get-tuple-element.26) | copy-start | bytes 98308
  226.4 76.2 %copy-start.9 = (f32[208,128]{1,0:T(8,128)S(1)}, f32[208,128]{1,0:T(8,128)}, u32[]{:S(2)}) copy-start(f32[208,128]{1,0:T(8,128)} %get-tuple-element.31) | copy-start | bytes 319492
  226.4 411.3 %copy-start.16 = (f32[240]{0:T(256)S(1)}, f32[240]{0:T(256)}, u32[]{:S(2)}) copy-start(f32[240]{0:T(256)} %param.30) | copy-start | bytes 2884
  226.4 411.3 %copy-start.17 = (f32[240]{0:T(256)S(1)}, f32[240]{0:T(256)}, u32[]{:S(2)}) copy-start(f32[240]{0:T(256)} %param.31) | copy-start | bytes 2884
  226.4 411.9 %copy-start.3 = (f32[48,512]{1,0:T(8,128)S(1)}, f32[48,512]{1,0:T(8,128)}, u32[]{:S(2)}) copy-start(f32[48,512]{1,0:T(8,128)} %param.23) | copy-start | bytes 294916
  226.4 411.9 %copy-start.10 = (f32[48,512]{1,0:T(8,128)S(1)}, f32[48,512]{1,0:T(8,128)}, u32[]{:S(2)}) copy-start(f32[48,512]{1,0:T(8,128)} %param.28) | copy-start | bytes 294916
  226.5 411.9 %copy-start.11 = (f32[48,512]{1,0:T(8,128)S(1)}, f32[48,512]{1,0:T(8,128)}, u32[]{:S(2)}) copy-start(f32[48,512]{1,0:T(8,128)} %param.29) | copy-start | bytes 294916
  226.5 413.6 %copy-start.1 = (f32[2,512,48]{1,2,0:T(8,128)S(1)}, f32[2,512,48]{1,2,0:T(8,128)}, u32[]{:S(2)}) copy-start(f32[2,512,48]{1,2,0:T(8,128)} %param.22) | copy-start | bytes 589828
  226.5 413.6 %copy-start.7 = (f32[2,512,48]{1,2,0:T(8,128)S(1)}, f32[2,512,48]{1,2,0:T(8,128)}, u32[]{:S(2)}) copy-start(f32[2,512,48]{1,2,0:T(8,128)} %param.26) | copy-start | bytes 589828
  226.5 413.6 %copy-start.8 = (f32[2,512,48]{1,2,0:T(8,128)S(1)}, f32[2,512,48]{1,2,0:T(8,128)}, u32[]{:S(2)}) copy-start(f32[2,512,48]{1,2,0:T(8,128)} %param.27) | copy-start | bytes 589828
  233.0 408.9 %copy-start.4 = (f32[197,196]{1,0:T(8,128)S(1)}, f32[197,196]{1,0:T(8,128)}, u32[]{:S(2)}) copy-start(f32[197,196]{1,0:T(8,128)} %param.32) | copy-start | bytes 463348
  233.0 408.9 %copy-start.5 = (f32[197,196]{1,0:T(8,128)S(1)}, f32[197,196]{1,0:T(8,128)}, u32[]{:S(2)}) copy-start(f32[197,196]{1,0:T(8,128)} %param.33) | copy-start | bytes 463348
Sparse Core Ops, SparseCore 0:
  11.6 57.8 all-gather.4
  73.0 57.9 all-gather.2
  216.0 129.4 reduce-scatter.4
  351.0 113.4 reduce-scatter.2
  471.3 122.2 all-reduce.6

commit v2 on v1

--- a/solution.py
+++ b/solution.py
@@ -52,7 +52,6 @@
     cot_hbm,
     pool_ref,
     wt_ref,
-    outer_ref,
     vec_ref,
     sp_ref,
     spt_ref,
@@ -60,9 +59,9 @@
     out_hbm,
     ig_hbm,
     pooled_ref,
-    inner_acc,
-    outer_acc,
-    vecg_ref,
+    grads_hbm,
+    small_ref,
+    acc,
     sg_ref,
     sbg_ref,
     off_s,
@@ -88,6 +87,7 @@
     vacc,
     in_sem,
     out_sem,
+    grad_sem,
 ):
     images, patches, width, gate, rows_cap, tm, kw, classes = cfg
     nv = width // 512
@@ -140,8 +140,7 @@
     for ref in (normed_b, bg_b, h0_b, e0_b, mg_b, xm_b, u2_b, d1_b):
         zero_rows(ref, ref.shape[0] // 16, 0)
     vacc[...] = jnp.zeros_like(vacc)
-    inner_acc[...] = jnp.zeros_like(inner_acc)
-    outer_acc[...] = jnp.zeros_like(outer_acc)
+    acc[...] = jnp.zeros_like(acc)
     sg_ref[...] = jnp.zeros_like(sg_ref)
     sbg_ref[...] = jnp.zeros_like(sbg_ref)
     stat_b[...] = jnp.zeros_like(stat_b)
@@ -222,7 +221,7 @@
             cols = slice(j * cw, (j + 1) * cw)
             a0 = dot(nb, wt_ref[0, cols, :], NT) + vrow(b0_base, j)
             h0, d0 = gelu_pair(a0)
-            gg = dot(bgt, outer_ref[cols, :], NT)
+            gg = dot(bgt, wt_ref[2, cols, :], NT)
             mg = gg * h0
             h0_b[rows, cols] = h0.astype(BF)
             mg_b[rows, cols] = mg.astype(BF)
@@ -292,7 +291,7 @@
     def phase_c(t):
         r0 = pl.multiple_of(t * tm, tm)
         rows = pl.ds(r0, tm)
-        br_b[rows, :] = dot(h0_b[rows, :], outer_ref[...], NN)
+        br_b[rows, :] = dot(h0_b[rows, :], wt_ref[2], NN)
         ng_b[rows, :] = dot(e0_b[rows, :], wt_ref[0], NN) + dot(d1_b[rows, :], wt_ref[1], NN)
         base = b0_base // 512
         for a, ref in ((0, e0_b), (1, d1_b)):
@@ -306,9 +305,9 @@
         bgt = bg_b[rows, :]
         for j in range(gate // 256):
             cols = slice(j * 256, (j + 1) * 256)
-            outer_acc[cols, :] += dot(h0_b[rows, cols], bgt, TN)
-            inner_acc[0, cols, :] += dot(e0_b[rows, cols], nb, TN)
-            inner_acc[1, cols, :] += dot(d1_b[rows, cols], nb, TN)
+            acc[0, cols, :] += dot(e0_b[rows, cols], nb, TN)
+            acc[1, cols, :] += dot(d1_b[rows, cols], nb, TN)
+            acc[2, cols, :] += dot(h0_b[rows, cols], bgt, TN)
 
     def out_copies(b, slot):
         return (
@@ -402,12 +401,42 @@
     for b in (images - 2, images - 1):
         for cp in out_copies(b, b % 2):
             cp.wait()
-    vecg_ref[...] = jnp.sum(vacc[...], axis=1)
-
-
-def run_block(counts, keeps, tokens, cot, pool, wt, outer, vec, sp, spt, sbias, *, rows_cap=1024, tm=128, kw=256, classes=(112, 160, 208)):
+    half = gate // 2
+    copies = []
+    for i in range(6):
+        q, lo = i // 2, (i % 2) * half
+        buf = (normed_b, bg_b)[i % 2]
+        if i >= 2:
+            copies[i - 2].wait()
+        buf[0:half, :] = acc[q, lo : lo + half, :].astype(BF)
+        cp = pltpu.make_async_copy(
+            buf.at[pl.ds(0, half)], grads_hbm.at[q, pl.ds(lo, half)], grad_sem.at[i]
+        )
+        cp.start()
+        copies.append(cp)
+    small_ref[...] = jnp.zeros_like(small_ref)
+    sums = jnp.sum(vacc[...], axis=1)
+    for v in range(sums.shape[0]):
+        for h in range(width // 256):
+            row = v * (width // 256) + h
+            small_ref[row : row + 1, :] = sums[v : v + 1, h * 256 : (h + 1) * 256]
+    sg_row = 32
+    pad = sg_ref.shape[0]
+    small_ref[sg_row : sg_row + pad, 0:pad] = sg_ref[...]
+    bias = jnp.sum(sbg_ref[...], axis=1, keepdims=True)
+    wide = jnp.where(
+        lax.broadcasted_iota(jnp.int32, (pad, pad), 0) == lax.broadcasted_iota(jnp.int32, (pad, pad), 1),
+        bias,
+        0.0,
+    )
+    small_ref[sg_row + patches : sg_row + patches + 1, 0:pad] = jnp.sum(wide, axis=0, keepdims=True)
+    for cp in copies[4:]:
+        cp.wait()
+
+
+def run_block(counts, keeps, tokens, cot, pool, wt, vec, sp, spt, sbias, *, rows_cap=1024, tm=128, kw=256, classes=(112, 160, 208)):
     images, patches, width = tokens.shape
-    gate = outer.shape[0]
+    gate = wt.shape[1]
     pad = sp.shape[0]
     nvec = vec.shape[0]
     cap = rows_cap + 256
@@ -421,15 +450,15 @@
             jax.ShapeDtypeStruct((images, patches, width), F32),
             jax.ShapeDtypeStruct((images, patches, width), F32),
             jax.ShapeDtypeStruct((images, 1, width), F32),
-            jax.ShapeDtypeStruct((2, gate, width), F32),
-            jax.ShapeDtypeStruct((gate, width), F32),
-            jax.ShapeDtypeStruct((nvec, width), F32),
-            jax.ShapeDtypeStruct((pad, pad), F32),
-            jax.ShapeDtypeStruct((pad, 128), F32),
+            jax.ShapeDtypeStruct((3, gate, width), BF),
+            jax.ShapeDtypeStruct((256, 256), F32),
         ),
-        in_specs=[smem, smem, anyb, anyb] + [vmem] * 7,
-        out_specs=[anyb, anyb] + [vmem] * 6,
+        in_specs=[smem, smem, anyb, anyb] + [vmem] * 6,
+        out_specs=[anyb, anyb, vmem, anyb, vmem],
         scratch_shapes=[
+            pltpu.VMEM((3, gate, width), F32),
+            pltpu.VMEM((pad, pad), F32),
+            pltpu.VMEM((pad, 128), F32),
             pltpu.SMEM((images,), jnp.int32),
             pltpu.SMEM((images,), jnp.int32),
             pltpu.SMEM((images,), jnp.int32),
@@ -450,10 +479,376 @@
             pltpu.VMEM((nvec, 8, width), F32),
             pltpu.SemaphoreType.DMA((2, images)),
             pltpu.SemaphoreType.DMA((2, 2)),
+            pltpu.SemaphoreType.DMA((6,)),
         ],
         compiler_params=pltpu.CompilerParams(vmem_limit_bytes=60 * 2**20),
         name="block",
-    )(counts, keeps, tokens, cot, pool, wt, outer, vec, sp, spt, sbias)
+    )(counts, keeps, tokens, cot, pool, wt, vec, sp, spt, sbias)
+
+
+MESH = pl.DeviceIdType.MESH
+
+
+def place():
+    d = lax.axis_index("dp")
+    f = lax.axis_index("fsdp")
+    return d % 2, d // 2, f // 2, f % 2
+
+
+def device(x, y, z, c):
+    return (y * 2 + x, z * 2 + c)
+
+
+def greet_all():
+    d = lax.axis_index("dp")
+    f = lax.axis_index("fsdp")
+    barrier = pltpu.get_barrier_semaphore()
+    total = 32
+    me = d * 8 + f
+
+    def body(k, carry):
+        peer = (me + k) % total
+        pl.semaphore_signal(
+            barrier, inc=1, device_id=(peer // 8, peer % 8), device_id_type=MESH
+        )
+        return carry
+
+    lax.fori_loop(1, total, body, 0)
+    pl.semaphore_wait(barrier, total - 1)
+
+
+def gather_kernel(inner_ref, outer_ref, vec_ref, all_ref, vecs_ref, own, vown, send, recv, vsend, vrecv, lsem):
+    x, y, z, c = place()
+    own[0] = inner_ref[0].astype(BF)
+    own[1] = inner_ref[1].astype(BF)
+    own[2] = outer_ref[...].astype(BF)
+    vown[...] = vec_ref[...].astype(BF).astype(F32)
+    greet_all()
+    me = (y * 2 + x) * 8 + z * 2 + c
+    local = pltpu.make_async_copy(own, all_ref.at[:, y, x, z, c], lsem.at[0])
+    local.start()
+    vlocal = pltpu.make_async_copy(vown, vecs_ref.at[me], lsem.at[1])
+    vlocal.start()
+
+    px, py = jnp.where(c == 0, 1 - x, x), jnp.where(c == 0, y, 1 - y)
+    rx, ry = jnp.where(c == 0, x, 1 - x), jnp.where(c == 0, 1 - y, y)
+    dx, dy = 1 - x, 1 - y
+    index = [0]
+
+    def remote(src, dst, dev):
+        k = index[0]
+        index[0] += 1
+        return pltpu.make_async_remote_copy(
+            src_ref=src, dst_ref=dst, send_sem=send.at[k], recv_sem=recv.at[k],
+            device_id=dev, device_id_type=MESH,
+        )
+
+    pnbr, rnbr, core = device(px, py, z, c), device(rx, ry, z, c), device(x, y, z, 1 - c)
+
+    def line(q, ly, lx):
+        return all_ref.at[q, ly, lx, :, c]
+
+    def z_sends(q, src, by, bx):
+        return [
+            remote(src, all_ref.at[q, by, bx, z, c], device(x, y, (z + k) % 4, c)) for k in (1, 2, 3)
+        ]
+
+    def send_line(q, ly, lx, dev):
+        return remote(line(q, ly, lx), line(q, ly, lx), dev)
+
+    started = []
+
+    def go(cps):
+        for cp in cps:
+            cp.start()
+            started.append(cp)
+
+    own2 = remote(own.at[2], all_ref.at[2, y, x, z, c], pnbr)
+    go([own2])
+    zs = {}
+    for q in (0, 1):
+        zs[q] = z_sends(q, own.at[q], y, x)
+        go(zs[q])
+    zs[2] = z_sends(2, own.at[2], y, x)
+    go(zs[2])
+    def vbody(k, carry):
+        peer = (me + k) % 32
+        pltpu.make_async_remote_copy(
+            src_ref=vown, dst_ref=vecs_ref.at[me], send_sem=vsend, recv_sem=vrecv,
+            device_id=(peer // 8, peer % 8), device_id_type=MESH,
+        ).start()
+        return carry
+    lax.fori_loop(1, 32, vbody, 0)
+    local.wait()
+    vlocal.wait()
+    own2.wait_recv()
+    zp2 = z_sends(2, all_ref.at[2, py, px, z, c], py, px)
+    go(zp2)
+    lines_p, lines_r, lines_r2 = {}, {}, {}
+    cores = []
+    for q in (0, 1, 2):
+        for cp in zs[q]:
+            cp.wait_recv()
+        if q < 2:
+            lines_p[q] = send_line(q, y, x, pnbr)
+            go([lines_p[q]])
+        lines_r[q] = send_line(q, y, x, rnbr)
+        cp = send_line(q, y, x, core)
+        cores.append(cp)
+        go([lines_r[q], cp])
+    for q in (0, 1, 2):
+        if q < 2:
+            lines_p[q].wait_recv()
+        else:
+            for cp in zp2:
+                cp.wait_recv()
+        lines_r2[q] = send_line(q, py, px, rnbr)
+        cp = send_line(q, py, px, core)
+        cores.append(cp)
+        go([lines_r2[q], cp])
+    for q in (0, 1, 2):
+        lines_r[q].wait_recv()
+        cp = send_line(q, ry, rx, core)
+        cores.append(cp)
+        go([cp])
+    for q in (0, 1, 2):
+        lines_r2[q].wait_recv()
+        cp = send_line(q, dy, dx, core)
+        cores.append(cp)
+        go([cp])
+    for cp in cores:
+        cp.wait_recv()
+    for cp in started:
+        cp.wait_send()
+    allv = pltpu.make_async_copy(vecs_ref.at[pl.ds(0, 31)], vecs_ref.at[pl.ds(0, 31)], vrecv)
+    allv.wait()
+    pltpu.make_async_copy(vecs_ref.at[pl.ds(0, 31)], vecs_ref.at[pl.ds(0, 31)], vsend).wait()
+
+
+NSEND = 33
+
+
+def gather_all(inner, outer, vec, space=pl.ANY):
+    rows, width = outer.shape
+    vmem = pl.BlockSpec(memory_space=pltpu.VMEM)
+    sp = pl.BlockSpec(memory_space=space)
+    return pl.pallas_call(
+        gather_kernel,
+        out_shape=(
+            jax.ShapeDtypeStruct((3, 2, 2, 4, 2, rows, width), BF),
+            jax.ShapeDtypeStruct((32, 8, 128), F32),
+        ),
+        in_specs=[vmem] * 3,
+        out_specs=[sp, sp],
+        scratch_shapes=[
+            pltpu.VMEM((3, rows, width), BF),
+            pltpu.VMEM((8, 128), F32),
+            pltpu.SemaphoreType.DMA((NSEND,)),
+            pltpu.SemaphoreType.DMA((NSEND,)),
+            pltpu.SemaphoreType.DMA,
+            pltpu.SemaphoreType.DMA,
+            pltpu.SemaphoreType.DMA((2,)),
+        ],
+        compiler_params=pltpu.CompilerParams(collective_id=0, has_side_effects=True, vmem_limit_bytes=40 * 2**20),
+        name="gather",
+    )(inner, outer, vec)
+
+
+def reduce_kernel(
+    g_hbm, small_ref, red_ref, tot_ref, norm_ref,
+    acc, rc, rr, rp, rz, rz2, rb, stage, sbuf, sred, nbuf, nown,
+    send, recv, lsem, s1s, s1r, s2s, s2r, ns, nr,
+):
+    x, y, z, c = place()
+    me = (y * 2 + x) * 8 + z * 2 + c
+    px, py = jnp.where(c == 0, 1 - x, x), jnp.where(c == 0, y, 1 - y)
+    rx, ry = jnp.where(c == 0, x, 1 - x), jnp.where(c == 0, 1 - y, y)
+    dx, dy = 1 - x, 1 - y
+    pnbr, rnbr, core = device(px, py, z, c), device(rx, ry, z, c), device(x, y, z, 1 - c)
+    lines = ((ry, rx), (dy, dx), (y, x), (py, px))
+    loads = [pltpu.make_async_copy(g_hbm.at[q, :, :, :, c], acc.at[q], lsem.at[q]) for q in range(3)]
+    for cp in loads:
+        cp.start()
+    greet_all()
+    index = [0]
+    started = []
+
+    def remote(src, dst, dev):
+        k = index[0]
+        index[0] += 1
+        cp = pltpu.make_async_remote_copy(
+            src_ref=src, dst_ref=dst, send_sem=send.at[k], recv_sem=recv.at[k],
+            device_id=dev, device_id_type=MESH,
+        )
+        cp.start()
+        started.append(cp)
+        return cp
+
+    swaps = {}
+    for i, (ly, lx) in enumerate(lines):
+        for q in range(3):
+            swaps[q, i] = None
+    for i, (ly, lx) in enumerate(((dy, dx), (ry, rx), (py, px), (y, x))):
+        for q in range(3):
+            swaps[q, i] = remote(g_hbm.at[q, ly, lx, :, 1 - c], rc.at[q, ly, lx], core)
+
+    def broadcast(src, dst_at, ssem, rsem):
+        def body(k, carry):
+            peer = (me + k) % 32
+            pltpu.make_async_remote_copy(
+                src_ref=src(peer), dst_ref=dst_at, send_sem=ssem, recv_sem=rsem,
+                device_id=(peer // 8, peer % 8), device_id_type=MESH,
+            ).start()
+            return carry
+        lax.fori_loop(1, 32, body, 0)
+
+    def wait31(ref, sem):
+        view = ref.at[pl.ds(0, 31)]
+        pltpu.make_async_copy(view, view, sem).wait()
+
+    broadcast(lambda p: small_ref.at[p], sbuf.at[me], s1s, s1r)
+    for cp in loads:
+        cp.wait()
+
+    def add_line(q, ly, lx, ref):
+        for b in range(4):
+            acc[q, ly, lx, b] = (acc[q, ly, lx, b].astype(F32) + ref[b].astype(F32)).astype(BF)
+
+    first = {}
+    for q in range(3):
+        swaps[q, 0].wait_recv()
+        add_line(q, dy, dx, rc.at[q, dy, dx])
+        first[q, 0] = remote(acc.at[q, dy, dx], rr.at[q, 0], rnbr)
+    for i in (1, 2):
+        for q in range(3):
+            swaps[q, i].wait_recv()
+    for q in range(3):
+        add_line(q, ry, rx, rc.at[q, ry, rx])
+        first[q, 1] = remote(acc.at[q, ry, rx], rr.at[q, 1], rnbr)
+    for q in range(3):
+        add_line(q, py, px, rc.at[q, py, px])
+        swaps[q, 3].wait_recv()
+        add_line(q, y, x, rc.at[q, y, x])
+    second = {}
+    for q in (2, 0, 1):
+        first[q, 0].wait_recv()
+        add_line(q, py, px, rr.at[q, 0])
+        if q < 2:
+            second[q] = remote(acc.at[q, py, px], rp.at[q], pnbr)
+        else:
+            second[q] = [
+                remote(acc.at[q, py, px, (z + k) % 4], rz2.at[k - 1], device(x, y, (z + k) % 4, c)) for k in (1, 2, 3)
+            ]
+    own2 = None
+    for q in (2, 0, 1):
+        first[q, 1].wait_recv()
+        add_line(q, y, x, rr.at[q, 1])
+        if q == 2:
+            own2 = [
+                remote(acc.at[q, y, x, (z + k) % 4], rz.at[q, k - 1], device(x, y, (z + k) % 4, c)) for k in (1, 2, 3)
+            ]
+    third = {}
+    for q in (0, 1):
+        second[q].wait_recv()
+        add_line(q, y, x, rp.at[q])
+        third[q] = [
+            remote(acc.at[q, y, x, (z + k) % 4], rz.at[q, k - 1], device(x, y, (z + k) % 4, c)) for k in (1, 2, 3)
+        ]
+    for cp in second[2]:
+        cp.wait_recv()
+    stage[...] = (
+        acc[2, py, px, z].astype(F32) + rz2[0].astype(F32) + rz2[1].astype(F32) + rz2[2].astype(F32)
+    ).astype(BF)
+    last = remote(stage, rb, pnbr)
+    sbuf[me] = small_ref[me]
+    wait31(sbuf, s1r)
+    total = sbuf[0]
+    for k in range(1, 32):
+        total = total + sbuf[k]
+    sred[...] = total
+    tot_ref[me] = total
+    broadcast(lambda p: sred, tot_ref.at[me], s2s, s2r)
+    sq = jnp.zeros((8, 128), F32)
+
+    def fold(v):
+        t = jnp.zeros((8, 128), F32)
+        for r in range(0, v.shape[0], 8):
+            for l in range(0, v.shape[1], 128):
+                p = v[r : r + 8, l : l + 128]
+                t = t + p * p
+        return t
+
+    sq = sq + fold(total)
+    for cp in own2:
+        cp.wait_recv()
+    for q in (0, 1):
+        for cp in third[q]:
+            cp.wait_recv()
+        v = (
+            acc[q, y, x, z].astype(F32) + rz[q, 0].astype(F32) + rz[q, 1].astype(F32) + rz[q, 2].astype(F32)
+        )
+        red_ref[q] = v
+        sq = sq + fold(v)
+    last.wait_recv()
+    v = (
+        acc[2, y, x, z].astype(F32) + rz[2, 0].astype(F32) + rz[2, 1].astype(F32) + rz[2, 2].astype(F32)
+    ) + rb[...].astype(F32)
+    red_ref[2] = v
+    sq = sq + fold(v)
+    nown[...] = sq
+    nbuf[me] = sq
+    broadcast(lambda p: nown, nbuf.at[me], ns, nr)
+    wait31(nbuf, nr)
+    wait31(tot_ref, s2r)
+    t = nbuf[0]
+    for k in range(1, 32):
+        t = t + nbuf[k]
+    t = jnp.sum(jnp.sum(t, axis=0, keepdims=True), axis=1, keepdims=True)
+    norm_ref[...] = jnp.broadcast_to(jnp.sqrt(t), (8, 128))
+    for cp in started:
+        cp.wait_send()
+    wait31(sbuf, s1s)
+    wait31(tot_ref, s2s)
+    wait31(nbuf, ns)
+
+
+NRED = 12 + 6 + 2 + 3 + 3 + 6 + 1
+
+
+def reduce_all(g, small):
+    rows, width = g.shape[-2:]
+    vmem = pl.BlockSpec(memory_space=pltpu.VMEM)
+    anyb = pl.BlockSpec(memory_space=pl.ANY)
+    dma = pltpu.SemaphoreType.DMA
+    blk = (rows, width)
+    return pl.pallas_call(
+        reduce_kernel,
+        out_shape=(
+            jax.ShapeDtypeStruct((3,) + blk, F32),
+            jax.ShapeDtypeStruct(small.shape, F32),
+            jax.ShapeDtypeStruct((8, 128), F32),
+        ),
+        in_specs=[anyb, vmem],
+        out_specs=[vmem] * 3,
+        scratch_shapes=[
+            pltpu.VMEM((3, 2, 2, 4) + blk, BF),
+            pltpu.VMEM((3, 2, 2, 4) + blk, BF),
+            pltpu.VMEM((3, 2, 4) + blk, BF),
+            pltpu.VMEM((2, 4) + blk, BF),
+            pltpu.VMEM((3, 3) + blk, BF),
+            pltpu.VMEM((3,) + blk, BF),
+            pltpu.VMEM(blk, BF),
+            pltpu.VMEM(blk, BF),
+            pltpu.VMEM(small.shape, F32),
+            pltpu.VMEM(small.shape[1:], F32),
+            pltpu.VMEM((32, 8, 128), F32),
+            pltpu.VMEM((8, 128), F32),
+            dma((NRED,)), dma((NRED,)), dma((3,)),
+            dma, dma, dma, dma, dma, dma,
+        ],
+        compiler_params=pltpu.CompilerParams(collective_id=1, has_side_effects=True, vmem_limit_bytes=40 * 2**20),
+        name="reduce",
+    )(g, small)
 
 
 STEP = 10
@@ -465,20 +860,80 @@
 RATE_VECTOR = 0.8
 CLIP_BOUND = 1.0
 BOTH = ("dp", "fsdp")
+SPATIAL_ROW = 32
 
 
 def adam_step(weight, first, second, gradient, step_rate, weight_decay):
     first_new = BETA_FIRST * first + (1.0 - BETA_FIRST) * gradient
     second_new = BETA_SECOND * second + (1.0 - BETA_SECOND) * gradient * gradient
-    first_hat = first_new / (1.0 - BETA_FIRST**STEP)
-    second_hat = second_new / (1.0 - BETA_SECOND**STEP)
+    first_hat = first_new * (1.0 / (1.0 - BETA_FIRST**STEP))
+    second_hat = second_new * (1.0 / (1.0 - BETA_SECOND**STEP))
     weight_new = weight - step_rate * (
         first_hat / (jnp.sqrt(second_hat) + ADAM_EPS) + weight_decay * weight
     )
     return (weight_new, first_new, second_new)
 
 
+def adam_kernel(red, tot, norm, iw, i1, i2, ow, o1, o2, sw, s1, s2, *outs):
+    clip = CLIP_BOUND / jnp.maximum(norm[0:1, 0:1], CLIP_BOUND)
+    rows = ow.shape[0]
+    for q in range(2):
+        for r in range(0, rows, 8):
+            cut = slice(r, r + 8)
+            new = adam_step(
+                iw[q, cut], i1[q, cut], i2[q, cut], red[q, cut] * clip, RATE_MATRIX, DECAY_RATE
+            )
+            for ref, val in zip(outs[0:3], new):
+                ref[q, cut] = val
+    for r in range(0, rows, 8):
+        cut = slice(r, r + 8)
+        new = adam_step(ow[cut], o1[cut], o2[cut], red[2, cut] * clip, RATE_MATRIX, DECAY_RATE)
+        for ref, val in zip(outs[3:6], new):
+            ref[cut] = val
+    side, cols = sw.shape
+    grad = tot[SPATIAL_ROW : SPATIAL_ROW + side, 0:cols] * clip
+    last = lax.broadcasted_iota(jnp.int32, (side, 1), 0) == side - 1
+    rate = jnp.where(last, RATE_VECTOR, RATE_MATRIX)
+    decay = jnp.where(last, 0.0, DECAY_RATE)
+    new = adam_step(sw[...], s1[...], s2[...], grad, rate, decay)
+    for ref, val in zip(outs[6:9], new):
+        ref[...] = val
+
+
+def adam_all(red, tot, norm, inner, outer, spatial):
+    vmem = pl.BlockSpec(memory_space=pltpu.VMEM)
+    shape = lambda a: jax.ShapeDtypeStruct(a.shape, F32)
+    return pl.pallas_call(
+        adam_kernel,
+        out_shape=tuple(shape(a) for a in inner + outer + spatial),
+        in_specs=[vmem] * 12,
+        out_specs=[vmem] * 9,
+        compiler_params=pltpu.CompilerParams(vmem_limit_bytes=32 * 2**20),
+        name="adam",
+    )(red, tot, norm, *inner, *outer, *spatial)
+
+
+def slow_gather(inner_t, outer_weight, vectors):
+    wt = jnp.concatenate(
+        [
+            lax.all_gather(inner_t.astype(BF), BOTH, axis=1, tiled=True),
+            lax.all_gather(outer_weight.astype(BF), BOTH, axis=0, tiled=True)[None],
+        ],
+        axis=0,
+    )
+    vec = lax.all_gather(vectors.astype(BF), BOTH, axis=0, tiled=True).astype(F32)
+    return wt, vec
+
+
+def slow_reduce(grads, small):
+    red = lax.psum_scatter(grads.astype(F32), BOTH, scatter_dimension=1, tiled=True)
+    tot = lax.psum(small, BOTH)
+    squares = lax.psum(jnp.sum(red * red), BOTH) + jnp.sum(tot * tot)
+    return red, tot, jnp.broadcast_to(jnp.sqrt(squares), (8, 128))
+
+
 def per_device(
+    fast,
     tokens,
     valid_mask,
     keep_mask,
@@ -499,12 +954,18 @@
 ):
     images, patches, width = tokens.shape
     pad = (patches + 15) // 16 * 16
-    wt = lax.all_gather(
-        inner_weight.astype(BF).transpose(0, 2, 1), BOTH, axis=1, tiled=True
-    )
-    outer = lax.all_gather(outer_weight.astype(BF), BOTH, axis=0, tiled=True)
-    vec = lax.all_gather(vectors.astype(BF), BOTH, axis=0, tiled=True)
-    vec = vec.astype(F32).reshape(-1, width)
+    own = vectors.shape[0]
+    rows = outer_weight.shape[0]
+    inner_t = tuple(a.transpose(0, 2, 1) for a in (inner_weight, inner_first, inner_second))
+    if fast:
+        wt, vec = gather_all(
+            inner_t[0], outer_weight, jnp.pad(vectors, (0, 1024 - own)).reshape(8, 128)
+        )
+        wt = wt.reshape(3, 32 * rows, width)
+        vec = vec.reshape(32, 1024)[:, :own]
+    else:
+        wt, vec = slow_gather(inner_t[0], outer_weight, vectors)
+    vec = vec.reshape(-1, width)
     counts = jnp.sum(valid_mask, axis=1)
     pool = (pool_cotangent.astype(F32) / counts.astype(F32)[:, None])[:, None, :]
     low = spatial[:patches].astype(BF)
@@ -512,53 +973,44 @@
     sp = jnp.pad(low, edge)
     spt = jnp.pad(low.T, edge)
     sbias = jnp.pad(spatial[patches][:, None], ((0, pad - patches), (0, 0)))
-    output, input_grad, pooled, inner_g, outer_g, vec_g, sg, sbg = run_block(
-        counts, keep_mask, tokens, out_cotangent, pool, wt, outer, vec, sp, spt, sbias
+    output, input_grad, pooled, grads, small = run_block(
+        counts, keep_mask, tokens, out_cotangent, pool, wt, vec, sp, spt, sbias
     )
     pooled = pooled.reshape(images, width)
-    spatial_local = jnp.concatenate(
-        [sg[:patches, :patches], jnp.sum(sbg[:patches], axis=1)[None, :]], axis=0
+    if fast:
+        red, tot, norm = reduce_all(
+            grads.reshape(3, 2, 2, 4, 2, rows, width), small.reshape(32, 8, 256)
+        )
+        tot = tot.reshape(256, 256)
+    else:
+        red, tot, norm = slow_reduce(grads, small)
+    new = adam_all(
+        red,
+        tot,
+        norm,
+        inner_t,
+        (outer_weight, outer_first, outer_second),
+        (spatial, spatial_first, spatial_second),
     )
-    spatial_total = lax.psum(spatial_local, BOTH)
-    vector_red = lax.psum_scatter(vec_g.reshape(-1), BOTH, scatter_dimension=0, tiled=True)
-    inner_red = lax.psum_scatter(inner_g, BOTH, scatter_dimension=1, tiled=True)
-    inner_red = inner_red.transpose(0, 2, 1)
-    outer_red = lax.psum_scatter(outer_g, BOTH, scatter_dimension=0, tiled=True)
-    shard_squares = (
-        jnp.sum(inner_red * inner_red)
-        + jnp.sum(outer_red * outer_red)
-        + jnp.sum(vector_red * vector_red)
-    )
-    squares_total = lax.psum(shard_squares, BOTH)
-    squares_total = squares_total + jnp.sum(spatial_total * spatial_total)
-    grad_norm = jnp.sqrt(squares_total)
+    grad_norm = norm[0, 0]
     clip_factor = CLIP_BOUND / jnp.maximum(grad_norm, CLIP_BOUND)
-    inner_out = adam_step(
-        inner_weight, inner_first, inner_second, inner_red * clip_factor, RATE_MATRIX, DECAY_RATE
-    )
-    outer_out = adam_step(
-        outer_weight, outer_first, outer_second, outer_red * clip_factor, RATE_MATRIX, DECAY_RATE
-    )
+    me = lax.axis_index("dp") * lax.axis_size("fsdp") + lax.axis_index("fsdp")
+    flat = tot[: vec.size // 256].reshape(-1)
+    vector_red = lax.dynamic_slice(flat, (me * own,), (own,))
     vector_out = adam_step(
         vectors, vector_first, vector_second, vector_red * clip_factor, RATE_VECTOR, 0.0
     )
-    row_index = jnp.arange(patches + 1)[:, None]
-    spatial_rate = jnp.where(row_index < patches, RATE_MATRIX, RATE_VECTOR)
-    spatial_decay = jnp.where(row_index < patches, DECAY_RATE, 0.0)
-    spatial_out = adam_step(
-        spatial,
-        spatial_first,
-        spatial_second,
-        spatial_total * clip_factor,
-        spatial_rate,
-        spatial_decay,
+    return (
+        (output, input_grad, pooled, grad_norm)
+        + tuple(a.transpose(0, 2, 1) for a in new[0:3])
+        + tuple(new[3:6])
+        + vector_out
+        + tuple(new[6:9])
     )
-    return (
-        (output, input_grad, pooled, grad_norm) + inner_out + outer_out + vector_out + spatial_out
-    )
 
 
 def solution(mesh):
+    fast = mesh.shape["dp"] == 4 and mesh.shape["fsdp"] == 8
     rows3 = P(BOTH, None, None)
     rows2 = P(BOTH, None)
     rows1 = P(BOTH)
@@ -574,5 +1026,9 @@
         (rows3, rows3, rows2, P()) + (cols3,) * 3 + (rows2,) * 3 + (rows1,) * 3 + (P(),) * 3
     )
     return jax.shard_map(
-        per_device, mesh=mesh, in_specs=in_specs, out_specs=out_specs, check_vma=False
+        functools.partial(per_device, fast),
+        mesh=mesh,
+        in_specs=in_specs,
+        out_specs=out_specs,
+        check_vma=False,
     )

time: 651 us -> 242 us (0.37)
  waiting for transfers between devices: 348 us -> 0 us
  blocking collectives: 152 us -> 0 us
  Pallas kernels: 84.8 us -> 197 us
  between operations: 18.5 us -> 1.62 us
  other arithmetic: 17 us -> 2.45 us
  local copies, waits for them, and re-layouts: 30.7 us -> 41.3 us
    reduce_scatter x2 -> x0, waiting for transfers between devices: 159 us -> none  [the longest x1 117 us: per_device(): inner_red = lax.psum_scatter(inner_g, BOTH, scatter_dimension=1, tiled=True)]
    psum x1 -> x0, waiting for transfers between devices: 126 us -> none  [per_device(): spatial_total = lax.psum(spatial_local, BOTH)]
    unnamed x2 -> x0, blocking collectives: 110 us -> none
    pallas_call x0 -> x3, Pallas kernels: none -> 86.9 us  [the longest x1 49 us: reduce_all(): pl.pallas_call(reduce_kernel, out_shape=(jax.ShapeDtypeStruct((3,) + blk,...]
    all_gather x2 -> x0, waiting for transfers between devices: 62.7 us -> none  [the longest x1 61.6 us: per_device(): lax.all_gather(inner_weight.astype(BF).transpose(0, 2, 1), BOTH, axis=1,...]
    psum x1 -> x0, blocking collectives: 41.1 us -> none  [per_device(): squares_total = lax.psum(shard_squares, BOTH)]
    pallas_call x1, Pallas kernels: 84.8 us -> 110 us  [run_block(): pl.pallas_call(functools.partial(block_kernel, cfg), out_shape=(jax.Shape...]
    unnamed x49 -> x48, local copies, waits for them, and re-layouts: 26.4 us -> 35.7 us
  transfers between devices with their start and end apart: 5 -> 0, of which waited for: 5 -> 0; matrix products, arithmetic and copies ran while one was open for 6% -> 0% of each run, Pallas kernels for 0% -> 0%
where the time goes in v2:
time: 242 us
  Pallas kernels  197 us (81%)
  local copies, waits for them, and re-layouts  41.3 us (17%)
  other arithmetic  2.45 us (1%)
    pallas_call x1, Pallas kernels, run_block(): pl.pallas_call(functools.partial(block_kernel, cfg), out_shape=(jax.Shape...  110 us
    pallas_call x1, Pallas kernels, reduce_all(): pl.pallas_call(reduce_kernel, out_shape=(jax.ShapeDtypeStruct((3,) + blk,...  49 us
    pallas_call x1, Pallas kernels, gather_all(): pl.pallas_call(gather_kernel, out_shape=(jax.ShapeDtypeStruct((3, 2, 2, 4...  36.6 us
    unnamed x48, local copies, waits for them, and re-layouts  35.7 us

profile of v2, /device:TPU:0, one launch (start us, length us, event | category | flops | bytes accessed | tf_op | source)
XLA Modules:
  0.0 242.1 jit_solution(12012802736893246203)
XLA Ops:
  0.6 0.7 pad_bitcast_fusion.vec_ref
  1.3 0.0 copy-start.2
  1.3 0.9 copy-done.2
  2.3 0.0 copy-start.5
  2.3 0.9 copy-done.5
  3.1 36.6 %gather.1 = (bf16[3,2,2,4,2,48,512]{6,5,4,3,2,1,0:T(8,128)(2,1)S(1)}, f32[32,8,128]{2,1,0:T(8,128)S(1)}) custom-call(f32[2,48,512]{2,1,0:T(8,128)S(1)} %bitcast.25, f32[48,512]{1,0:T(8,128)S(1)} %copy-done.5, f32[8,128]{1,0:T(8,128)S(1)} %pad_bitcast_fusion.vec_ref), custom_call_target="tpu_custom_call" | custom-call | tf_op jit(solution)/shard_map/gather/pallas_call | solution.py:635
  39.7 0.0 copy-start
  39.7 2.2 copy-done
  42.0 0.7 reshape.65.vec_ref
  42.7 0.9 slice.22
  43.6 0.1 copy.48
  43.7 0.1 copy.47
  43.8 0.7 pad.16.clone.sp_ref
  44.5 0.7 pad.17.spt_ref
  45.1 0.8 reduce_sum.9.counts
  46.0 0.0 copy-start.17
  46.0 0.0 copy-start.14
  46.0 0.9 convert_divide_fusion
  47.0 0.6 broadcast_in_dim.4.pool_ref
  47.6 5.4 %copy.41.tokens_hbm = bf16[16,196,512]{2,1,0:T(8,128)(2,1)} copy(bf16[16,196,512]{2,0,1:T(8,128)(2,1)} %param.17) | data formatting | bytes 6422528 | tf_op args[0]
  53.0 0.0 copy-done.14
  53.0 0.0 copy-start.4
  53.0 3.5 %copy.42.cot_hbm = bf16[16,196,512]{2,1,0:T(8,128)(2,1)} copy(bf16[16,196,512]{2,0,1:T(8,128)(2,1)S(1)} %copy-done.14) | data formatting | bytes 6422528 | tf_op args[3]
  56.5 0.0 copy-done.17
  56.5 0.0 copy-done.4
  56.5 0.1 copy.40
  56.6 0.7 pad.18.sbias_ref
  57.3 0.0 copy-start.3
  57.3 0.0 copy-start.6
  57.3 0.0 copy-start.8
  57.3 0.0 copy-start.9
  57.3 0.0 copy-start.10
  57.3 0.0 copy-start.11
  57.3 0.0 copy-start.12
  57.3 0.0 copy-start.13
  57.3 109.8 %block.1 = (f32[16,196,512]{2,1,0:T(8,128)}, f32[16,196,512]{2,1,0:T(8,128)}, f32[16,1,512]{2,1,0:T(1,128)}, bf16[3,1536,512]{2,1,0:T(8,128)(2,1)}, f32[256,256]{1,0:T(8,128)}) custom-call(s32[16]{0:T(128)} %copy-done.17, s32[16]{0:T(128)} %keeps.1, bf16[16,196,512]{2,1,0:T(8,128)(2,1)} %copy.41.tokens_hbm, bf16[16,196,512]{2,1,0:T(8,128)(2,1)} %copy.42.cot_hbm, ...), custom_call_target="tpu_custom_call" | custom-call | tf_op jit(solution)/shard_map/block/pallas_call | solution.py:447
  167.1 0.0 copy-start.16
  167.1 0.0 copy-start.18
  167.1 0.0 copy-start.19
  167.1 0.0 copy-start.1
  167.1 2.3 copy-done.1
  169.5 0.0 copy-start.7
  169.5 0.9 copy-done.7
  170.4 49.0 %reduce.1 = (f32[3,48,512]{2,1,0:T(8,128)S(1)}, f32[32,8,256]{2,1,0:T(8,128)S(1)}, f32[8,128]{1,0:T(8,128)S(1)}) custom-call(bf16[3,2,2,4,2,48,512]{6,5,4,3,2,1,0:T(8,128)(2,1)S(1)} %bitcast.24, f32[32,8,256]{2,1,0:T(8,128)S(1)} %bitcast.29), custom_call_target="tpu_custom_call" | custom-call | tf_op jit(solution)/shard_map/reduce/pallas_call | solution.py:824
  219.5 0.0 copy-done.3
  219.5 0.0 copy-done.6
  219.5 0.0 copy-done.8
  219.5 0.0 copy-done.9
  219.5 0.0 copy-done.10
  219.5 0.0 copy-done.11
  219.6 0.0 copy-done.12
  219.6 0.0 copy-done.13
  219.6 1.3 adam.1
  220.9 0.5 slice.19
  222.1 0.0 copy-done.16
  222.1 0.0 copy-done.18
  222.1 0.0 copy-done.19
  222.1 0.7 multiply_subtract_fusion
  222.8 9.3 %copy.44 = f32[16,196,512]{2,0,1:T(8,128)} copy(f32[16,196,512]{2,1,0:T(8,128)} %get-tuple-element.70) | data formatting | bytes 12845056
  232.1 0.0 copy-start.15
  232.1 9.3 %copy.45 = f32[16,196,512]{2,0,1:T(8,128)} copy(f32[16,196,512]{2,1,0:T(8,128)} %get-tuple-element.71) | data formatting | bytes 12845056
  241.4 0.0 copy-done.15
  241.5 0.6 copy.53
  (6 shorter events, 0.0 us)
Async XLA Ops:
  1.3 0.9 copy-start.2
  2.3 0.9 copy-start.5
  39.7 2.2 copy-start
  46.0 10.5 %copy-start.17 = (s32[16]{0:T(128)}, s32[16]{0:T(128)S(1)}, u32[]{:S(2)}) copy-start(s32[16]{0:T(128)S(1)} %reduce_sum.9.counts) | copy-start | bytes 196
  46.0 7.0 %copy-start.14 = (bf16[16,196,512]{2,0,1:T(8,128)(2,1)S(1)}, bf16[16,196,512]{2,0,1:T(8,128)(2,1)}, u32[]{:S(2)}) copy-start(bf16[16,196,512]{2,0,1:T(8,128)(2,1)} %param.20) | copy-start | bytes 9633796
  53.0 3.5 %copy-start.4 = (f32[197,196]{1,0:T(8,128)S(1)}, f32[197,196]{1,0:T(8,128)}, u32[]{:S(2)}) copy-start(f32[197,196]{1,0:T(8,128)} %sw.1) | copy-start | bytes 463348
  57.3 162.2 %copy-start.3 = (f32[2,512,48]{1,2,0:T(8,128)S(1)}, f32[2,512,48]{1,2,0:T(8,128)}, u32[]{:S(2)}) copy-start(f32[2,512,48]{1,2,0:T(8,128)} %param.22) | copy-start | bytes 589828
  57.3 162.2 %copy-start.6 = (f32[48,512]{1,0:T(8,128)S(1)}, f32[48,512]{1,0:T(8,128)}, u32[]{:S(2)}) copy-start(f32[48,512]{1,0:T(8,128)} %ow.1) | copy-start | bytes 294916
  57.3 162.2 %copy-start.8 = (f32[197,196]{1,0:T(8,128)S(1)}, f32[197,196]{1,0:T(8,128)}, u32[]{:S(2)}) copy-start(f32[197,196]{1,0:T(8,128)} %s1_.1) | copy-start | bytes 463348
  57.3 162.2 %copy-start.9 = (f32[197,196]{1,0:T(8,128)S(1)}, f32[197,196]{1,0:T(8,128)}, u32[]{:S(2)}) copy-start(f32[197,196]{1,0:T(8,128)} %s2_.1) | copy-start | bytes 463348
  57.3 162.2 %copy-start.10 = (f32[2,512,48]{1,2,0:T(8,128)S(1)}, f32[2,512,48]{1,2,0:T(8,128)}, u32[]{:S(2)}) copy-start(f32[2,512,48]{1,2,0:T(8,128)} %param.26) | copy-start | bytes 589828
  57.3 162.2 %copy-start.11 = (f32[2,512,48]{1,2,0:T(8,128)S(1)}, f32[2,512,48]{1,2,0:T(8,128)}, u32[]{:S(2)}) copy-start(f32[2,512,48]{1,2,0:T(8,128)} %param.27) | copy-start | bytes 589828
  57.3 162.2 %copy-start.12 = (f32[48,512]{1,0:T(8,128)S(1)}, f32[48,512]{1,0:T(8,128)}, u32[]{:S(2)}) copy-start(f32[48,512]{1,0:T(8,128)} %o1.1) | copy-start | bytes 294916
  57.3 162.2 %copy-start.13 = (f32[48,512]{1,0:T(8,128)S(1)}, f32[48,512]{1,0:T(8,128)}, u32[]{:S(2)}) copy-start(f32[48,512]{1,0:T(8,128)} %o2.1) | copy-start | bytes 294916
  167.1 55.0 %copy-start.16 = (f32[240]{0:T(256)S(1)}, f32[240]{0:T(256)}, u32[]{:S(2)}) copy-start(f32[240]{0:T(256)} %param.24) | copy-start | bytes 2884
  167.1 55.0 %copy-start.18 = (f32[240]{0:T(256)S(1)}, f32[240]{0:T(256)}, u32[]{:S(2)}) copy-start(f32[240]{0:T(256)} %param.30) | copy-start | bytes 2884
  167.1 55.0 %copy-start.19 = (f32[240]{0:T(256)S(1)}, f32[240]{0:T(256)}, u32[]{:S(2)}) copy-start(f32[240]{0:T(256)} %param.31) | copy-start | bytes 2884
  167.1 2.4 copy-start.1
  169.5 0.9 copy-start.7
  232.1 9.3 %copy-start.15 = (f32[16,1,512]{2,1,0:T(1,128)S(1)}, f32[16,1,512]{2,1,0:T(1,128)}, u32[]{:S(2)}) copy-start(f32[16,1,512]{2,1,0:T(1,128)} %get-tuple-element.39) | copy-start | bytes 98308

commit v3 on v2

v3 whole, which is shorter than its diff:
```python
import functools

import jax
import jax.numpy as jnp
from jax import lax
from jax.experimental import pallas as pl
from jax.experimental.pallas import tpu as pltpu
from jax.sharding import PartitionSpec as P

NORM_EPS = 1e-05
DROP_RATE = 0.1
BF = jnp.bfloat16
F32 = jnp.float32
MESH = pl.DeviceIdType.MESH
GELU_K = 0.7978845608
GELU_C = 0.044715
NN = (((1,), (0,)), ((), ()))
NT = (((1,), (1,)), ((), ()))
TN = (((0,), (0,)), ((), ()))
LOT = 16
CUTS = 1


def dot(a, b, dims):
    return lax.dot_general(a, b, dims, preferred_element_type=F32)


def norm(x):
    c = x - jnp.mean(x, axis=-1, keepdims=True)
    inv = lax.rsqrt(jnp.mean(c * c, axis=-1, keepdims=True) + NORM_EPS)
    return c * inv, inv


def swap_matrix(images):
    side = LOT * images
    r = lax.broadcasted_iota(jnp.int32, (side, side), 0)
    s = lax.broadcasted_iota(jnp.int32, (side, side), 1)
    return jnp.where(s == (r % LOT) * images + r // LOT, 1.0, 0.0).astype(BF)


def unswap_matrix(images):
    side = LOT * images
    r = lax.broadcasted_iota(jnp.int32, (side, side), 0)
    s = lax.broadcasted_iota(jnp.int32, (side, side), 1)
    return jnp.where(s == (r % images) * LOT + r // images, 1.0, 0.0).astype(BF)


def place():
    d = lax.axis_index("dp")
    f = lax.axis_index("fsdp")
    return d % 2, d // 2, f // 2, f % 2


def device(x, y, z, c):
    return (y * 2 + x, z * 2 + c)


def greet_all():
    me = lax.axis_index("dp") * 8 + lax.axis_index("fsdp")
    barrier = pltpu.get_barrier_semaphore()

    def body(k, carry):
        peer = (me + k) % 32
        pl.semaphore_signal(
            barrier, inc=1, device_id=(peer // 8, peer % 8), device_id_type=MESH
        )
        return carry

    lax.fori_loop(1, 32, body, 0)
    pl.semaphore_wait(barrier, 31)


def gather_kernel(
    own_len,
    inner_ref, outer_ref, vec_ref, tokens_hbm, cot_hbm, mask_ref, keep_ref, pool_ref, spatial_ref,
    all_ref, vecs_ref, nm_ref, bg_ref, info_ref, poolc_ref, bsum_ref, sp_ref, spt_ref, sbias_ref,
    own, vown, vgot, wide, xblk, cblk, nrow, brow, send, recv, vsend, vrecv, lsem, isem,
):
    x, y, z, c = place()
    patches, images, width = tokens_hbm.shape
    own[0] = inner_ref[0].astype(BF)
    own[1] = inner_ref[1].astype(BF)
    own[2] = outer_ref[...].astype(BF)
    vown[...] = vec_ref[...].astype(BF).astype(F32)
    loads = [
        pltpu.make_async_copy(tokens_hbm, xblk, isem.at[0]),
        pltpu.make_async_copy(cot_hbm, cblk, isem.at[1]),
    ]
    for cp in loads:
        cp.start()
    greet_all()
    me = (y * 2 + x) * 8 + z * 2 + c
    local = pltpu.make_async_copy(own, all_ref.at[:, y, x, z, c], lsem)
    local.start()
    vgot[me] = vown[...]

    px, py = jnp.where(c == 0, 1 - x, x), jnp.where(c == 0, y, 1 - y)
    rx, ry = jnp.where(c == 0, x, 1 - x), jnp.where(c == 0, 1 - y, y)
    dx, dy = 1 - x, 1 - y
    index = [0]
    pnbr, rnbr, core = device(px, py, z, c), device(rx, ry, z, c), device(x, y, z, 1 - c)
    cut = outer_ref.shape[0] // CUTS
    started = []

    def remote(src, dst, dev):
        k = index[0]
        index[0] += 1
        cp = pltpu.make_async_remote_copy(
            src_ref=src, dst_ref=dst, send_sem=send.at[k], recv_sem=recv.at[k],
            device_id=dev, device_id_type=MESH,
        )
        cp.start()
        started.append(cp)
        return cp

    def span(s):
        return pl.ds(s * cut, cut)

    def block(q, s, by, bx):
        return all_ref.at[q, by, bx, z, c, span(s)]

    def z_sends(src, q, s, by, bx):
        return [remote(src, block(q, s, by, bx), device(x, y, (z + k) % 4, c)) for k in (1, 2, 3)]

    def send_line(q, s, ly, lx, dev):
        ref = all_ref.at[q, ly, lx, :, c, span(s)]
        return remote(ref, ref, dev)

    def vbody(k, carry):
        peer = (me + k) % 32
        pltpu.make_async_remote_copy(
            src_ref=vown, dst_ref=vgot.at[me], send_sem=vsend, recv_sem=vrecv,
            device_id=(peer // 8, peer % 8), device_id_type=MESH,
        ).start()
        return carry

    lax.fori_loop(1, 32, vbody, 0)
    cuts = [(q, s) for s in range(CUTS) for q in range(3)]
    zs = [None] * len(cuts)

    def start_z(k):
        if k < len(cuts):
            q, s = cuts[k]
            zs[k] = z_sends(own.at[q, span(s)], q, s, y, x)

    for k in range(WINDOW):
        start_z(k)
    local.wait()

    counts = jnp.sum(mask_ref[...], axis=1, keepdims=True)
    keeps = keep_ref[...]
    scale = keeps.astype(F32) * (1.0 / (1.0 - DROP_RATE))
    lane = lax.broadcasted_iota(jnp.int32, info_ref.shape, 1)
    info_ref[...] = jnp.where(lane == 0, counts, keeps)
    poolc = pool_ref[...].astype(F32) / counts.astype(F32)
    poolc_ref[...] = poolc
    side = spatial_ref.shape[1]
    wide[...] = jnp.zeros_like(wide)
    wide[0 : side + 1, 0:side] = spatial_ref[...]
    mat = wide[...]
    mat_t = mat.T
    span_a = lax.broadcasted_iota(jnp.int32, mat.shape, 0)
    span_b = lax.broadcasted_iota(jnp.int32, mat.shape, 1)
    sp_ref[...] = jnp.where(span_a < side, mat, 0.0).astype(BF)
    spt_ref[...] = jnp.where(span_b < side, mat_t, 0.0).astype(BF)
    sbias_ref[...] = mat_t[:, side : side + 1]
    bsum_ref[...] = jnp.zeros_like(bsum_ref)
    vecs_ref[...] = jnp.zeros_like(vecs_ref)

    def stack_vectors():
        view = vgot.at[pl.ds(0, 31)]
        pltpu.make_async_copy(view, view, vrecv).wait()
        per = width // 128
        for d in range(32):
            start = own_len * d
            shift = start % 128
            row = jnp.concatenate(
                [jnp.broadcast_to(vgot[d, i : i + 1, :], (8, 128)) for i in range(3)], axis=1
            )
            row = pltpu.roll(row, shift, 1) if shift else row
            for i in range(3):
                r = start // 128 + i
                if r * 128 < start + own_len:
                    at = (slice(r // per, r // per + 1), slice(r % per * 128, r % per * 128 + 128))
                    vecs_ref[at] += row[0:1, i * 128 : i * 128 + 128]

    swap = swap_matrix(images)

    def token_block(k, many):
        gain, shift = vecs_ref[0:1, :], vecs_ref[1:2, :]
        for p in range(many):
            patch = k * LOT + p
            xv = xblk[patch].astype(F32)
            unit, _ = norm(xv)
            nrow[p * images : (p + 1) * images, :] = (unit * gain + shift).astype(BF)
            live = jnp.where(counts > patch, 1.0, 0.0)
            og = cblk[patch].astype(F32) + live * poolc
            bg = (scale * og).astype(BF).astype(F32)
            bsum_ref[...] += bg
            brow[p * images : (p + 1) * images, :] = (live * bg).astype(BF)
        part = swap[:, 0 : many * images]
        for src, dst in ((nrow, nm_ref), (brow, bg_ref)):
            moved = dot(part, src[0 : many * images, :], NN).astype(BF)
            at = pl.ds(pl.multiple_of(k * LOT, LOT), LOT)
            dst[:, at, :] = moved.reshape(images, LOT, width)

    full = patches // LOT
    todo = list(range(full + (1 if patches % LOT else 0)))

    def some_tokens(many):
        for _ in range(many):
            if todo:
                k = todo.pop(0)
                token_block(k, LOT if k < full else patches % LOT)

    lines_p, lines_r, lines_r2, cores = {}, {}, {}, []

    def stage_two(k):
        q, s = cuts[k]
        for cp in zs[k]:
            cp.wait_recv()
        start_z(k + WINDOW)
        lines_p[k] = send_line(q, s, y, x, pnbr)
        lines_r[k] = send_line(q, s, y, x, rnbr)
        cores.append(send_line(q, s, y, x, core))

    def stage_three(k):
        q, s = cuts[k]
        lines_p[k].wait_recv()
        lines_r2[k] = send_line(q, s, py, px, rnbr)
        cores.append(send_line(q, s, py, px, core))

    def stage_four(k):
        q, s = cuts[k]
        lines_r[k].wait_recv()
        cores.append(send_line(q, s, ry, rx, core))

    def stage_five(k):
        q, s = cuts[k]
        lines_r2[k].wait_recv()
        cores.append(send_line(q, s, dy, dx, core))

    n = len(cuts)
    for t in range(n + 3):
        if t < n:
            stage_two(t)
        if 0 <= t - 1 < n:
            stage_three(t - 1)
            stage_four(t - 1)
        if 0 <= t - 2 < n:
            stage_five(t - 2)
        if t == 1:
            stack_vectors()
            for cp in loads:
                cp.wait()
        if t >= 1:
            some_tokens(2)
    some_tokens(len(todo))
    for cp in cores:
        cp.wait_recv()
    for cp in started:
        cp.wait_send()
    view = vgot.at[pl.ds(0, 31)]
    pltpu.make_async_copy(view, view, vsend).wait()


NSEND = 30 * CUTS
WINDOW = 3


def gather_all(own_len, inner, outer, vec, tokens, cot, mask, keep, pool, spatial):
    rows, width = outer.shape
    patches, images, _ = tokens.shape
    pad = -(-patches // LOT) * LOT
    vmem = pl.BlockSpec(memory_space=pltpu.VMEM)
    anyb = pl.BlockSpec(memory_space=pl.ANY)
    dma = pltpu.SemaphoreType.DMA
    shape = jax.ShapeDtypeStruct
    return pl.pallas_call(
        functools.partial(gather_kernel, own_len),
        out_shape=(
            shape((3, 2, 2, 4, 2, rows, width), BF),
            shape((16, width), F32),
            shape((images, pad, width), BF),
            shape((images, pad, width), BF),
            shape((images, 128), jnp.int32),
            shape((images, width), F32),
            shape((images, width), F32),
            shape((256, 256), BF),
            shape((256, 256), BF),
            shape((256, 1), F32),
        ),
        in_specs=[vmem] * 3 + [anyb] * 2 + [vmem] * 4,
        out_specs=[anyb] + [vmem] * 9,
        scratch_shapes=[
            pltpu.VMEM((3, rows, width), BF),
            pltpu.VMEM((8, 128), F32),
            pltpu.VMEM((32, 8, 128), F32),
            pltpu.VMEM((256, 256), F32),
            pltpu.VMEM((patches, images, width), BF),
            pltpu.VMEM((patches, images, width), BF),
            pltpu.VMEM((LOT * images, width), BF),
            pltpu.VMEM((LOT * images, width), BF),
            dma((NSEND,)), dma((NSEND,)), dma, dma, dma, dma((2,)),
        ],
        compiler_params=pltpu.CompilerParams(
            collective_id=0, has_side_effects=True, vmem_limit_bytes=60 * 2**20
        ),
        name="gather",
    )(inner, outer, vec, tokens, cot, mask, keep, pool, spatial)


def gelu_pair(v):
    u = v * v
    s = 0.5 * jnp.tanh(v * (GELU_K + (GELU_K * GELU_C) * u)) + 0.5
    h = v * s
    d = s + (h - h * s) * (2.0 * GELU_K + (6.0 * GELU_K * GELU_C) * u)
    return h, d


def fold8(x):
    total = x[0:8]
    for r in range(8, x.shape[0], 8):
        total = total + x[r : r + 8]
    return total


def lanes(x):
    total = x[:, 0:128]
    for c in range(128, x.shape[1], 128):
        total = total + x[:, c : c + 128]
    return total


def loop(lo, hi, fn):
    def body(i, c):
        fn(i)
        return c

    lax.fori_loop(lo, hi, body, 0)


def block_kernel(
    cfg,
    info_s,
    tokens_hbm, cot_hbm, nm_hbm, bg_hbm,
    info_ref, poolc_ref, bsum_ref, wt_ref, vec_ref, sp_ref, spt_ref, sbias_ref,
    out_hbm, ig_hbm, pooled_ref, grads_hbm, small_ref,
    acc, sg_ref, sbg_ref, off_s, gend_s, grows_s,
    wtt, nm_b, bg_b, h0_b, e0_b, mg_b, xm_b, u2_b, d1_b, stat_b, h1_s, t_s,
    xblk, cblk, br_s, ng_s, out_st, ig_st, vacc,
    pack_sem, in_sem, out_sem, grad_sem,
):
    images, patches, width, gate, rows_cap, tm, kw, classes = cfg
    cw = 256
    nj = gate // cw
    chunks = -(-patches // LOT)
    zero_row = nm_b.shape[0] - LOT
    g2_base, s2_base = 3 * width, 3 * width + gate
    b0_base, b1_base = 3 * width + 2 * gate, 3 * width + 3 * gate

    def vrow(base, j):
        start = base + j * cw
        return vec_ref[start // width : start // width + 1, start % width : start % width + cw]

    def count(b):
        return info_s[b, 0]

    def keep(b):
        return info_s[b, 1]

    def need_of(b):
        return keep(b) * ((count(b) + LOT - 1) // LOT)

    def plan(b, carry):
        group, row, first = carry
        need = need_of(b) * LOT
        over = row + need - first > rows_cap
        group = group + over.astype(jnp.int32)
        first = jnp.where(over, row, first)
        off_s[b] = row
        row = row + need
        gend_s[group] = b + 1
        grows_s[group] = row - first
        return group, row, first

    zero = jnp.int32(0)
    last_group, all_rows, _ = lax.fori_loop(0, images, plan, (zero, zero, zero))

    def pack(b, act):
        lots = need_of(b)
        o = off_s[b]
        done = jnp.int32(0)
        for size in (8, 4, 2, 1):
            @pl.when((lots & size) != 0)
            def _(size=size, done=done):
                src = pl.ds(pl.multiple_of(done * LOT, LOT), size * LOT)
                dst = pl.ds(pl.multiple_of(o + done * LOT, LOT), size * LOT)
                for i, (far, near) in enumerate(((nm_hbm, nm_b), (bg_hbm, bg_b))):
                    act(pltpu.make_async_copy(far.at[b, src], near.at[dst], pack_sem.at[i, b]))

            done = done + (lots & size)

    loop(0, images, lambda b: pack(b, lambda cp: cp.start()))

    full = patches // LOT
    rest = patches % LOT

    def load_lot(k, many, slot):
        at = pl.ds(k * LOT, many)
        return (
            pltpu.make_async_copy(tokens_hbm.at[at], xblk.at[slot, pl.ds(0, many)], in_sem.at[0, slot]),
            pltpu.make_async_copy(cot_hbm.at[at], cblk.at[slot, pl.ds(0, many)], in_sem.at[1, slot]),
        )

    for k in (0, 1):
        for cp in load_lot(k, LOT, k):
            cp.start()

    for q in range(3):
        for j in range(nj):
            wtt[q, :, j * cw : (j + 1) * cw] = wt_ref[q, j * cw : (j + 1) * cw, :].T

    def zero_rows(ref, n_chunks, start):
        z = jnp.zeros((LOT, ref.shape[1]), ref.dtype)

        def body(i):
            ref[pl.ds(pl.multiple_of(start + i * LOT, LOT), LOT), :] = z

        loop(0, n_chunks, body)

    for ref in (mg_b, xm_b, u2_b):
        zero_rows(ref, ref.shape[0] // LOT, 0)
    for ref in (nm_b, bg_b):
        zero_rows(ref, tm // LOT, all_rows)
    z = jnp.zeros((LOT, width), BF)
    nm_b[zero_row : zero_row + LOT, :] = z
    bg_b[zero_row : zero_row + LOT, :] = z
    vacc[...] = jnp.zeros_like(vacc)
    acc[...] = jnp.zeros_like(acc)
    sg_ref[...] = jnp.zeros_like(sg_ref)
    sbg_ref[...] = jnp.zeros_like(sbg_ref)
    loop(0, images, lambda b: pack(b, lambda cp: cp.wait()))

    def phase_a(t, gs):
        r0 = pl.multiple_of(t * tm, tm)
        rows = pl.ds(r0, tm)
        here = pl.ds(pl.multiple_of(gs + r0, LOT), tm)
        nb = nm_b[here, :]
        bgt = bg_b[here, :]
        s1 = jnp.zeros((tm, 128), F32)
        for j in range(nj):
            cols = slice(j * cw, (j + 1) * cw)
            a1 = dot(nb, wtt[1, :, cols], NN) + vrow(b1_base, j)
            h1, d1 = gelu_pair(a1)
            h1_s[:, cols] = h1
            d1_b[rows, cols] = d1.astype(BF)
            s1 = s1 + lanes(h1)
        mean = jnp.sum(s1, axis=1, keepdims=True) * (1.0 / gate)
        q1 = jnp.zeros((tm, 128), F32)
        rs1 = jnp.zeros((tm, 128), F32)
        for j in range(nj):
            cols = slice(j * cw, (j + 1) * cw)
            a0 = dot(nb, wtt[0, :, cols], NN) + vrow(b0_base, j)
            h0, d0 = gelu_pair(a0)
            gg = dot(bgt, wtt[2, :, cols], NN)
            mg = gg * h0
            h0_b[rows, cols] = h0.astype(BF)
            mg_b[rows, cols] = mg.astype(BF)
            e0_b[rows, cols] = (gg * d0).astype(BF)
            rs1 = rs1 + lanes(mg)
            c = h1_s[:, cols] - mean
            q1 = q1 + lanes(c * c)
        inv = lax.rsqrt(jnp.sum(q1, axis=1, keepdims=True) * (1.0 / gate) + NORM_EPS)
        stat_b[rows, 0:128] = jnp.broadcast_to(inv, (tm, 128))
        stat_b[rows, 128:256] = rs1
        for j in range(nj):
            cols = slice(j * cw, (j + 1) * cw)
            u2 = (h1_s[:, cols] - mean) * inv
            u2_b[rows, cols] = u2.astype(BF)
            xm_b[rows, cols] = (u2 * vrow(g2_base, j) + vrow(s2_base, j)).astype(BF)

    def phase_b(b, m, gs):
        n = count(b)
        o = pl.multiple_of(off_s[b] - gs, LOT)
        rows = pl.ds(o, m)
        rid = lax.broadcasted_iota(jnp.int32, (m, 1), 0)
        cid = lax.broadcasted_iota(jnp.int32, (m, m), 1)
        rid2 = lax.broadcasted_iota(jnp.int32, (m, m), 0)
        both = (cid < n) & (rid2 < n)
        sp = jnp.where(both, sp_ref[0:m, 0:m], 0.0).astype(BF)
        spt = jnp.where(both, spt_ref[0:m, 0:m], 0.0).astype(BF)
        sbias = sbias_ref[0:m, :]
        valid = rid < n
        fill = jnp.where(rid < need_of(b) * LOT, 0.0, 1.0)
        inv = stat_b[rows, 0:1]
        tsum = jnp.zeros((m, 128), F32)
        tdot = jnp.zeros((m, 128), F32)
        sg = jnp.zeros((m, m), F32)
        for j in range(nj):
            cols = slice(j * cw, (j + 1) * cw)
            xm = xm_b[rows, cols]
            mg = mg_b[rows, cols]
            so = dot(sp, xm, NN) + sbias
            so = jnp.where(valid, so, fill)
            mix = dot(spt, mg, NN)
            sg = sg + dot(mg, xm, NT)
            h0_b[rows, cols] = (h0_b[rows, cols].astype(F32) * so).astype(BF)
            e0_b[rows, cols] = (e0_b[rows, cols].astype(F32) * so).astype(BF)
            u2 = u2_b[rows, cols].astype(F32)
            mu = mix * u2
            gain = vrow(g2_base, j)
            t = mix * gain
            t_s[0:m, cols] = t
            tsum = tsum + lanes(t)
            tdot = tdot + lanes(mu * gain)
            vi, lo = j * cw // width, j * cw % width
            vacc[g2_base // width + vi, :, lo : lo + cw] += fold8(mu)
            vacc[s2_base // width + vi, :, lo : lo + cw] += fold8(mix)
        sg_ref[0:m, 0:m] += jnp.where(both, sg, 0.0)
        sbg_ref[0:m, :] += jnp.where(valid, stat_b[rows, 128:256], 0.0)
        m1 = jnp.sum(tsum, axis=1, keepdims=True) * (1.0 / gate)
        m2 = jnp.sum(tdot, axis=1, keepdims=True) * (1.0 / gate)
        for j in range(nj):
            cols = slice(j * cw, (j + 1) * cw)
            u2 = u2_b[rows, cols].astype(F32)
            sec = inv * (t_s[0:m, cols] - m1 - u2 * m2)
            sec = jnp.where(valid, sec, fill)
            d1_b[rows, cols] = (d1_b[rows, cols].astype(F32) * sec).astype(BF)

    def phase_w(k, gs):
        r0 = pl.multiple_of(k * kw, kw)
        rows = pl.ds(r0, kw)
        here = pl.ds(pl.multiple_of(gs + r0, LOT), kw)
        nb = nm_b[here, :]
        bgt = bg_b[here, :]
        for j in range(gate // 256):
            cols = slice(j * 256, (j + 1) * 256)
            acc[0, cols, :] += dot(e0_b[rows, cols], nb, TN)
            acc[1, cols, :] += dot(d1_b[rows, cols], nb, TN)
            acc[2, cols, :] += dot(h0_b[rows, cols], bgt, TN)

    def phase_c(t, gs, group_rows):
        r0 = pl.multiple_of(t * tm, tm)
        rows = pl.ds(r0, tm)
        here = pl.ds(pl.multiple_of(gs + r0, LOT), tm)
        mine = lax.broadcasted_iota(jnp.int32, (tm, 1), 0) < group_rows - r0
        br = dot(h0_b[rows, :], wt_ref[2], NN)
        bg_b[here, :] = jnp.where(mine, br, bg_b[here, :].astype(F32)).astype(BF)
        ng = dot(e0_b[rows, :], wt_ref[0], NN) + dot(d1_b[rows, :], wt_ref[1], NN)
        nm_b[here, :] = jnp.where(mine, ng, nm_b[here, :].astype(F32)).astype(BF)
        for base, ref in ((b0_base // width, e0_b), (b1_base // width, d1_b)):
            for v in range(gate // width):
                vacc[base + v] += fold8(ref[rows, v * width : (v + 1) * width].astype(F32))

    def group(g, carry):
        b_start, gs = carry
        b_end = gend_s[g]
        rows = grows_s[g]
        tiles = (rows + tm - 1) // tm
        loop(0, tiles, lambda t: phase_a(t, gs))

        def do_b(b):
            low = 0
            for m in classes:
                @pl.when((keep(b) == 1) & (count(b) > low) & (count(b) <= m))
                def _(m=m):
                    phase_b(b, m, gs)

                low = m

        loop(b_start, b_end, do_b)
        tail = (tiles * tm - rows) // LOT
        for ref in (h0_b, e0_b, d1_b):
            zero_rows(ref, tail, rows)
        loop(0, (rows + kw - 1) // kw, lambda k: phase_w(k, gs))
        loop(0, tiles, lambda t: phase_c(t, gs, rows))
        return b_end, gs + rows

    lax.fori_loop(0, last_group + 1, group, (zero, zero))

    half = gate // 2
    grad_out = []
    per = gate // width
    for i in range(6):
        q, lo = i // 2, (i % 2) * half
        buf = (h1_s, t_s)[0]
        del buf
        stage = (mg_b, xm_b)[i % 2]
        if i >= 2:
            for cp in grad_out[i - 2]:
                cp.wait()
        cps = []
        for v in range(per):
            third = half // per
            cut = slice(v * width, (v + 1) * width)
            stage[0:third, cut] = acc[q, lo + v * third : lo + (v + 1) * third, :].astype(BF)
            cps.append(
                pltpu.make_async_copy(
                    stage.at[pl.ds(0, third), pl.ds(v * width, width)],
                    grads_hbm.at[q, pl.ds(lo + v * third, third)],
                    grad_sem.at[i, v],
                )
            )
        for cp in cps:
            cp.start()
        grad_out.append(cps)

    counts = info_ref[:, 0:1]
    live_counts = counts * info_ref[:, 1:2]
    scale = info_ref[:, 1:2].astype(F32) * (1.0 / (1.0 - DROP_RATE))
    poolc = poolc_ref[...]
    gain_one, bias_out = vec_ref[0:1, :], vec_ref[2:3, :]
    back = unswap_matrix(images)

    def store_lot(k, many, slot):
        at = pl.ds(k * LOT, many)
        return (
            pltpu.make_async_copy(out_st.at[slot, pl.ds(0, many)], out_hbm.at[at], out_sem.at[0, slot]),
            pltpu.make_async_copy(ig_st.at[slot, pl.ds(0, many)], ig_hbm.at[at], out_sem.at[1, slot]),
        )

    pooled_ref[...] = jnp.zeros_like(pooled_ref)

    def lot(k, many, slot):
        for cp in load_lot(k, many, slot):
            cp.wait()
        parts = [[], []]
        for b in range(images):
            there = k < need_of(b)
            row = pl.multiple_of(jnp.where(there, off_s[b] + k * LOT, zero_row), LOT)
            parts[0].append(bg_b[pl.ds(row, LOT), :])
            parts[1].append(nm_b[pl.ds(row, LOT), :])
        mat = back[0 : many * images, :]
        br_s[0 : many * images, :] = dot(mat, jnp.concatenate(parts[0], axis=0), NN)
        ng_s[0 : many * images, :] = dot(mat, jnp.concatenate(parts[1], axis=0), NN)
        psum = jnp.zeros((images, width), F32)
        g1 = jnp.zeros((images, width), F32)
        s1 = jnp.zeros((images, width), F32)
        for p in range(many):
            patch = k * LOT + p
            x = xblk[slot, p].astype(F32)
            unit, inv = norm(x)
            live = jnp.where(counts > patch, 1.0, 0.0)
            og = cblk[slot, p].astype(F32) + live * poolc
            cut = slice(p * images, (p + 1) * images)
            out = x + scale * (br_s[cut, :] + bias_out)
            out_st[slot, p] = out
            psum = psum + live * out
            ng = ng_s[cut, :]
            t = ng * gain_one
            m1 = jnp.mean(t, axis=-1, keepdims=True)
            m2 = jnp.mean(t * unit, axis=-1, keepdims=True)
            ig_st[slot, p] = og + inv * (t - m1 - unit * m2)
            g1 = g1 + ng * unit
            s1 = s1 + ng
        pooled_ref[...] += psum
        vacc[0] += fold8(g1)
        vacc[1] += fold8(s1)
        for cp in store_lot(k, many, slot):
            cp.start()

    def lots(k):
        slot = lax.rem(k, 2)

        @pl.when(k >= 2)
        def _():
            for cp in store_lot(k - 2, LOT, slot):
                cp.wait()

        lot(k, LOT, slot)

        @pl.when(k + 2 < full)
        def _():
            for cp in load_lot(k + 2, LOT, slot):
                cp.start()

        if rest:
            @pl.when(k + 2 == full)
            def _():
                for cp in load_lot(full, rest, full % 2):
                    cp.start()

    loop(0, full, lots)
    if rest:
        for cp in store_lot(full - 2, LOT, full % 2):
            cp.wait()
        lot(full, rest, full % 2)
    pooled_ref[...] = pooled_ref[...] / counts.astype(F32)

    vacc[2] += fold8(bsum_ref[...])
    small_ref[...] = jnp.zeros_like(small_ref)
    sums = jnp.sum(vacc[...], axis=1)
    for v in range(sums.shape[0]):
        for h in range(width // 256):
            row = v * (width // 256) + h
            small_ref[row : row + 1, :] = sums[v : v + 1, h * 256 : (h + 1) * 256]
    pad = sg_ref.shape[0]
    small_ref[SPATIAL_ROW : SPATIAL_ROW + pad, 0:pad] = sg_ref[...]
    bias = jnp.sum(sbg_ref[...], axis=1, keepdims=True)
    eye = lax.broadcasted_iota(jnp.int32, (pad, pad), 0) == lax.broadcasted_iota(jnp.int32, (pad, pad), 1)
    bias_row = jnp.sum(jnp.where(eye, bias, 0.0), axis=0, keepdims=True)
    small_ref[SPATIAL_ROW + patches : SPATIAL_ROW + patches + 1, 0:pad] = bias_row
    for cps in grad_out[4:]:
        for cp in cps:
            cp.wait()
    if rest:
        for cp in store_lot(full - 1, LOT, (full - 1) % 2) + store_lot(full, rest, full % 2):
            cp.wait()
    else:
        for k in (full - 2, full - 1):
            for cp in store_lot(k, LOT, k % 2):
                cp.wait()


SPATIAL_ROW = 32


def run_block(
    tokens, cot, nm, bg, info, poolc, bsum, wt, vec, sp, spt, sbias,
    *, rows_cap=1024, tm=256, kw=256, classes=(112, 160, 208),
):
    patches, images, width = tokens.shape
    gate = wt.shape[1]
    pad = -(-patches // LOT) * LOT
    classes = tuple(m for m in classes if m < pad) + (pad,)
    cap = rows_cap + pad + 48
    cap = -(-cap // tm) * tm
    long = images * pad + tm + LOT
    cfg = (images, patches, width, gate, rows_cap, tm, kw, classes)
    smem = pl.BlockSpec(memory_space=pltpu.SMEM)
    vmem = pl.BlockSpec(memory_space=pltpu.VMEM)
    anyb = pl.BlockSpec(memory_space=pl.ANY)
    dma = pltpu.SemaphoreType.DMA
    shape = jax.ShapeDtypeStruct
    nvec = 3 + 4 * gate // width
    return pl.pallas_call(
        functools.partial(block_kernel, cfg),
        out_shape=(
            shape((patches, images, width), F32),
            shape((patches, images, width), F32),
            shape((images, width), F32),
            shape((3, gate, width), BF),
            shape((256, 256), F32),
        ),
        in_specs=[smem] + [anyb] * 4 + [vmem] * 8,
        out_specs=[anyb, anyb, vmem, anyb, vmem],
        scratch_shapes=[
            pltpu.VMEM((3, gate, width), F32),
            pltpu.VMEM((pad, pad), F32),
            pltpu.VMEM((pad, 128), F32),
            pltpu.SMEM((images,), jnp.int32),
            pltpu.SMEM((images,), jnp.int32),
            pltpu.SMEM((images,), jnp.int32),
            pltpu.VMEM((3, width, gate), BF),
            pltpu.VMEM((long, width), BF),
            pltpu.VMEM((long, width), BF),
        ]
        + [pltpu.VMEM((cap, gate), BF)] * 6
        + [
            pltpu.VMEM((cap, 256), F32),
            pltpu.VMEM((tm, gate), F32),
            pltpu.VMEM((pad, gate), F32),
            pltpu.VMEM((2, LOT, images, width), BF),
            pltpu.VMEM((2, LOT, images, width), BF),
            pltpu.VMEM((LOT * images, width), F32),
            pltpu.VMEM((LOT * images, width), F32),
            pltpu.VMEM((2, LOT, images, width), F32),
            pltpu.VMEM((2, LOT, images, width), F32),
            pltpu.VMEM((nvec, 8, width), F32),
            dma((2, images)),
            dma((2, 2)),
            dma((2, 2)),
            dma((6, gate // width)),
        ],
        compiler_params=pltpu.CompilerParams(vmem_limit_bytes=60 * 2**20),
        name="block",
    )(info, tokens, cot, nm, bg, info, poolc, bsum, wt, vec, sp, spt, sbias)


def reduce_kernel(
    g_hbm, small_ref, red_ref, tot_ref, norm_ref,
    acc, rc, rr, rp, rz, rz2, rb, stage, sbuf, sred, nbuf, nown,
    send, recv, lsem, s1s, s1r, s2s, s2r, ns, nr,
):
    x, y, z, c = place()
    me = (y * 2 + x) * 8 + z * 2 + c
    px, py = jnp.where(c == 0, 1 - x, x), jnp.where(c == 0, y, 1 - y)
    rx, ry = jnp.where(c == 0, x, 1 - x), jnp.where(c == 0, 1 - y, y)
    dx, dy = 1 - x, 1 - y
    pnbr, rnbr, core = device(px, py, z, c), device(rx, ry, z, c), device(x, y, z, 1 - c)
    lines = ((ry, rx), (dy, dx), (y, x), (py, px))
    loads = [pltpu.make_async_copy(g_hbm.at[q, :, :, :, c], acc.at[q], lsem.at[q]) for q in range(3)]
    for cp in loads:
        cp.start()
    greet_all()
    index = [0]
    started = []

    def remote(src, dst, dev):
        k = index[0]
        index[0] += 1
        cp = pltpu.make_async_remote_copy(
            src_ref=src, dst_ref=dst, send_sem=send.at[k], recv_sem=recv.at[k],
            device_id=dev, device_id_type=MESH,
        )
        cp.start()
        started.append(cp)
        return cp

    swaps = {}
    for i, (ly, lx) in enumerate(lines):
        for q in range(3):
            swaps[q, i] = None
    for i, (ly, lx) in enumerate(((dy, dx), (ry, rx), (py, px), (y, x))):
        for q in range(3):
            swaps[q, i] = remote(g_hbm.at[q, ly, lx, :, 1 - c], rc.at[q, ly, lx], core)

    def broadcast(src, dst_at, ssem, rsem):
        def body(k, carry):
            peer = (me + k) % 32
            pltpu.make_async_remote_copy(
                src_ref=src(peer), dst_ref=dst_at, send_sem=ssem, recv_sem=rsem,
                device_id=(peer // 8, peer % 8), device_id_type=MESH,
            ).start()
            return carry
        lax.fori_loop(1, 32, body, 0)

    def wait31(ref, sem):
        view = ref.at[pl.ds(0, 31)]
        pltpu.make_async_copy(view, view, sem).wait()

    broadcast(lambda p: small_ref.at[p], sbuf.at[me], s1s, s1r)
    for cp in loads:
        cp.wait()

    def add_line(q, ly, lx, ref):
        for b in range(4):
            acc[q, ly, lx, b] = (acc[q, ly, lx, b].astype(F32) + ref[b].astype(F32)).astype(BF)

    first = {}
    for q in range(3):
        swaps[q, 0].wait_recv()
        add_line(q, dy, dx, rc.at[q, dy, dx])
        first[q, 0] = remote(acc.at[q, dy, dx], rr.at[q, 0], rnbr)
    for i in (1, 2):
        for q in range(3):
            swaps[q, i].wait_recv()
    for q in range(3):
        add_line(q, ry, rx, rc.at[q, ry, rx])
        first[q, 1] = remote(acc.at[q, ry, rx], rr.at[q, 1], rnbr)
    for q in range(3):
        add_line(q, py, px, rc.at[q, py, px])
        swaps[q, 3].wait_recv()
        add_line(q, y, x, rc.at[q, y, x])
    second = {}
    for q in (2, 0, 1):
        first[q, 0].wait_recv()
        add_line(q, py, px, rr.at[q, 0])
        if q < 2:
            second[q] = remote(acc.at[q, py, px], rp.at[q], pnbr)
        else:
            second[q] = [
                remote(acc.at[q, py, px, (z + k) % 4], rz2.at[k - 1], device(x, y, (z + k) % 4, c)) for k in (1, 2, 3)
            ]
    own2 = None
    for q in (2, 0, 1):
        first[q, 1].wait_recv()
        add_line(q, y, x, rr.at[q, 1])
        if q == 2:
            own2 = [
                remote(acc.at[q, y, x, (z + k) % 4], rz.at[q, k - 1], device(x, y, (z + k) % 4, c)) for k in (1, 2, 3)
            ]
    third = {}
    for q in (0, 1):
        second[q].wait_recv()
        add_line(q, y, x, rp.at[q])
        third[q] = [
            remote(acc.at[q, y, x, (z + k) % 4], rz.at[q, k - 1], device(x, y, (z + k) % 4, c)) for k in (1, 2, 3)
        ]
    for cp in second[2]:
        cp.wait_recv()
    stage[...] = (
        acc[2, py, px, z].astype(F32) + rz2[0].astype(F32) + rz2[1].astype(F32) + rz2[2].astype(F32)
    ).astype(BF)
    last = remote(stage, rb, pnbr)
    sbuf[me] = small_ref[me]
    wait31(sbuf, s1r)
    total = sbuf[0]
    for k in range(1, 32):
        total = total + sbuf[k]
    sred[...] = total
    tot_ref[me] = total
    broadcast(lambda p: sred, tot_ref.at[me], s2s, s2r)
    sq = jnp.zeros((8, 128), F32)

    def fold(v):
        t = jnp.zeros((8, 128), F32)
        for r in range(0, v.shape[0], 8):
            for l in range(0, v.shape[1], 128):
                p = v[r : r + 8, l : l + 128]
                t = t + p * p
        return t

    sq = sq + fold(total)
    for cp in own2:
        cp.wait_recv()
    for q in (0, 1):
        for cp in third[q]:
            cp.wait_recv()
        v = (
            acc[q, y, x, z].astype(F32) + rz[q, 0].astype(F32) + rz[q, 1].astype(F32) + rz[q, 2].astype(F32)
        )
        red_ref[q] = v
        sq = sq + fold(v)
    last.wait_recv()
    v = (
        acc[2, y, x, z].astype(F32) + rz[2, 0].astype(F32) + rz[2, 1].astype(F32) + rz[2, 2].astype(F32)
    ) + rb[...].astype(F32)
    red_ref[2] = v
    sq = sq + fold(v)
    nown[...] = sq
    nbuf[me] = sq
    broadcast(lambda p: nown, nbuf.at[me], ns, nr)
    wait31(nbuf, nr)
    wait31(tot_ref, s2r)
    t = nbuf[0]
    for k in range(1, 32):
        t = t + nbuf[k]
    t = jnp.sum(jnp.sum(t, axis=0, keepdims=True), axis=1, keepdims=True)
    norm_ref[...] = jnp.broadcast_to(jnp.sqrt(t), (8, 128))
    for cp in started:
        cp.wait_send()
    wait31(sbuf, s1s)
    wait31(tot_ref, s2s)
    wait31(nbuf, ns)


NRED = 12 + 6 + 2 + 3 + 3 + 6 + 1


def reduce_all(g, small):
    rows, width = g.shape[-2:]
    vmem = pl.BlockSpec(memory_space=pltpu.VMEM)
    anyb = pl.BlockSpec(memory_space=pl.ANY)
    dma = pltpu.SemaphoreType.DMA
    blk = (rows, width)
    return pl.pallas_call(
        reduce_kernel,
        out_shape=(
            jax.ShapeDtypeStruct((3,) + blk, F32),
            jax.ShapeDtypeStruct(small.shape, F32),
            jax.ShapeDtypeStruct((8, 128), F32),
        ),
        in_specs=[anyb, vmem],
        out_specs=[vmem] * 3,
        scratch_shapes=[
            pltpu.VMEM((3, 2, 2, 4) + blk, BF),
            pltpu.VMEM((3, 2, 2, 4) + blk, BF),
            pltpu.VMEM((3, 2, 4) + blk, BF),
            pltpu.VMEM((2, 4) + blk, BF),
            pltpu.VMEM((3, 3) + blk, BF),
            pltpu.VMEM((3,) + blk, BF),
            pltpu.VMEM(blk, BF),
            pltpu.VMEM(blk, BF),
            pltpu.VMEM(small.shape, F32),
            pltpu.VMEM(small.shape[1:], F32),
            pltpu.VMEM((32, 8, 128), F32),
            pltpu.VMEM((8, 128), F32),
            dma((NRED,)), dma((NRED,)), dma((3,)),
            dma, dma, dma, dma, dma, dma,
        ],
        compiler_params=pltpu.CompilerParams(collective_id=1, has_side_effects=True, vmem_limit_bytes=60 * 2**20),
        name="reduce",
    )(g, small)


STEP = 10
BETA_FIRST = 0.9
BETA_SECOND = 0.95
ADAM_EPS = 1e-08
DECAY_RATE = 0.05
RATE_MATRIX = 0.05
RATE_VECTOR = 0.8
CLIP_BOUND = 1.0
BOTH = ("dp", "fsdp")


def adam_step(weight, first, second, gradient, step_rate, weight_decay):
    first_new = BETA_FIRST * first + (1.0 - BETA_FIRST) * gradient
    second_new = BETA_SECOND * second + (1.0 - BETA_SECOND) * gradient * gradient
    first_hat = first_new * (1.0 / (1.0 - BETA_FIRST**STEP))
    second_hat = second_new * (1.0 / (1.0 - BETA_SECOND**STEP))
    weight_new = weight - step_rate * (
        first_hat / (jnp.sqrt(second_hat) + ADAM_EPS) + weight_decay * weight
    )
    return (weight_new, first_new, second_new)


def adam_kernel(red, tot, norm, iw, i1, i2, ow, o1, o2, sw, s1, s2, *outs):
    clip = CLIP_BOUND / jnp.maximum(norm[0:1, 0:1], CLIP_BOUND)
    rows = ow.shape[0]
    for q in range(2):
        for r in range(0, rows, 8):
            cut = slice(r, r + 8)
            new = adam_step(
                iw[q, cut], i1[q, cut], i2[q, cut], red[q, cut] * clip, RATE_MATRIX, DECAY_RATE
            )
            for ref, val in zip(outs[0:3], new):
                ref[q, cut] = val
    for r in range(0, rows, 8):
        cut = slice(r, r + 8)
        new = adam_step(ow[cut], o1[cut], o2[cut], red[2, cut] * clip, RATE_MATRIX, DECAY_RATE)
        for ref, val in zip(outs[3:6], new):
            ref[cut] = val
    side, cols = sw.shape
    grad = tot[SPATIAL_ROW : SPATIAL_ROW + side, 0:cols] * clip
    last = lax.broadcasted_iota(jnp.int32, (side, 1), 0) == side - 1
    rate = jnp.where(last, RATE_VECTOR, RATE_MATRIX)
    decay = jnp.where(last, 0.0, DECAY_RATE)
    new = adam_step(sw[...], s1[...], s2[...], grad, rate, decay)
    for ref, val in zip(outs[6:9], new):
        ref[...] = val


def adam_all(red, tot, norm, inner, outer, spatial):
    vmem = pl.BlockSpec(memory_space=pltpu.VMEM)
    shape = lambda a: jax.ShapeDtypeStruct(a.shape, F32)
    return pl.pallas_call(
        adam_kernel,
        out_shape=tuple(shape(a) for a in inner + outer + spatial),
        in_specs=[vmem] * 12,
        out_specs=[vmem] * 9,
        compiler_params=pltpu.CompilerParams(vmem_limit_bytes=32 * 2**20),
        name="adam",
    )(red, tot, norm, *inner, *outer, *spatial)


def slow_prepare(inner_t, outer_weight, vectors, tokens, cot, mask, keep, pool_cot, spatial):
    patches, images, width = tokens.shape
    pad = -(-patches // LOT) * LOT
    wt = jnp.concatenate(
        [
            lax.all_gather(inner_t.astype(BF), BOTH, axis=1, tiled=True),
            lax.all_gather(outer_weight.astype(BF), BOTH, axis=0, tiled=True)[None],
        ],
        axis=0,
    )
    vec = lax.all_gather(vectors.astype(BF), BOTH, axis=0, tiled=True).astype(F32)
    vec = vec.reshape(-1, width)
    counts = jnp.sum(mask, axis=1)
    info = jnp.zeros((images, 128), jnp.int32).at[:, 0].set(counts).at[:, 1].set(keep)
    poolc = pool_cot.astype(F32) / counts.astype(F32)[:, None]
    unit, _ = norm(tokens.astype(F32))
    edge = ((0, 0), (0, pad - patches), (0, 0))
    nm = (unit * vec[0] + vec[1]).astype(BF)
    live = mask.astype(F32).T[:, :, None]
    scale = keep.astype(F32) * (1.0 / (1.0 - DROP_RATE))
    bg = (scale[:, None] * (cot.astype(F32) + live * poolc)).astype(BF)
    bsum = jnp.sum(bg, axis=0, dtype=F32)
    nm = jnp.pad(nm.transpose(1, 0, 2), edge)
    bg = jnp.pad((bg * live.astype(BF)).transpose(1, 0, 2), edge)
    low = spatial[:patches].astype(BF)
    square = ((0, 256 - patches), (0, 256 - patches))
    sbias = jnp.pad(spatial[patches][:, None], ((0, 256 - patches), (0, 0)))
    return wt, vec, nm, bg, info, poolc, bsum, jnp.pad(low, square), jnp.pad(low.T, square), sbias


def slow_reduce(grads, small):
    red = lax.psum_scatter(grads.astype(F32), BOTH, scatter_dimension=1, tiled=True)
    tot = lax.psum(small, BOTH)
    squares = lax.psum(jnp.sum(red * red), BOTH) + jnp.sum(tot * tot)
    return red, tot, jnp.broadcast_to(jnp.sqrt(squares), (8, 128))


def per_device(
    fast,
    tokens,
    valid_mask,
    keep_mask,
    out_cotangent,
    pool_cotangent,
    inner_weight,
    outer_weight,
    vectors,
    spatial,
    inner_first,
    inner_second,
    outer_first,
    outer_second,
    vector_first,
    vector_second,
    spatial_first,
    spatial_second,
):
    own = vectors.shape[0]
    rows, width = outer_weight.shape
    inner_t = tuple(a.transpose(0, 2, 1) for a in (inner_weight, inner_first, inner_second))
    tokens = tokens.transpose(1, 0, 2)
    cot = out_cotangent.transpose(1, 0, 2)
    if fast:
        wt, *ready = gather_all(
            own,
            inner_t[0],
            outer_weight,
            jnp.pad(vectors, (0, 1024 - own)).reshape(8, 128),
            tokens,
            cot,
            valid_mask,
            keep_mask[:, None],
            pool_cotangent,
            spatial,
        )
        wt = wt.reshape(3, 32 * rows, width)
    else:
        wt, *ready = slow_prepare(
            inner_t[0], outer_weight, vectors, tokens, cot, valid_mask, keep_mask, pool_cotangent, spatial
        )
    vec, nm, bg, info, poolc, bsum, sp, spt, sbias = ready
    output, input_grad, pooled, grads, small = run_block(
        tokens, cot, nm, bg, info, poolc, bsum, wt, vec, sp, spt, sbias
    )
    output = output.transpose(1, 0, 2)
    input_grad = input_grad.transpose(1, 0, 2)
    if fast:
        red, tot, norm = reduce_all(
            grads.reshape(3, 2, 2, 4, 2, rows, width), small.reshape(32, 8, 256)
        )
        tot = tot.reshape(256, 256)
    else:
        red, tot, norm = slow_reduce(grads, small)
    new = adam_all(
        red,
        tot,
        norm,
        inner_t,
        (outer_weight, outer_first, outer_second),
        (spatial, spatial_first, spatial_second),
    )
    grad_norm = norm[0, 0]
    clip_factor = CLIP_BOUND / jnp.maximum(grad_norm, CLIP_BOUND)
    me = lax.axis_index("dp") * lax.axis_size("fsdp") + lax.axis_index("fsdp")
    total_vec = own * lax.axis_size("dp") * lax.axis_size("fsdp")
    flat = tot[: total_vec // 256].reshape(-1)
    vector_red = lax.dynamic_slice(flat, (me * own,), (own,))
    vector_out = adam_step(
        vectors, vector_first, vector_second, vector_red * clip_factor, RATE_VECTOR, 0.0
    )
    return (
        (output, input_grad, pooled, grad_norm)
        + tuple(a.transpose(0, 2, 1) for a in new[0:3])
        + tuple(new[3:6])
        + vector_out
        + tuple(new[6:9])
    )


def solution(mesh):
    fast = mesh.shape["dp"] == 4 and mesh.shape["fsdp"] == 8
    rows3 = P(BOTH, None, None)
    rows2 = P(BOTH, None)
    rows1 = P(BOTH)
    cols3 = P(None, None, BOTH)
    in_specs = (
        (rows3, rows2, rows1, rows3, rows2, cols3, rows2, rows1, P())
        + (cols3,) * 2
        + (rows2,) * 2
        + (rows1,) * 2
        + (P(),) * 2
    )
    out_specs = (
        (rows3, rows3, rows2, P()) + (cols3,) * 3 + (rows2,) * 3 + (rows1,) * 3 + (P(),) * 3
    )
    return jax.shard_map(
        functools.partial(per_device, fast),
        mesh=mesh,
        in_specs=in_specs,
        out_specs=out_specs,
        check_vma=False,
    )
```

time: 242 us -> 211 us (0.87); the launches traced: 242 us -> 214 us
  local copies, waits for them, and re-layouts: 41.3 us -> 7.23 us
  Pallas kernels: 197 us -> 205 us
    unnamed x48 -> x30, local copies, waits for them, and re-layouts: 35.7 us -> 2.66 us
    pallas_call x1, Pallas kernels: 49 us -> 73.7 us  [reduce_all(): pl.pallas_call(reduce_kernel, out_shape=(jax.ShapeDtypeStruct((3,) + blk,...]
    pallas_call x2, Pallas kernels: 146 us -> 130 us  [the longest x1 84.5 us: run_block(): pl.pallas_call(functools.partial(block_kernel, cfg), out_shape=(shape((pa...]
where the time goes in v3:
time: 211 us; the launch traced here: 214 us
  Pallas kernels  205 us (97%)
  local copies, waits for them, and re-layouts  7.23 us (3%)
    pallas_call x1, Pallas kernels, run_block(): pl.pallas_call(functools.partial(block_kernel, cfg), out_shape=(shape((pa...  84.5 us
    pallas_call x1, Pallas kernels, reduce_all(): pl.pallas_call(reduce_kernel, out_shape=(jax.ShapeDtypeStruct((3,) + blk,...  73.7 us
    pallas_call x1, Pallas kernels, gather_all(): pl.pallas_call(functools.partial(gather_kernel, own_len), out_shape=(shap...  45.2 us

profile of v3, /device:TPU:0, one launch (start us, length us, event | category | flops | bytes accessed | tf_op | source)
XLA Modules:
  0.0 214.1 jit_solution(5911354731857667448)
XLA Ops:
  0.6 1.3 copy.33.keep_ref
  2.0 1.3 pad_bitcast_fusion.vec_ref
  3.2 45.2 %gather.1 = (bf16[3,2,2,4,2,48,512]{6,5,4,3,2,1,0:T(8,128)(2,1)}, f32[16,512]{1,0:T(8,128)}, bf16[16,208,512]{2,1,0:T(8,128)(2,1)}, bf16[16,208,512]{2,1,0:T(8,1...) custom-call(f32[2,48,512]{2,1,0:T(8,128)} %bitcast.18, ...), custom_call_target="tpu_custom_call" | custom-call | tf_op jit(solution)/shard_map/gather/pallas_call | solution.py:279
  48.5 84.5 %block.1 = (f32[196,16,512]{2,1,0:T(8,128)}, f32[196,16,512]{2,1,0:T(8,128)}, f32[16,512]{1,0:T(8,128)}, bf16[3,1536,512]{2,1,0:T(8,128)(2,1)}, f32[256,256]{1,0:T(8,128)}) custom-call(s32[16,128]{1,0:T(8,128)} %get-tuple-element.43.info_s.info_ref, bf16[196,16,512]{2,1,0:T(8,128)(2,1)} %bitcast.25, bf16[196,16,512]{2,1,0:T(8,128)(2,1)} %bitcast.27, ...), custom_call_target="tpu_custom_call" | custom-call | tf_op jit(solution)/shard_map/block/pallas_call | solution.py:737
  133.0 0.0 copy-start.12
  133.0 0.0 copy-start.13
  133.0 0.0 copy-start.14
  133.0 0.0 copy-start
  133.1 0.0 copy-start.1
  133.1 0.0 copy-start.2
  133.1 0.0 copy-start.5
  133.1 0.0 copy-start.6
  133.1 0.0 copy-start.7
  133.1 0.0 copy-start.8
  133.1 0.0 copy-start.9
  133.1 0.0 copy-start.10
  133.1 73.7 %reduce.1 = (f32[3,48,512]{2,1,0:T(8,128)}, f32[32,8,256]{2,1,0:T(8,128)}, f32[8,128]{1,0:T(8,128)}) custom-call(bf16[3,2,2,4,2,48,512]{6,5,4,3,2,1,0:T(8,128)(2,1)} %bitcast.28, f32[32,8,256]{2,1,0:T(8,128)} %bitcast.30), custom_call_target="tpu_custom_call" | custom-call | tf_op jit(solution)/shard_map/reduce/pallas_call | solution.py:948
  206.8 0.8 slice.8
  207.6 1.2 slice.6
  209.5 0.0 copy-done.12
  209.5 0.0 copy-done.13
  209.5 0.0 copy-done.14
  209.5 0.7 multiply_subtract_fusion
  210.2 0.0 copy-done
  210.2 0.0 copy-done.1
  210.2 0.0 copy-done.2
  210.2 0.0 copy-done.5
  210.2 0.0 copy-done.6
  210.2 0.0 copy-done.7
  210.2 0.0 copy-done.8
  210.2 0.0 copy-done.9
  210.3 0.0 copy-done.10
  210.3 0.0 copy-start.3
  210.3 0.9 copy-done.3
  211.2 0.0 copy-start.4
  211.2 1.0 copy-done.4
  212.2 0.0 copy-start.11
  212.2 0.7 copy-done.11
  212.9 1.3 adam.1
  (1 shorter events, 0.0 us)
Async XLA Ops:
  133.0 76.5 %copy-start.12 = (f32[240]{0:T(256)S(1)}, f32[240]{0:T(256)}, u32[]{:S(2)}) copy-start(f32[240]{0:T(256)} %param.24) | copy-start | bytes 2884
  133.0 76.5 %copy-start.13 = (f32[240]{0:T(256)S(1)}, f32[240]{0:T(256)}, u32[]{:S(2)}) copy-start(f32[240]{0:T(256)} %param.30) | copy-start | bytes 2884
  133.0 76.5 %copy-start.14 = (f32[240]{0:T(256)S(1)}, f32[240]{0:T(256)}, u32[]{:S(2)}) copy-start(f32[240]{0:T(256)} %param.31) | copy-start | bytes 2884
  133.0 77.2 %copy-start = (f32[197,196]{1,0:T(8,128)S(1)}, f32[197,196]{1,0:T(8,128)}, u32[]{:S(2)}) copy-start(f32[197,196]{1,0:T(8,128)} %sw.1) | copy-start | bytes 463348
  133.1 77.1 %copy-start.1 = (f32[2,512,48]{1,2,0:T(8,128)S(1)}, f32[2,512,48]{1,2,0:T(8,128)}, u32[]{:S(2)}) copy-start(f32[2,512,48]{1,2,0:T(8,128)} %param.22) | copy-start | bytes 589828
  133.1 77.1 %copy-start.2 = (f32[48,512]{1,0:T(8,128)S(1)}, f32[48,512]{1,0:T(8,128)}, u32[]{:S(2)}) copy-start(f32[48,512]{1,0:T(8,128)} %ow.1) | copy-start | bytes 294916
  133.1 77.1 %copy-start.5 = (f32[197,196]{1,0:T(8,128)S(1)}, f32[197,196]{1,0:T(8,128)}, u32[]{:S(2)}) copy-start(f32[197,196]{1,0:T(8,128)} %s1_.1) | copy-start | bytes 463348
  133.1 77.1 %copy-start.6 = (f32[197,196]{1,0:T(8,128)S(1)}, f32[197,196]{1,0:T(8,128)}, u32[]{:S(2)}) copy-start(f32[197,196]{1,0:T(8,128)} %s2_.1) | copy-start | bytes 463348
  133.1 77.1 %copy-start.7 = (f32[2,512,48]{1,2,0:T(8,128)S(1)}, f32[2,512,48]{1,2,0:T(8,128)}, u32[]{:S(2)}) copy-start(f32[2,512,48]{1,2,0:T(8,128)} %param.26) | copy-start | bytes 589828
  133.1 77.1 %copy-start.8 = (f32[2,512,48]{1,2,0:T(8,128)S(1)}, f32[2,512,48]{1,2,0:T(8,128)}, u32[]{:S(2)}) copy-start(f32[2,512,48]{1,2,0:T(8,128)} %param.27) | copy-start | bytes 589828
  133.1 77.1 %copy-start.9 = (f32[48,512]{1,0:T(8,128)S(1)}, f32[48,512]{1,0:T(8,128)}, u32[]{:S(2)}) copy-start(f32[48,512]{1,0:T(8,128)} %o1.1) | copy-start | bytes 294916
  133.1 77.1 %copy-start.10 = (f32[48,512]{1,0:T(8,128)S(1)}, f32[48,512]{1,0:T(8,128)}, u32[]{:S(2)}) copy-start(f32[48,512]{1,0:T(8,128)} %o2.1) | copy-start | bytes 294916
  210.3 1.0 copy-start.3
  211.2 1.0 copy-start.4
  212.2 0.7 copy-start.11

commit v4 on v3

--- a/solution.py
+++ b/solution.py
@@ -18,7 +18,7 @@
 NT = (((1,), (1,)), ((), ()))
 TN = (((0,), (0,)), ((), ()))
 LOT = 16
-CUTS = 1
+CUTS = 3
 
 
 def dot(a, b, dims):
@@ -55,26 +55,21 @@
     return (y * 2 + x, z * 2 + c)
 
 
-def greet_all():
-    me = lax.axis_index("dp") * 8 + lax.axis_index("fsdp")
+def greet_partners():
+    x, y, z, c = place()
     barrier = pltpu.get_barrier_semaphore()
-
-    def body(k, carry):
-        peer = (me + k) % 32
-        pl.semaphore_signal(
-            barrier, inc=1, device_id=(peer // 8, peer % 8), device_id_type=MESH
-        )
-        return carry
-
-    lax.fori_loop(1, 32, body, 0)
-    pl.semaphore_wait(barrier, 31)
+    peers = [device(1 - x, y, z, c), device(x, 1 - y, z, c), device(x, y, z, 1 - c)]
+    peers += [device(x, y, (z + k) % 4, c) for k in (1, 2, 3)]
+    for peer in peers:
+        pl.semaphore_signal(barrier, inc=1, device_id=peer, device_id_type=MESH)
+    pl.semaphore_wait(barrier, len(peers))
 
 
 def gather_kernel(
     own_len,
     inner_ref, outer_ref, vec_ref, tokens_hbm, cot_hbm, mask_ref, keep_ref, pool_ref, spatial_ref,
     all_ref, vecs_ref, nm_ref, bg_ref, info_ref, poolc_ref, bsum_ref, sp_ref, spt_ref, sbias_ref,
-    own, vown, vgot, wide, xblk, cblk, nrow, brow, send, recv, vsend, vrecv, lsem, isem,
+    own, vown, vgot, wide, xblk, cblk, nrow, brow, nm_v, bg_v, send, recv, lsem, isem, osem,
 ):
     x, y, z, c = place()
     patches, images, width = tokens_hbm.shape
@@ -88,11 +83,10 @@
     ]
     for cp in loads:
         cp.start()
-    greet_all()
-    me = (y * 2 + x) * 8 + z * 2 + c
+    greet_partners()
     local = pltpu.make_async_copy(own, all_ref.at[:, y, x, z, c], lsem)
     local.start()
-    vgot[me] = vown[...]
+    vgot[y, x, z, c] = vown[...]
 
     px, py = jnp.where(c == 0, 1 - x, x), jnp.where(c == 0, y, 1 - y)
     rx, ry = jnp.where(c == 0, x, 1 - x), jnp.where(c == 0, 1 - y, y)
@@ -117,38 +111,35 @@
         return pl.ds(s * cut, cut)
 
     def block(q, s, by, bx):
+        if q == 3:
+            return vgot.at[by, bx, z, c]
         return all_ref.at[q, by, bx, z, c, span(s)]
 
     def z_sends(src, q, s, by, bx):
         return [remote(src, block(q, s, by, bx), device(x, y, (z + k) % 4, c)) for k in (1, 2, 3)]
 
     def send_line(q, s, ly, lx, dev):
-        ref = all_ref.at[q, ly, lx, :, c, span(s)]
+        ref = vgot.at[ly, lx, :, c] if q == 3 else all_ref.at[q, ly, lx, :, c, span(s)]
         return remote(ref, ref, dev)
 
-    def vbody(k, carry):
-        peer = (me + k) % 32
-        pltpu.make_async_remote_copy(
-            src_ref=vown, dst_ref=vgot.at[me], send_sem=vsend, recv_sem=vrecv,
-            device_id=(peer // 8, peer % 8), device_id_type=MESH,
-        ).start()
-        return carry
-
-    lax.fori_loop(1, 32, vbody, 0)
-    cuts = [(q, s) for s in range(CUTS) for q in range(3)]
+    cuts = [(3, 0)] + [(q, s) for s in range(CUTS) for q in range(3)]
     zs = [None] * len(cuts)
 
     def start_z(k):
         if k < len(cuts):
             q, s = cuts[k]
-            zs[k] = z_sends(own.at[q, span(s)], q, s, y, x)
+            src = vown if q == 3 else own.at[q, span(s)]
+            zs[k] = z_sends(src, q, s, y, x)
 
     for k in range(WINDOW):
         start_z(k)
     local.wait()
 
     counts = jnp.sum(mask_ref[...], axis=1, keepdims=True)
-    keeps = keep_ref[...]
+    keeps = jnp.zeros((images, 1), jnp.int32)
+    image = lax.broadcasted_iota(jnp.int32, (images, 1), 0)
+    for b in range(images):
+        keeps = jnp.where(image == b, keep_ref[b], keeps)
     scale = keeps.astype(F32) * (1.0 / (1.0 - DROP_RATE))
     lane = lax.broadcasted_iota(jnp.int32, info_ref.shape, 1)
     info_ref[...] = jnp.where(lane == 0, counts, keeps)
@@ -168,14 +159,13 @@
     vecs_ref[...] = jnp.zeros_like(vecs_ref)
 
     def stack_vectors():
-        view = vgot.at[pl.ds(0, 31)]
-        pltpu.make_async_copy(view, view, vrecv).wait()
         per = width // 128
         for d in range(32):
             start = own_len * d
             shift = start % 128
+            blk = vgot[d // 16, d // 8 % 2, d // 2 % 4, d % 2]
             row = jnp.concatenate(
-                [jnp.broadcast_to(vgot[d, i : i + 1, :], (8, 128)) for i in range(3)], axis=1
+                [jnp.broadcast_to(blk[i : i + 1, :], (8, 128)) for i in range(3)], axis=1
             )
             row = pltpu.roll(row, shift, 1) if shift else row
             for i in range(3):
@@ -199,7 +189,7 @@
             bsum_ref[...] += bg
             brow[p * images : (p + 1) * images, :] = (live * bg).astype(BF)
         part = swap[:, 0 : many * images]
-        for src, dst in ((nrow, nm_ref), (brow, bg_ref)):
+        for src, dst in ((nrow, nm_v), (brow, bg_v)):
             moved = dot(part, src[0 : many * images, :], NN).astype(BF)
             at = pl.ds(pl.multiple_of(k * LOT, LOT), LOT)
             dst[:, at, :] = moved.reshape(images, LOT, width)
@@ -207,13 +197,29 @@
     full = patches // LOT
     todo = list(range(full + (1 if patches % LOT else 0)))
 
+    stores = []
+    pad = nm_v.shape[1]
+    marks = [pad // (2 * LOT) * LOT, pad]
+
     def some_tokens(many):
         for _ in range(many):
-            if todo:
-                k = todo.pop(0)
-                token_block(k, LOT if k < full else patches % LOT)
-
-    lines_p, lines_r, lines_r2, cores = {}, {}, {}, []
+            if not todo:
+                return
+            k = todo.pop(0)
+            token_block(k, LOT if k < full else patches % LOT)
+            end = (k + 1) * LOT
+            if end in marks:
+                at = pl.ds(0, end) if end == marks[0] else pl.ds(marks[0], end - marks[0])
+                for src, dst in ((nm_v, nm_ref), (bg_v, bg_ref)):
+                    cp = pltpu.make_async_copy(src.at[:, at], dst.at[:, at], osem.at[len(stores)])
+                    cp.start()
+                    stores.append(cp)
+
+    lines_p, lines_r, lines_r2, cores = {}, {}, {}, {}
+
+    def swap_core(k, cp):
+        cores.setdefault(k, []).append(cp)
+
 
     def stage_two(k):
         q, s = cuts[k]
@@ -222,50 +228,55 @@
         start_z(k + WINDOW)
         lines_p[k] = send_line(q, s, y, x, pnbr)
         lines_r[k] = send_line(q, s, y, x, rnbr)
-        cores.append(send_line(q, s, y, x, core))
+        swap_core(k, send_line(q, s, y, x, core))
 
     def stage_three(k):
         q, s = cuts[k]
         lines_p[k].wait_recv()
         lines_r2[k] = send_line(q, s, py, px, rnbr)
-        cores.append(send_line(q, s, py, px, core))
+        swap_core(k, send_line(q, s, py, px, core))
 
     def stage_four(k):
         q, s = cuts[k]
         lines_r[k].wait_recv()
-        cores.append(send_line(q, s, ry, rx, core))
+        swap_core(k, send_line(q, s, ry, rx, core))
 
     def stage_five(k):
         q, s = cuts[k]
         lines_r2[k].wait_recv()
-        cores.append(send_line(q, s, dy, dx, core))
+        swap_core(k, send_line(q, s, dy, dx, core))
 
     n = len(cuts)
-    for t in range(n + 3):
+    for t in range(n + LAG_FIVE):
         if t < n:
             stage_two(t)
-        if 0 <= t - 1 < n:
-            stage_three(t - 1)
-            stage_four(t - 1)
-        if 0 <= t - 2 < n:
-            stage_five(t - 2)
-        if t == 1:
+        if 0 <= t - LAG_THREE < n:
+            stage_three(t - LAG_THREE)
+            stage_four(t - LAG_THREE)
+        if 0 <= t - LAG_FIVE < n:
+            stage_five(t - LAG_FIVE)
+        if t == LAG_FIVE + 1:
+            for cp in cores[0]:
+                cp.wait_recv()
             stack_vectors()
             for cp in loads:
                 cp.wait()
-        if t >= 1:
-            some_tokens(2)
+        if t > LAG_FIVE:
+            some_tokens(-(-13 // (n - 1)))
     some_tokens(len(todo))
-    for cp in cores:
-        cp.wait_recv()
+    for k in range(1, n):
+        for cp in cores[k]:
+            cp.wait_recv()
     for cp in started:
         cp.wait_send()
-    view = vgot.at[pl.ds(0, 31)]
-    pltpu.make_async_copy(view, view, vsend).wait()
-
-
-NSEND = 30 * CUTS
-WINDOW = 3
+    for cp in stores:
+        cp.wait()
+
+
+NSEND = 10 * (3 * CUTS + 1)
+LAG_THREE = 3
+LAG_FIVE = 6
+WINDOW = 4
 
 
 def gather_all(own_len, inner, outer, vec, tokens, cot, mask, keep, pool, spatial):
@@ -273,6 +284,7 @@
     patches, images, _ = tokens.shape
     pad = -(-patches // LOT) * LOT
     vmem = pl.BlockSpec(memory_space=pltpu.VMEM)
+    smem = pl.BlockSpec(memory_space=pltpu.SMEM)
     anyb = pl.BlockSpec(memory_space=pl.ANY)
     dma = pltpu.SemaphoreType.DMA
     shape = jax.ShapeDtypeStruct
@@ -290,18 +302,20 @@
             shape((256, 256), BF),
             shape((256, 1), F32),
         ),
-        in_specs=[vmem] * 3 + [anyb] * 2 + [vmem] * 4,
-        out_specs=[anyb] + [vmem] * 9,
+        in_specs=[vmem] * 3 + [anyb] * 2 + [vmem, smem, vmem, vmem],
+        out_specs=[anyb, vmem, anyb, anyb] + [vmem] * 6,
         scratch_shapes=[
             pltpu.VMEM((3, rows, width), BF),
             pltpu.VMEM((8, 128), F32),
-            pltpu.VMEM((32, 8, 128), F32),
+            pltpu.VMEM((2, 2, 4, 2, 8, 128), F32),
             pltpu.VMEM((256, 256), F32),
             pltpu.VMEM((patches, images, width), BF),
             pltpu.VMEM((patches, images, width), BF),
             pltpu.VMEM((LOT * images, width), BF),
             pltpu.VMEM((LOT * images, width), BF),
-            dma((NSEND,)), dma((NSEND,)), dma, dma, dma, dma((2,)),
+            pltpu.VMEM((images, pad, width), BF),
+            pltpu.VMEM((images, pad, width), BF),
+            dma((NSEND,)), dma((NSEND,)), dma, dma((2,)), dma((4,)),
         ],
         compiler_params=pltpu.CompilerParams(
             collective_id=0, has_side_effects=True, vmem_limit_bytes=60 * 2**20
@@ -458,7 +472,6 @@
             s1 = s1 + lanes(h1)
         mean = jnp.sum(s1, axis=1, keepdims=True) * (1.0 / gate)
         q1 = jnp.zeros((tm, 128), F32)
-        rs1 = jnp.zeros((tm, 128), F32)
         for j in range(nj):
             cols = slice(j * cw, (j + 1) * cw)
             a0 = dot(nb, wtt[0, :, cols], NN) + vrow(b0_base, j)
@@ -468,12 +481,10 @@
             h0_b[rows, cols] = h0.astype(BF)
             mg_b[rows, cols] = mg.astype(BF)
             e0_b[rows, cols] = (gg * d0).astype(BF)
-            rs1 = rs1 + lanes(mg)
             c = h1_s[:, cols] - mean
             q1 = q1 + lanes(c * c)
         inv = lax.rsqrt(jnp.sum(q1, axis=1, keepdims=True) * (1.0 / gate) + NORM_EPS)
-        stat_b[rows, 0:128] = jnp.broadcast_to(inv, (tm, 128))
-        stat_b[rows, 128:256] = rs1
+        stat_b[rows, :] = jnp.broadcast_to(inv, (tm, 128))
         for j in range(nj):
             cols = slice(j * cw, (j + 1) * cw)
             u2 = (h1_s[:, cols] - mean) * inv
@@ -490,23 +501,25 @@
         both = (cid < n) & (rid2 < n)
         sp = jnp.where(both, sp_ref[0:m, 0:m], 0.0).astype(BF)
         spt = jnp.where(both, spt_ref[0:m, 0:m], 0.0).astype(BF)
-        sbias = sbias_ref[0:m, :]
         valid = rid < n
         fill = jnp.where(rid < need_of(b) * LOT, 0.0, 1.0)
-        inv = stat_b[rows, 0:1]
+        sbias = jnp.where(valid, sbias_ref[0:m, :], fill)
+        inv = jnp.where(valid, stat_b[rows, 0:1], 0.0)
+        ones = jnp.ones((LOT, gate), BF)
         tsum = jnp.zeros((m, 128), F32)
         tdot = jnp.zeros((m, 128), F32)
-        sg = jnp.zeros((m, m), F32)
+        xm_ones = jnp.concatenate([xm_b[rows, :], ones], axis=0)
+        sg = dot(mg_b[rows, :], xm_ones, NT)
+        sg_ref[0:m, 0:m] += jnp.where(both, sg[:, 0:m], 0.0)
+        sbg_ref[0:m, 0:1] += jnp.where(valid, sg[:, m : m + 1], 0.0)
         for j in range(nj):
             cols = slice(j * cw, (j + 1) * cw)
             xm = xm_b[rows, cols]
             mg = mg_b[rows, cols]
-            so = dot(sp, xm, NN) + sbias
-            so = jnp.where(valid, so, fill)
+            so = (dot(sp, xm, NN) + sbias).astype(BF)
             mix = dot(spt, mg, NN)
-            sg = sg + dot(mg, xm, NT)
-            h0_b[rows, cols] = (h0_b[rows, cols].astype(F32) * so).astype(BF)
-            e0_b[rows, cols] = (e0_b[rows, cols].astype(F32) * so).astype(BF)
+            h0_b[rows, cols] = h0_b[rows, cols] * so
+            e0_b[rows, cols] = e0_b[rows, cols] * so
             u2 = u2_b[rows, cols].astype(F32)
             mu = mix * u2
             gain = vrow(g2_base, j)
@@ -517,16 +530,14 @@
             vi, lo = j * cw // width, j * cw % width
             vacc[g2_base // width + vi, :, lo : lo + cw] += fold8(mu)
             vacc[s2_base // width + vi, :, lo : lo + cw] += fold8(mix)
-        sg_ref[0:m, 0:m] += jnp.where(both, sg, 0.0)
-        sbg_ref[0:m, :] += jnp.where(valid, stat_b[rows, 128:256], 0.0)
         m1 = jnp.sum(tsum, axis=1, keepdims=True) * (1.0 / gate)
         m2 = jnp.sum(tdot, axis=1, keepdims=True) * (1.0 / gate)
+        base, slope = fill - inv * m1, inv * m2
         for j in range(nj):
             cols = slice(j * cw, (j + 1) * cw)
             u2 = u2_b[rows, cols].astype(F32)
-            sec = inv * (t_s[0:m, cols] - m1 - u2 * m2)
-            sec = jnp.where(valid, sec, fill)
-            d1_b[rows, cols] = (d1_b[rows, cols].astype(F32) * sec).astype(BF)
+            sec = (inv * t_s[0:m, cols] + (base - u2 * slope)).astype(BF)
+            d1_b[rows, cols] = d1_b[rows, cols] * sec
 
     def phase_w(k, gs):
         r0 = pl.multiple_of(k * kw, kw)
@@ -697,7 +708,7 @@
             small_ref[row : row + 1, :] = sums[v : v + 1, h * 256 : (h + 1) * 256]
     pad = sg_ref.shape[0]
     small_ref[SPATIAL_ROW : SPATIAL_ROW + pad, 0:pad] = sg_ref[...]
-    bias = jnp.sum(sbg_ref[...], axis=1, keepdims=True)
+    bias = sbg_ref[:, 0:1]
     eye = lax.broadcasted_iota(jnp.int32, (pad, pad), 0) == lax.broadcasted_iota(jnp.int32, (pad, pad), 1)
     bias_row = jnp.sum(jnp.where(eye, bias, 0.0), axis=0, keepdims=True)
     small_ref[SPATIAL_ROW + patches : SPATIAL_ROW + patches + 1, 0:pad] = bias_row
@@ -718,7 +729,7 @@
 
 def run_block(
     tokens, cot, nm, bg, info, poolc, bsum, wt, vec, sp, spt, sbias,
-    *, rows_cap=1024, tm=256, kw=256, classes=(112, 160, 208),
+    *, rows_cap=1024, tm=256, kw=256, classes=(96, 144, 208),
 ):
     patches, images, width = tokens.shape
     gate = wt.shape[1]
@@ -758,7 +769,7 @@
         ]
         + [pltpu.VMEM((cap, gate), BF)] * 6
         + [
-            pltpu.VMEM((cap, 256), F32),
+            pltpu.VMEM((cap, 128), F32),
             pltpu.VMEM((tm, gate), F32),
             pltpu.VMEM((pad, gate), F32),
             pltpu.VMEM((2, LOT, images, width), BF),
@@ -780,163 +791,173 @@
 
 def reduce_kernel(
     g_hbm, small_ref, red_ref, tot_ref, norm_ref,
-    acc, rc, rr, rp, rz, rz2, rb, stage, sbuf, sred, nbuf, nown,
-    send, recv, lsem, s1s, s1r, s2s, s2r, ns, nr,
+    acc, rc, rr, rp, rz, sacc, src, srr, srp, srz, nbuf, mbuf, nown, mown,
+    send, recv, lsem,
 ):
     x, y, z, c = place()
-    me = (y * 2 + x) * 8 + z * 2 + c
     px, py = jnp.where(c == 0, 1 - x, x), jnp.where(c == 0, y, 1 - y)
     rx, ry = jnp.where(c == 0, x, 1 - x), jnp.where(c == 0, 1 - y, y)
     dx, dy = 1 - x, 1 - y
     pnbr, rnbr, core = device(px, py, z, c), device(rx, ry, z, c), device(x, y, z, 1 - c)
-    lines = ((ry, rx), (dy, dx), (y, x), (py, px))
     loads = [pltpu.make_async_copy(g_hbm.at[q, :, :, :, c], acc.at[q], lsem.at[q]) for q in range(3)]
     for cp in loads:
         cp.start()
-    greet_all()
+    column = [device(x, y, (z + k) % 4, c) for k in (1, 2, 3)]
+    column += [device(x, y, (z + k) % 4, 1 - c) for k in (0, 1, 2, 3)]
+    plane = [device(dx, y, z, c), device(x, dy, z, c), device(dx, dy, z, c)]
+    barrier = pltpu.get_barrier_semaphore()
+    for peer in column + plane:
+        pl.semaphore_signal(barrier, inc=1, device_id=peer, device_id_type=MESH)
+    pl.semaphore_wait(barrier, len(column + plane))
     index = [0]
     started = []
 
-    def remote(src, dst, dev):
+    def remote(src_ref, dst_ref, dev):
         k = index[0]
         index[0] += 1
         cp = pltpu.make_async_remote_copy(
-            src_ref=src, dst_ref=dst, send_sem=send.at[k], recv_sem=recv.at[k],
+            src_ref=src_ref, dst_ref=dst_ref, send_sem=send.at[k], recv_sem=recv.at[k],
             device_id=dev, device_id_type=MESH,
         )
         cp.start()
         started.append(cp)
         return cp
 
-    swaps = {}
-    for i, (ly, lx) in enumerate(lines):
-        for q in range(3):
-            swaps[q, i] = None
-    for i, (ly, lx) in enumerate(((dy, dx), (ry, rx), (py, px), (y, x))):
-        for q in range(3):
-            swaps[q, i] = remote(g_hbm.at[q, ly, lx, :, 1 - c], rc.at[q, ly, lx], core)
-
-    def broadcast(src, dst_at, ssem, rsem):
-        def body(k, carry):
-            peer = (me + k) % 32
-            pltpu.make_async_remote_copy(
-                src_ref=src(peer), dst_ref=dst_at, send_sem=ssem, recv_sem=rsem,
-                device_id=(peer // 8, peer % 8), device_id_type=MESH,
-            ).start()
-            return carry
-        lax.fori_loop(1, 32, body, 0)
-
-    def wait31(ref, sem):
-        view = ref.at[pl.ds(0, 31)]
-        pltpu.make_async_copy(view, view, sem).wait()
-
-    broadcast(lambda p: small_ref.at[p], sbuf.at[me], s1s, s1r)
-    for cp in loads:
-        cp.wait()
-
-    def add_line(q, ly, lx, ref):
-        for b in range(4):
-            acc[q, ly, lx, b] = (acc[q, ly, lx, b].astype(F32) + ref[b].astype(F32)).astype(BF)
-
-    first = {}
-    for q in range(3):
-        swaps[q, 0].wait_recv()
-        add_line(q, dy, dx, rc.at[q, dy, dx])
-        first[q, 0] = remote(acc.at[q, dy, dx], rr.at[q, 0], rnbr)
-    for i in (1, 2):
-        for q in range(3):
-            swaps[q, i].wait_recv()
-    for q in range(3):
-        add_line(q, ry, rx, rc.at[q, ry, rx])
-        first[q, 1] = remote(acc.at[q, ry, rx], rr.at[q, 1], rnbr)
-    for q in range(3):
-        add_line(q, py, px, rc.at[q, py, px])
-        swaps[q, 3].wait_recv()
-        add_line(q, y, x, rc.at[q, y, x])
-    second = {}
-    for q in (2, 0, 1):
-        first[q, 0].wait_recv()
-        add_line(q, py, px, rr.at[q, 0])
-        if q < 2:
-            second[q] = remote(acc.at[q, py, px], rp.at[q], pnbr)
+    cut = acc.shape[4] // RCUTS
+    cuts = [(3, 0)] + [(q, s) for s in range(RCUTS) for q in range(3)]
+
+    def views(k):
+        q, s = cuts[k]
+        if q == 3:
+            return (
+                F32, lambda *i: sacc.at[i], lambda *i: src.at[i], lambda *i: srr.at[i],
+                lambda *i: srp.at[i], lambda *i: srz.at[i],
+            )
+        at = pl.ds(s * cut, cut)
+
+        def of(ref, dims):
+            def view(*i):
+                rest = (slice(None),) * (dims - len(i))
+                return ref.at[(q,) + i + rest + (at,)]
+
+            return view
+
+        return BF, of(acc, 3), of(rc, 3), of(rr, 2), of(rp, 1), of(rz, 1)
+
+    def plus(kind, a, b):
+        a[...] = (a[...].astype(F32) + b[...].astype(F32)).astype(kind)
+
+    swaps, r_in, p_in, z_in = {}, {}, {}, {}
+    scopy = pltpu.make_async_copy(small_ref.at[:, :, :, c], sacc, lsem.at[3])
+    scopy.start()
+    for k, (q, s) in enumerate(cuts):
+        if q == 3:
+            swaps[k] = remote(small_ref.at[:, :, :, 1 - c], src, core)
         else:
-            second[q] = [
-                remote(acc.at[q, py, px, (z + k) % 4], rz2.at[k - 1], device(x, y, (z + k) % 4, c)) for k in (1, 2, 3)
-            ]
-    own2 = None
-    for q in (2, 0, 1):
-        first[q, 1].wait_recv()
-        add_line(q, y, x, rr.at[q, 1])
-        if q == 2:
-            own2 = [
-                remote(acc.at[q, y, x, (z + k) % 4], rz.at[q, k - 1], device(x, y, (z + k) % 4, c)) for k in (1, 2, 3)
-            ]
-    third = {}
-    for q in (0, 1):
-        second[q].wait_recv()
-        add_line(q, y, x, rp.at[q])
-        third[q] = [
-            remote(acc.at[q, y, x, (z + k) % 4], rz.at[q, k - 1], device(x, y, (z + k) % 4, c)) for k in (1, 2, 3)
+            at = pl.ds(s * cut, cut)
+            swaps[k] = remote(g_hbm.at[q, :, :, :, 1 - c, at], rc.at[q, :, :, :, at], core)
+
+    def stage_two(k):
+        kind, a, b, r, p, zz = views(k)
+        if k == 0:
+            scopy.wait()
+        elif k <= 3:
+            loads[cuts[k][0]].wait()
+        swaps[k].wait_recv()
+        for ly in range(2):
+            for lx in range(2):
+                for lz in range(4):
+                    plus(kind, a(ly, lx, lz), b(ly, lx, lz))
+        r_in[k] = [remote(a(dy, dx), r(0), rnbr), remote(a(ry, rx), r(1), rnbr)]
+
+    def stage_three(k):
+        kind, a, b, r, p, zz = views(k)
+        for cp in r_in[k]:
+            cp.wait_recv()
+        for lz in range(4):
+            plus(kind, a(py, px, lz), r(0, lz))
+        p_in[k] = remote(a(py, px), p(), pnbr)
+        for lz in range(4):
+            plus(kind, a(y, x, lz), r(1, lz))
+
+    def stage_four(k):
+        kind, a, b, r, p, zz = views(k)
+        p_in[k].wait_recv()
+        for lz in range(4):
+            plus(kind, a(y, x, lz), p(lz))
+        z_in[k] = [
+            remote(a(y, x, (z + j) % 4), zz(j - 1), device(x, y, (z + j) % 4, c)) for j in (1, 2, 3)
         ]
-    for cp in second[2]:
-        cp.wait_recv()
-    stage[...] = (
-        acc[2, py, px, z].astype(F32) + rz2[0].astype(F32) + rz2[1].astype(F32) + rz2[2].astype(F32)
-    ).astype(BF)
-    last = remote(stage, rb, pnbr)
-    sbuf[me] = small_ref[me]
-    wait31(sbuf, s1r)
-    total = sbuf[0]
-    for k in range(1, 32):
-        total = total + sbuf[k]
-    sred[...] = total
-    tot_ref[me] = total
-    broadcast(lambda p: sred, tot_ref.at[me], s2s, s2r)
-    sq = jnp.zeros((8, 128), F32)
 
     def fold(v):
         t = jnp.zeros((8, 128), F32)
         for r in range(0, v.shape[0], 8):
             for l in range(0, v.shape[1], 128):
-                p = v[r : r + 8, l : l + 128]
-                t = t + p * p
+                part = v[r : r + 8, l : l + 128]
+                t = t + part * part
         return t
 
-    sq = sq + fold(total)
-    for cp in own2:
+    squares = [jnp.zeros((8, 128), F32)]
+    tots = []
+
+    def stage_five(k):
+        kind, a, b, r, p, zz = views(k)
+        for cp in z_in[k]:
+            cp.wait_recv()
+        v = (a(y, x, z)[...].astype(F32) + zz(0)[...].astype(F32)) + (
+            zz(1)[...].astype(F32) + zz(2)[...].astype(F32)
+        )
+        squares[0] = squares[0] + fold(v)
+        q, s = cuts[k]
+        if q == 3:
+            tot_ref[y, x, z, c] = v
+            mine = tot_ref.at[y, x, z, c]
+            tots.append([remote(mine, mine, dev) for dev in column])
+        else:
+            red_ref[q, s * cut : (s + 1) * cut] = v
+
+    n = len(cuts)
+    for t in range(n + 3 * RLAG):
+        if t < n:
+            stage_two(t)
+        if 0 <= t - RLAG < n:
+            stage_three(t - RLAG)
+        if 0 <= t - 2 * RLAG < n:
+            stage_four(t - 2 * RLAG)
+        if 0 <= t - 3 * RLAG < n:
+            stage_five(t - 3 * RLAG)
+        if t == n:
+            for cp in tots[0]:
+                cp.wait_recv()
+            lines = tot_ref.at[y, x]
+            tots.append([remote(lines, lines, dev) for dev in plane])
+    nown[...] = squares[0]
+    sent = [remote(nown, nbuf.at[z * 2 + c], dev) for dev in column]
+    nbuf[z * 2 + c] = squares[0]
+    for cp in sent:
         cp.wait_recv()
-    for q in (0, 1):
-        for cp in third[q]:
-            cp.wait_recv()
-        v = (
-            acc[q, y, x, z].astype(F32) + rz[q, 0].astype(F32) + rz[q, 1].astype(F32) + rz[q, 2].astype(F32)
-        )
-        red_ref[q] = v
-        sq = sq + fold(v)
-    last.wait_recv()
-    v = (
-        acc[2, y, x, z].astype(F32) + rz[2, 0].astype(F32) + rz[2, 1].astype(F32) + rz[2, 2].astype(F32)
-    ) + rb[...].astype(F32)
-    red_ref[2] = v
-    sq = sq + fold(v)
-    nown[...] = sq
-    nbuf[me] = sq
-    broadcast(lambda p: nown, nbuf.at[me], ns, nr)
-    wait31(nbuf, nr)
-    wait31(tot_ref, s2r)
-    t = nbuf[0]
-    for k in range(1, 32):
-        t = t + nbuf[k]
-    t = jnp.sum(jnp.sum(t, axis=0, keepdims=True), axis=1, keepdims=True)
-    norm_ref[...] = jnp.broadcast_to(jnp.sqrt(t), (8, 128))
+    total = nbuf[0]
+    for i in range(1, 8):
+        total = total + nbuf[i]
+    mown[...] = total
+    sent = [remote(mown, mbuf.at[y * 2 + x], dev) for dev in plane]
+    mbuf[y * 2 + x] = total
+    for cp in sent:
+        cp.wait_recv()
+    total = mbuf[0]
+    for i in range(1, 4):
+        total = total + mbuf[i]
+    total = jnp.sum(jnp.sum(total, axis=0, keepdims=True), axis=1, keepdims=True)
+    norm_ref[...] = jnp.broadcast_to(jnp.sqrt(total), norm_ref.shape)
+    for cp in tots[1]:
+        cp.wait_recv()
     for cp in started:
         cp.wait_send()
-    wait31(sbuf, s1s)
-    wait31(tot_ref, s2s)
-    wait31(nbuf, ns)
-
-
-NRED = 12 + 6 + 2 + 3 + 3 + 6 + 1
+
+
+RCUTS = 3
+RLAG = 2
+NRED = 7 * (3 * RCUTS + 1) + 20
 
 
 def reduce_all(g, small):
@@ -944,7 +965,7 @@
     vmem = pl.BlockSpec(memory_space=pltpu.VMEM)
     anyb = pl.BlockSpec(memory_space=pl.ANY)
     dma = pltpu.SemaphoreType.DMA
-    blk = (rows, width)
+    blk, sblk = (rows, width), small.shape[-2:]
     return pl.pallas_call(
         reduce_kernel,
         out_shape=(
@@ -958,19 +979,22 @@
             pltpu.VMEM((3, 2, 2, 4) + blk, BF),
             pltpu.VMEM((3, 2, 2, 4) + blk, BF),
             pltpu.VMEM((3, 2, 4) + blk, BF),
-            pltpu.VMEM((2, 4) + blk, BF),
+            pltpu.VMEM((3, 4) + blk, BF),
             pltpu.VMEM((3, 3) + blk, BF),
-            pltpu.VMEM((3,) + blk, BF),
-            pltpu.VMEM(blk, BF),
-            pltpu.VMEM(blk, BF),
-            pltpu.VMEM(small.shape, F32),
-            pltpu.VMEM(small.shape[1:], F32),
-            pltpu.VMEM((32, 8, 128), F32),
+            pltpu.VMEM((2, 2, 4) + sblk, F32),
+            pltpu.VMEM((2, 2, 4) + sblk, F32),
+            pltpu.VMEM((2, 4) + sblk, F32),
+            pltpu.VMEM((4,) + sblk, F32),
+            pltpu.VMEM((3,) + sblk, F32),
+            pltpu.VMEM((8, 8, 128), F32),
+            pltpu.VMEM((4, 8, 128), F32),
             pltpu.VMEM((8, 128), F32),
-            dma((NRED,)), dma((NRED,)), dma((3,)),
-            dma, dma, dma, dma, dma, dma,
+            pltpu.VMEM((8, 128), F32),
+            dma((NRED,)), dma((NRED,)), dma((4,)),
         ],
-        compiler_params=pltpu.CompilerParams(collective_id=1, has_side_effects=True, vmem_limit_bytes=60 * 2**20),
+        compiler_params=pltpu.CompilerParams(
+            collective_id=1, has_side_effects=True, vmem_limit_bytes=60 * 2**20
+        ),
         name="reduce",
     )(g, small)
 
@@ -1031,7 +1055,7 @@
         out_shape=tuple(shape(a) for a in inner + outer + spatial),
         in_specs=[vmem] * 12,
         out_specs=[vmem] * 9,
-        compiler_params=pltpu.CompilerParams(vmem_limit_bytes=32 * 2**20),
+        compiler_params=pltpu.CompilerParams(vmem_limit_bytes=60 * 2**20),
         name="adam",
     )(red, tot, norm, *inner, *outer, *spatial)
 
@@ -1107,7 +1131,7 @@
             tokens,
             cot,
             valid_mask,
-            keep_mask[:, None],
+            keep_mask,
             pool_cotangent,
             spatial,
         )
@@ -1124,7 +1148,7 @@
     input_grad = input_grad.transpose(1, 0, 2)
     if fast:
         red, tot, norm = reduce_all(
-            grads.reshape(3, 2, 2, 4, 2, rows, width), small.reshape(32, 8, 256)
+            grads.reshape(3, 2, 2, 4, 2, rows, width), small.reshape(2, 2, 4, 2, 8, 256)
         )
         tot = tot.reshape(256, 256)
     else:

time: 211 us -> 185 us (0.88); the launches traced: 214 us -> 185 us
  Pallas kernels: 205 us -> 179 us
  local copies, waits for them, and re-layouts: 7.23 us -> 3.25 us
    pallas_call x1, Pallas kernels: 45.2 us -> 35.5 us  [gather_all(): pl.pallas_call(functools.partial(gather_kernel, own_len), out_shape=(shap...]
    pallas_call x1, Pallas kernels: 73.7 us -> 64.7 us  [reduce_all(): pl.pallas_call(reduce_kernel, out_shape=(jax.ShapeDtypeStruct((3,) + blk,...]
    pallas_call x1, Pallas kernels: 84.5 us -> 76.3 us  [run_block(): pl.pallas_call(functools.partial(block_kernel, cfg), out_shape=(shape((pa...]
    unnamed x30 -> x6, local copies, waits for them, and re-layouts: 2.66 us -> 0.02 us
where the time goes in v4:
time: 185 us
  Pallas kernels  179 us (97%)
  local copies, waits for them, and re-layouts  3.25 us (2%)
    pallas_call x1, Pallas kernels, run_block(): pl.pallas_call(functools.partial(block_kernel, cfg), out_shape=(shape((pa...  76.3 us
    pallas_call x1, Pallas kernels, reduce_all(): pl.pallas_call(reduce_kernel, out_shape=(jax.ShapeDtypeStruct((3,) + blk,...  64.7 us
    pallas_call x1, Pallas kernels, gather_all(): pl.pallas_call(functools.partial(gather_kernel, own_len), out_shape=(shap...  35.5 us

profile of v4, /device:TPU:0, one launch (start us, length us, event | category | flops | bytes accessed | tf_op | source)
XLA Modules:
  0.0 184.7 jit_solution(14519249238277895174)
XLA Ops:
  0.6 1.3 pad_bitcast_fusion.vec_ref
  1.9 35.5 %gather.1 = (bf16[3,2,2,4,2,48,512]{6,5,4,3,2,1,0:T(8,128)(2,1)}, f32[16,512]{1,0:T(8,128)}, bf16[16,208,512]{2,1,0:T(8,128)(2,1)}, bf16[16,208,512]{2,1,0:T(8,1...) custom-call(f32[2,48,512]{2,1,0:T(8,128)} %bitcast.23, ...), custom_call_target="tpu_custom_call" | custom-call | tf_op jit(solution)/shard_map/gather/pallas_call | solution.py:291
  37.5 76.3 %block.1 = (f32[196,16,512]{2,1,0:T(8,128)}, f32[196,16,512]{2,1,0:T(8,128)}, f32[16,512]{1,0:T(8,128)}, bf16[3,1536,512]{2,1,0:T(8,128)(2,1)}, f32[256,256]{1,0:T(8,128)}) custom-call(s32[16,128]{1,0:T(8,128)} %get-tuple-element.43.info_s.info_ref, bf16[196,16,512]{2,1,0:T(8,128)(2,1)} %bitcast.18, bf16[196,16,512]{2,1,0:T(8,128)(2,1)} %bitcast.20, ...), custom_call_target="tpu_custom_call" | custom-call | tf_op jit(solution)/shard_map/block/pallas_call | solution.py:748
  113.7 0.0 copy-start
  113.7 0.0 copy-start.1
  113.8 0.0 copy-start.2
  113.8 64.7 %reduce.1 = (f32[3,48,512]{2,1,0:T(8,128)}, f32[2,2,4,2,8,256]{5,4,3,2,1,0:T(8,128)}, f32[8,128]{1,0:T(8,128)}) custom-call(bf16[3,2,2,4,2,48,512]{6,5,4,3,2,1,0:T(8,128)(2,1)} %bitcast.21, f32[2,2,4,2,8,256]{5,4,3,2,1,0:T(8,128)} %bitcast.27), custom_call_target="tpu_custom_call" | custom-call | tf_op jit(solution)/shard_map/reduce/pallas_call | solution.py:969
  178.5 0.8 slice.8
  179.3 1.2 slice.6
  181.1 0.0 copy-done
  181.2 0.0 copy-done.1
  181.2 0.0 copy-done.2
  181.2 0.7 multiply_subtract_fusion
  181.8 2.8 %adam.1 = (f32[2,48,512]{2,1,0:T(8,128)}, f32[2,48,512]{2,1,0:T(8,128)}, f32[2,48,512]{2,1,0:T(8,128)}, f32[48,512]{1,0:T(8,128)}, f32[48,512]{1,0:T(8,128)}, /*...) custom-call(f32[3,48,512]{2,1,0:T(8,128)} %get-tuple-element.59.red, ...), custom_call_target="tpu_custom_call" | custom-call | tf_op jit(solution)/shard_map/adam/pallas_call | solution.py:1053
  (1 shorter events, 0.0 us)
Async XLA Ops:
  113.7 67.4 %copy-start = (f32[240]{0:T(256)S(1)}, f32[240]{0:T(256)}, u32[]{:S(2)}) copy-start(f32[240]{0:T(256)} %param.24) | copy-start | bytes 2884
  113.7 67.4 %copy-start.1 = (f32[240]{0:T(256)S(1)}, f32[240]{0:T(256)}, u32[]{:S(2)}) copy-start(f32[240]{0:T(256)} %param.30) | copy-start | bytes 2884
  113.8 67.4 %copy-start.2 = (f32[240]{0:T(256)S(1)}, f32[240]{0:T(256)}, u32[]{:S(2)}) copy-start(f32[240]{0:T(256)} %param.31) | copy-start | bytes 2884

commit v5 on v4

--- a/solution.py
+++ b/solution.py
@@ -358,14 +358,14 @@
     cfg,
     info_s,
     tokens_hbm, cot_hbm, nm_hbm, bg_hbm,
-    info_ref, poolc_ref, bsum_ref, wt_ref, vec_ref, sp_ref, spt_ref, sbias_ref,
+    info_ref, poolc_ref, bsum_ref, wt_hbm, vec_ref, sp_ref, spt_ref, sbias_ref,
     out_hbm, ig_hbm, pooled_ref, grads_hbm, small_ref,
     acc, sg_ref, sbg_ref, off_s, gend_s, grows_s,
-    wtt, nm_b, bg_b, h0_b, e0_b, mg_b, xm_b, u2_b, d1_b, stat_b, h1_s, t_s,
+    wt_ref, wtt, nm_b, bg_b, h0_b, e0_b, mg_b, xm_b, u2_b, d1_b, stat_b, h1_s, t_s,
     xblk, cblk, br_s, ng_s, out_st, ig_st, vacc,
-    pack_sem, in_sem, out_sem, grad_sem,
+    wt_sem, pack_sem, in_sem, out_sem, grad_sem,
 ):
-    images, patches, width, gate, rows_cap, tm, kw, classes = cfg
+    images, patches, width, gate, rows_cap, tm, classes = cfg
     cw = 256
     nj = gate // cw
     chunks = -(-patches // LOT)
@@ -385,6 +385,10 @@
 
     def need_of(b):
         return keep(b) * ((count(b) + LOT - 1) // LOT)
+
+    wt_loads = [pltpu.make_async_copy(wt_hbm.at[q], wt_ref.at[q], wt_sem.at[q]) for q in range(3)]
+    for q in (1, 0, 2):
+        wt_loads[q].start()
 
     def plan(b, carry):
         group, row, first = carry
@@ -431,10 +435,6 @@
         for cp in load_lot(k, LOT, k):
             cp.start()
 
-    for q in range(3):
-        for j in range(nj):
-            wtt[q, :, j * cw : (j + 1) * cw] = wt_ref[q, j * cw : (j + 1) * cw, :].T
-
     def zero_rows(ref, n_chunks, start):
         z = jnp.zeros((LOT, ref.shape[1]), ref.dtype)
 
@@ -454,6 +454,10 @@
     acc[...] = jnp.zeros_like(acc)
     sg_ref[...] = jnp.zeros_like(sg_ref)
     sbg_ref[...] = jnp.zeros_like(sbg_ref)
+    for q in (1, 0, 2):
+        wt_loads[q].wait()
+        for j in range(nj):
+            wtt[q, :, j * cw : (j + 1) * cw] = wt_ref[q, j * cw : (j + 1) * cw, :].T
     loop(0, images, lambda b: pack(b, lambda cp: cp.wait()))
 
     def phase_a(t, gs):
@@ -539,30 +543,26 @@
             sec = (inv * t_s[0:m, cols] + (base - u2 * slope)).astype(BF)
             d1_b[rows, cols] = d1_b[rows, cols] * sec
 
-    def phase_w(k, gs):
-        r0 = pl.multiple_of(k * kw, kw)
-        rows = pl.ds(r0, kw)
-        here = pl.ds(pl.multiple_of(gs + r0, LOT), kw)
-        nb = nm_b[here, :]
-        bgt = bg_b[here, :]
-        for j in range(gate // 256):
-            cols = slice(j * 256, (j + 1) * 256)
-            acc[0, cols, :] += dot(e0_b[rows, cols], nb, TN)
-            acc[1, cols, :] += dot(d1_b[rows, cols], nb, TN)
-            acc[2, cols, :] += dot(h0_b[rows, cols], bgt, TN)
-
     def phase_c(t, gs, group_rows):
         r0 = pl.multiple_of(t * tm, tm)
         rows = pl.ds(r0, tm)
         here = pl.ds(pl.multiple_of(gs + r0, LOT), tm)
+        nb = nm_b[here, :]
+        bgt = bg_b[here, :]
         mine = lax.broadcasted_iota(jnp.int32, (tm, 1), 0) < group_rows - r0
         br = dot(h0_b[rows, :], wt_ref[2], NN)
-        bg_b[here, :] = jnp.where(mine, br, bg_b[here, :].astype(F32)).astype(BF)
+        bg_b[here, :] = jnp.where(mine, br, bgt.astype(F32)).astype(BF)
         ng = dot(e0_b[rows, :], wt_ref[0], NN) + dot(d1_b[rows, :], wt_ref[1], NN)
-        nm_b[here, :] = jnp.where(mine, ng, nm_b[here, :].astype(F32)).astype(BF)
-        for base, ref in ((b0_base // width, e0_b), (b1_base // width, d1_b)):
-            for v in range(gate // width):
-                vacc[base + v] += fold8(ref[rows, v * width : (v + 1) * width].astype(F32))
+        nm_b[here, :] = jnp.where(mine, ng, nb.astype(F32)).astype(BF)
+        for j in range(nj):
+            cols = slice(j * cw, (j + 1) * cw)
+            vi, lo = j * cw // width, j * cw % width
+            e0, d1 = e0_b[rows, cols], d1_b[rows, cols]
+            acc[0, cols, :] += dot(e0, nb, TN)
+            acc[1, cols, :] += dot(d1, nb, TN)
+            acc[2, cols, :] += dot(h0_b[rows, cols], bgt, TN)
+            vacc[b0_base // width + vi, :, lo : lo + cw] += fold8(e0.astype(F32))
+            vacc[b1_base // width + vi, :, lo : lo + cw] += fold8(d1.astype(F32))
 
     def group(g, carry):
         b_start, gs = carry
@@ -584,7 +584,6 @@
         tail = (tiles * tm - rows) // LOT
         for ref in (h0_b, e0_b, d1_b):
             zero_rows(ref, tail, rows)
-        loop(0, (rows + kw - 1) // kw, lambda k: phase_w(k, gs))
         loop(0, tiles, lambda t: phase_c(t, gs, rows))
         return b_end, gs + rows
 
@@ -729,7 +728,7 @@
 
 def run_block(
     tokens, cot, nm, bg, info, poolc, bsum, wt, vec, sp, spt, sbias,
-    *, rows_cap=1024, tm=256, kw=256, classes=(96, 144, 208),
+    *, rows_cap=1024, tm=256, classes=(96, 144, 208),
 ):
     patches, images, width = tokens.shape
     gate = wt.shape[1]
@@ -738,7 +737,7 @@
     cap = rows_cap + pad + 48
     cap = -(-cap // tm) * tm
     long = images * pad + tm + LOT
-    cfg = (images, patches, width, gate, rows_cap, tm, kw, classes)
+    cfg = (images, patches, width, gate, rows_cap, tm, classes)
     smem = pl.BlockSpec(memory_space=pltpu.SMEM)
     vmem = pl.BlockSpec(memory_space=pltpu.VMEM)
     anyb = pl.BlockSpec(memory_space=pl.ANY)
@@ -754,7 +753,7 @@
             shape((3, gate, width), BF),
             shape((256, 256), F32),
         ),
-        in_specs=[smem] + [anyb] * 4 + [vmem] * 8,
+        in_specs=[smem] + [anyb] * 4 + [vmem] * 3 + [anyb] + [vmem] * 4,
         out_specs=[anyb, anyb, vmem, anyb, vmem],
         scratch_shapes=[
             pltpu.VMEM((3, gate, width), F32),
@@ -763,6 +762,7 @@
             pltpu.SMEM((images,), jnp.int32),
             pltpu.SMEM((images,), jnp.int32),
             pltpu.SMEM((images,), jnp.int32),
+            pltpu.VMEM((3, gate, width), BF),
             pltpu.VMEM((3, width, gate), BF),
             pltpu.VMEM((long, width), BF),
             pltpu.VMEM((long, width), BF),
@@ -779,6 +779,7 @@
             pltpu.VMEM((2, LOT, images, width), F32),
             pltpu.VMEM((2, LOT, images, width), F32),
             pltpu.VMEM((nvec, 8, width), F32),
+            dma((3,)),
             dma((2, images)),
             dma((2, 2)),
             dma((2, 2)),

time: 185 us -> 182 us (0.984)
  Pallas kernels: 179 us -> 176 us
    pallas_call x1, Pallas kernels: 64.7 us -> 57.7 us  [reduce_all(): pl.pallas_call(reduce_kernel, out_shape=(jax.ShapeDtypeStruct((3,) + blk,...]
    pallas_call x1, Pallas kernels: 76.3 us -> 80.3 us  [run_block(): pl.pallas_call(functools.partial(block_kernel, cfg), out_shape=(shape((pa...]
where the time goes in v5:
time: 182 us
  Pallas kernels  176 us (97%)
  local copies, waits for them, and re-layouts  3.25 us (2%)
    pallas_call x1, Pallas kernels, run_block(): pl.pallas_call(functools.partial(block_kernel, cfg), out_shape=(shape((pa...  80.3 us
    pallas_call x1, Pallas kernels, reduce_all(): pl.pallas_call(reduce_kernel, out_shape=(jax.ShapeDtypeStruct((3,) + blk,...  57.7 us
    pallas_call x1, Pallas kernels, gather_all(): pl.pallas_call(functools.partial(gather_kernel, own_len), out_shape=(shap...  35.5 us

profile of v5, /device:TPU:0, one launch (start us, length us, event | category | flops | bytes accessed | tf_op | source)
XLA Modules:
  0.0 181.7 jit_solution(14420163725224715379)
XLA Ops:
  0.6 1.3 pad_bitcast_fusion.vec_ref
  1.9 35.5 %gather.1 = (bf16[3,2,2,4,2,48,512]{6,5,4,3,2,1,0:T(8,128)(2,1)}, f32[16,512]{1,0:T(8,128)}, bf16[16,208,512]{2,1,0:T(8,128)(2,1)}, bf16[16,208,512]{2,1,0:T(8,1...) custom-call(f32[2,48,512]{2,1,0:T(8,128)} %bitcast.23, ...), custom_call_target="tpu_custom_call" | custom-call | tf_op jit(solution)/shard_map/gather/pallas_call | solution.py:291
  37.5 80.3 %block.1 = (f32[196,16,512]{2,1,0:T(8,128)}, f32[196,16,512]{2,1,0:T(8,128)}, f32[16,512]{1,0:T(8,128)}, bf16[3,1536,512]{2,1,0:T(8,128)(2,1)}, f32[256,256]{1,0:T(8,128)}) custom-call(s32[16,128]{1,0:T(8,128)} %get-tuple-element.43.info_s.info_ref, bf16[196,16,512]{2,1,0:T(8,128)(2,1)} %bitcast.18, bf16[196,16,512]{2,1,0:T(8,128)(2,1)} %bitcast.20, ...), custom_call_target="tpu_custom_call" | custom-call | tf_op jit(solution)/shard_map/block/pallas_call | solution.py:747
  117.7 0.0 copy-start
  117.7 0.0 copy-start.1
  117.7 0.0 copy-start.2
  117.8 57.7 %reduce.1 = (f32[3,48,512]{2,1,0:T(8,128)}, f32[2,2,4,2,8,256]{5,4,3,2,1,0:T(8,128)}, f32[8,128]{1,0:T(8,128)}) custom-call(bf16[3,2,2,4,2,48,512]{6,5,4,3,2,1,0:T(8,128)(2,1)} %bitcast.21, f32[2,2,4,2,8,256]{5,4,3,2,1,0:T(8,128)} %bitcast.27), custom_call_target="tpu_custom_call" | custom-call | tf_op jit(solution)/shard_map/reduce/pallas_call | solution.py:970
  175.4 0.8 slice.8
  176.2 1.2 slice.6
  178.1 0.0 copy-done
  178.1 0.0 copy-done.1
  178.1 0.0 copy-done.2
  178.1 0.7 multiply_subtract_fusion
  178.8 2.8 %adam.1 = (f32[2,48,512]{2,1,0:T(8,128)}, f32[2,48,512]{2,1,0:T(8,128)}, f32[2,48,512]{2,1,0:T(8,128)}, f32[48,512]{1,0:T(8,128)}, f32[48,512]{1,0:T(8,128)}, /*...) custom-call(f32[3,48,512]{2,1,0:T(8,128)} %get-tuple-element.59.red, ...), custom_call_target="tpu_custom_call" | custom-call | tf_op jit(solution)/shard_map/adam/pallas_call | solution.py:1054
  (1 shorter events, 0.0 us)
Async XLA Ops:
  117.7 60.4 %copy-start = (f32[240]{0:T(256)S(1)}, f32[240]{0:T(256)}, u32[]{:S(2)}) copy-start(f32[240]{0:T(256)} %param.24) | copy-start | bytes 2884
  117.7 60.4 %copy-start.1 = (f32[240]{0:T(256)S(1)}, f32[240]{0:T(256)}, u32[]{:S(2)}) copy-start(f32[240]{0:T(256)} %param.30) | copy-start | bytes 2884
  117.7 60.4 %copy-start.2 = (f32[240]{0:T(256)S(1)}, f32[240]{0:T(256)}, u32[]{:S(2)}) copy-start(f32[240]{0:T(256)} %param.31) | copy-start | bytes 2884
